TPU v7x, 32 devices: a whole 2x2x4 slice. The times are simulated.
32 devices in a mesh: basis: 4 (over x, core), fit: 8 (over z, y).
Axes of the slice: x: 2, y: 2, z: 4, core: 2. Of those that a mesh axis runs over, the one named last changes fastest.
Arguments:
- integrals: bfloat16 [512, 128, 1024], P('basis', 'fit'), may hold values from -6 to 6
- pair_mask: int32 [32, 64], replicated, may hold values 0 or 1
- row_blocks: int32 [32], replicated, may hold values from 0 to 31, each once
- occ_coef: bfloat16 [512, 64], P('basis'), may hold values from -0.375 to 0.375
- vir_coef: bfloat16 [1024, 8192], P(None, 'fit'), may hold values from -0.1875 to 0.1875
Outputs:
- transformed: bfloat16 [128, 64, 8192], P(None, 'basis', 'fit')
Inputs may be any that keep to these rules, and one draw needn't show every extreme that they name: `row_blocks`: each of the 32 atom blocks appears exactly once. `pair_mask`: 1 marks a significant pair of atom blocks.
All inputs are finite; a program needn't handle non-finite values.
Results may differ from a plain program's by a relative error of at most 0.0049.
Values may be sent and summed in bfloat16 or wider, within the bound.
No kernel may reach another device: no remote copies, remote signals or barrier semaphores. Data moves between devices by JAX's collectives and lax.ppermute only.
A program may use at most 128 MiB of HBM per device.

v0:
```python
import jax
import jax.numpy as jnp
from jax import lax
from jax.sharding import PartitionSpec as P

BLK = 16


def shards(integrals, pair_mask, row_blocks, occ_coef, vir_coef):
    mu_dev = integrals.shape[0]
    fit_dev = integrals.shape[1]
    width_nu = integrals.shape[2]
    nocc = occ_coef.shape[1]
    blocks_dev = mu_dev // BLK
    owned = lax.dynamic_slice_in_dim(row_blocks, lax.axis_index("basis") * blocks_dev, blocks_dev)
    panels = lax.all_gather(occ_coef, "basis", axis=0, tiled=True)
    panel_blocks = panels.reshape(-1, BLK, nocc)
    mask_rows = jnp.take(pair_mask, owned, axis=0).astype(jnp.bfloat16)
    mask_full = jnp.repeat(jnp.repeat(mask_rows, BLK, axis=0), BLK, axis=1)
    masked = integrals * mask_full[:, None, :]
    share = nocc // lax.axis_size("basis")
    occ_rows = jnp.take(panel_blocks, owned, axis=0).reshape(mu_dev, nocc)
    flat = masked.reshape(mu_dev, fit_dev * width_nu)
    summed = lax.psum_scatter(
        lax.dot_general(
            occ_rows, flat, (((0,), (0,)), ((), ())), preferred_element_type=jnp.float32
        ),
        "basis",
        scatter_dimension=0,
        tiled=True,
    )
    half = summed.astype(jnp.bfloat16).reshape(share, fit_dev, width_nu)
    product = jnp.einsum(
        "ipn,na->pia",
        lax.all_gather(half, "fit", axis=1, tiled=True),
        vir_coef,
        preferred_element_type=jnp.float32,
    )
    return product.astype(jnp.bfloat16)


def solution(mesh):
    placed = (P("basis", "fit", None), P(), P(), P("basis", None), P(None, "fit"))
    return jax.shard_map(
        shards, mesh=mesh, in_specs=placed, out_specs=P(None, "basis", "fit"), check_vma=False
    )
```

profile of v0, /device:TPU:0, one launch (start us, length us, event | category | flops | bytes accessed | tf_op | source)
XLA Modules:
  0.0 165.5 jit_solution(4190964608482174847)
XLA Ops:
  6.5 0.0 copy-start
  6.5 0.0 reduce-scatter.2.cloned.1.call-start
  6.5 0.9 compare_and_fusion
  7.4 1.3 gather_fusion.1
  8.7 0.1 select_convert_fusion
  8.8 0.1 copy.12
  8.9 0.8 copy.11
  9.7 6.5 %all_gather.6 = bf16[512,64]{1,0:T(8,128)(2,1)S(1)} all-gather(bf16[128,64]{1,0:T(8,128)(2,1)S(1)} %copy.11), channel_id=1, replica_groups=mesh['basis'=4,'fit'=8] {'basis'}, dimensions={0}, use_global_device_ids=true | all-gather | bytes 81920 | tf_op jit(solution)/shard_map/all_gather | solution.py:16
  16.2 0.6 gather_fusion
  16.8 0.1 broadcast_select_fusion
  16.9 0.1 copy.13
  17.0 2.6 %broadcast_multiply_fusion = bf16[128,16,1024]{2,1,0:T(8,128)(2,1)S(1)} fusion(bf16[128,16,1024]{2,1,0:T(8,128)(2,1)} %param.5, bf16[128,1024]{1,0:T(8,128)(2,1)S(1)} %copy.13), kind=kLoop, calls=%fused_computation.4 | loop fusion | flops 2097152 | bytes 8650752 | tf_op jit(solution)/shard_map/mul | solution.py:20
  19.6 2.7 %copy.15 = bf16[16,8,16,1024]{3,1,2,0:T(8,128)(2,1)S(1)} copy(bf16[16,8,16,1024]{3,2,1,0:T(8,128)(2,1)S(1)} %bitcast.17) | data formatting | bytes 8388608
  22.4 2.8 %fusion.1 = f32[64,16384]{1,0:T(8,128)} fusion(bf16[128,64]{1,0:T(8,128)(2,1)S(1)} %bitcast.22, bf16[128,16384]{1,0:T(8,128)(2,1)S(1)} %bitcast.16), kind=kOutput, calls=%fused_computation.10 | convolution fusion | flops 268435456 | bytes 8404992 | tf_op jit(solution)/shard_map/dot_general | solution.py:25
  25.1 0.0 reduce-scatter.2.cloned.1.call-update
  25.1 0.0 all-gather.2.cloned.1.call-start
  25.2 46.3 %reduce-scatter.2.cloned.1.call-done = f32[16,16384]{1,0:T(8,128)} async-done(((f32[64,16384]{1,0:T(8,128)}), f32[16,16384]{1,0:T(8,128)}) %reduce-scatter.2.cloned.1.call-update) | async-done | bytes 1048592 | tf_op jit(solution)/shard_map/reduce_scatter | solution.py:24
  71.5 1.3 convert_element_type.13
  72.8 1.1 copy.16
  73.9 0.0 all-gather.2.cloned.1.call-update
  73.9 73.5 %all-gather.2.cloned.1.call-done = bf16[16,128,1024]{2,1,0:T(8,128)(2,1)} async-done(((bf16[16,16,1024]{2,1,0:T(8,128)(2,1)}), bf16[16,128,1024]{2,1,0:T(8,128)(2,1)}) %all-gather.2.cloned.1.call-update) | async-done | bytes 4194320 | tf_op jit(solution)/shard_map/all_gather | solution.py:35
  147.4 0.0 copy-done
  147.4 6.9 %convert_bitcast_fusion = bf16[128,16,1024]{2,0,1:T(8,128)(2,1)S(1)} fusion(bf16[16,128,1024]{2,1,0:T(8,128)(2,1)} %all-gather.2.cloned.1.call-done, bf16[1024,1024]{1,0:T(8,128)(2,1)S(1)} %copy-done), kind=kOutput, calls=%fused_computation.2 | convolution fusion | flops 4297064448 | bytes 10485760 | tf_op jit(solution)/shard_map/ipn,na->pia/dot_general | solution.py:33
  154.3 4.3 %copy.14 = bf16[128,16,1024]{2,1,0:T(8,128)(2,1)} copy(bf16[128,16,1024]{2,0,1:T(8,128)(2,1)S(1)} %convert_bitcast_fusion) | data formatting | bytes 8388608 | tf_op jit(solution)/shard_map/convert_element_type | solution.py:39
  (3 shorter events, 0.1 us)
Async XLA Ops:
  6.5 140.9 %copy-start = (bf16[1024,1024]{1,0:T(8,128)(2,1)S(1)}, bf16[1024,1024]{1,0:T(8,128)(2,1)}, u32[]{:S(2)}) copy-start(bf16[1024,1024]{1,0:T(8,128)(2,1)} %param.9) | copy-start | bytes 6291460
  6.5 65.0 %reduce-scatter.2.cloned.1.call-start = ((), (), s32[]{:S(2)}) async-start(), calls=%async_computation.1 | async-start | bytes 5242880 | tf_op jit(solution)/shard_map/reduce_scatter | solution.py:24
  25.1 122.3 %all-gather.2.cloned.1.call-start = ((), (), s32[]{:S(2)}) async-start(), calls=%async_computation.2 | async-start | bytes 4718592 | tf_op jit(solution)/shard_map/all_gather | solution.py:35
Sparse Core Ops, SparseCore 0:
  25.3 46.1 reduce-scatter.1
  74.0 73.3 all-gather.1
where the time goes:
time: 166 us
  waiting for transfers between devices  120 us (72%)
  between operations  13.5 us (8%)
  local copies, waits for them, and re-layouts  11.1 us (7%)
  matrix products  9.68 us (6%)
  blocking collectives  6.48 us (4%)
  other arithmetic  4.88 us (3%)
    all_gather x1, waiting for transfers between devices, shards(): lax.all_gather(half, 'fit', axis=1, tiled=True)  73.5 us
    reduce_scatter x1, waiting for transfers between devices, shards(): lax.psum_scatter(lax.dot_general(occ_rows, flat, (((0,), (0,)), ((), ()))...  46.3 us
    dot_general x1, matrix products, shards(): jnp.einsum('ipn,na->pia', lax.all_gather(half, 'fit', axis=1, tiled=True)...  6.92 us
    all_gather x1, blocking collectives, shards(): panels = lax.all_gather(occ_coef, 'basis', axis=0, tiled=True)  6.48 us
    unnamed x5, local copies, waits for them, and re-layouts  4.67 us
    convert_element_type x1, local copies, waits for them, and re-layouts, shards(): return product.astype(jnp.bfloat16)  4.34 us
  transfers between devices with their start and end apart: 2, of which 2 were waited for; matrix products, arithmetic and copies ran while one was open for 0% of the time, Pallas kernels for 0%

commit v1 on v0

--- a/solution.py
+++ b/solution.py
@@ -1,9 +1,178 @@
+import functools
+
 import jax
 import jax.numpy as jnp
 from jax import lax
+from jax.experimental import pallas as pl
+from jax.experimental.pallas import tpu as pltpu
 from jax.sharding import PartitionSpec as P
 
 BLK = 16
+CHUNKS = 2
+ZS, YS = 4, 2
+TILE = 256
+
+CORE_SWAP = [(0, 1), (1, 0), (2, 3), (3, 2)]
+X_SWAP = [(0, 2), (2, 0), (1, 3), (3, 1)]
+Y_SWAP = [(f, f ^ 1) for f in range(ZS * YS)]
+Z_RING = [(f, (f + YS) % (ZS * YS)) for f in range(ZS * YS)]
+
+
+def half_kernel(chunk, p_chunk, fit_dev, share, scal, occ_ref, pm_ref, x_ref, own_ref, send_ref, w_ref, m_ref):
+    nblk = scal.shape[0] - 4
+    step = pl.program_id(0)
+    depth = BLK * fit_dev
+
+    @pl.when(step == 0)
+    def _():
+        lane = lax.broadcasted_iota(jnp.int32, (BLK, depth), 1)
+        row = lax.broadcasted_iota(jnp.int32, (BLK, depth), 0)
+        spread = (lane // fit_dev == row).astype(jnp.float32).astype(jnp.bfloat16)
+        pos = lax.broadcasted_iota(jnp.int32, (share, depth), 1) % fit_dev
+        for b in range(nblk):
+            rb = scal[4 + b]
+            occ_b = occ_ref[pl.ds(pl.multiple_of(rb * BLK, BLK), BLK), :]
+            wide = lax.dot_general(occ_b, spread, (((0,), (0,)), ((), ())), preferred_element_type=jnp.float32)
+            m_ref[pl.ds(b, 1), :] = pm_ref[pl.ds(rb, 1), :].astype(jnp.float32)
+            for d in range(4):
+                part = wide[d * share : (d + 1) * share, :]
+                for p in range(p_chunk):
+                    val = jnp.where(pos == chunk * p_chunk + p, part, 0.0).astype(jnp.bfloat16)
+                    base = scal[d] * (p_chunk * share) + p * share
+                    w_ref[pl.ds(pl.multiple_of(base, share), share), b * depth : (b + 1) * depth] = val
+
+    nnb = pm_ref.shape[1]
+    tile = x_ref.shape[1]
+    col = (lax.broadcasted_iota(jnp.int32, (nnb, tile), 1) + step * tile) // BLK
+    blk = lax.broadcasted_iota(jnp.int32, (nnb, tile), 0)
+    pick = (col == blk).astype(jnp.float32).astype(jnp.bfloat16)
+    mask = jnp.dot(m_ref[...].astype(jnp.bfloat16), pick, preferred_element_type=jnp.float32).astype(jnp.bfloat16)
+    xm = jnp.concatenate(
+        [x_ref[b * depth : (b + 1) * depth, :] * mask[b : b + 1, :] for b in range(nblk)], axis=0
+    )
+    out = jnp.dot(w_ref[...], xm, preferred_element_type=jnp.float32)
+    rows = 2 * p_chunk * share
+    own_ref[...] = out[:rows].reshape(own_ref.shape)
+    send_ref[...] = out[rows:].astype(jnp.bfloat16).reshape(send_ref.shape)
+
+
+def half_chunk(chunk, scal, occ_all, pair_mask, flat, fit_dev, share):
+    p_chunk = fit_dev // CHUNKS
+    rows, nu = flat.shape
+    nblk = rows // (BLK * fit_dev)
+    out_rows = 2 * p_chunk * share
+    return pl.pallas_call(
+        functools.partial(half_kernel, chunk, p_chunk, fit_dev, share),
+        grid_spec=pltpu.PrefetchScalarGridSpec(
+            num_scalar_prefetch=1,
+            grid=(nu // TILE,),
+            in_specs=[
+                pl.BlockSpec(occ_all.shape, lambda j, s: (0, 0)),
+                pl.BlockSpec(pair_mask.shape, lambda j, s: (0, 0)),
+                pl.BlockSpec((rows, TILE), lambda j, s: (0, j)),
+            ],
+            out_specs=[
+                pl.BlockSpec((out_rows, TILE), lambda j, s: (0, j)),
+                pl.BlockSpec((out_rows, TILE), lambda j, s: (0, j)),
+            ],
+            scratch_shapes=[
+                pltpu.VMEM((2 * out_rows, rows), jnp.bfloat16),
+                pltpu.VMEM((nblk, pair_mask.shape[1]), jnp.float32),
+            ],
+        ),
+        out_shape=[
+            jax.ShapeDtypeStruct((out_rows, nu), jnp.float32),
+            jax.ShapeDtypeStruct((out_rows, nu), jnp.bfloat16),
+        ],
+        compiler_params=pltpu.CompilerParams(vmem_limit_bytes=32 * 2**20),
+        cost_estimate=pl.CostEstimate(
+            flops=2 * 2 * out_rows * rows * nu, bytes_accessed=rows * nu * 2 + out_rows * nu * 6, transcendentals=0
+        ),
+        name="half_chunk",
+    )(scal, occ_all, pair_mask, flat)
+
+
+def project_kernel(n_h, idx, *refs):
+    h_refs, vir_ref, out_ref = refs[:n_h], refs[n_h], refs[-1]
+    which = pl.program_id(0)
+    for k in range(n_h):
+
+        @pl.when(which == k)
+        def _(k=k):
+            out_ref[...] = jnp.dot(
+                h_refs[k][...], vir_ref[...], preferred_element_type=jnp.float32
+            ).astype(jnp.bfloat16)
+
+
+def project(out, idx, hs, vir, total_rows):
+    rows, nu = hs[0].shape
+    nv = vir.shape[1]
+    n_h = len(hs)
+    ops = [idx, *hs, vir] + ([] if out is None else [out])
+    return pl.pallas_call(
+        functools.partial(project_kernel, n_h),
+        grid_spec=pltpu.PrefetchScalarGridSpec(
+            num_scalar_prefetch=1,
+            grid=(n_h,),
+            in_specs=[pl.BlockSpec((rows, nu), lambda g, s: (0, 0)) for _ in hs]
+            + [pl.BlockSpec(vir.shape, lambda g, s: (0, 0))]
+            + ([] if out is None else [pl.BlockSpec(memory_space=pl.ANY)]),
+            out_specs=pl.BlockSpec((rows, nv), lambda g, s: (s[g], 0)),
+        ),
+        out_shape=jax.ShapeDtypeStruct((total_rows, nv), jnp.bfloat16),
+        input_output_aliases={} if out is None else {len(ops) - 1: 0},
+        compiler_params=pltpu.CompilerParams(vmem_limit_bytes=32 * 2**20),
+        cost_estimate=pl.CostEstimate(
+            flops=2 * n_h * rows * nu * nv, bytes_accessed=n_h * rows * (nu + nv) * 2 + nu * nv * 2, transcendentals=0
+        ),
+        name="project",
+    )(*ops)
+
+
+def shards_blocked(integrals, pair_mask, row_blocks, occ_coef, vir_coef):
+    mu_dev, fit_dev, nu = integrals.shape
+    nocc = occ_coef.shape[1]
+    nbas, nfit = lax.axis_size("basis"), lax.axis_size("fit")
+    share = nocc // nbas
+    nblk = mu_dev // BLK
+    p_chunk = fit_dev // CHUNKS
+    me = lax.axis_index("basis")
+    x, c = me // 2, me % 2
+    f = lax.axis_index("fit")
+    z, y = f // YS, f % YS
+
+    pair = lax.ppermute(occ_coef, "basis", CORE_SWAP)
+    two = jnp.where(c == 0, jnp.concatenate([occ_coef, pair]), jnp.concatenate([pair, occ_coef]))
+    far = lax.ppermute(two, "basis", X_SWAP)
+    occ_all = jnp.where(x == 0, jnp.concatenate([two, far]), jnp.concatenate([far, two]))
+
+    owned = lax.dynamic_slice_in_dim(row_blocks, me * nblk, nblk)
+    dest = jnp.arange(nbas, dtype=jnp.int32)
+    place = (dest // 2 != x).astype(jnp.int32) + 2 * (dest % 2 != c).astype(jnp.int32)
+    scal = jnp.concatenate([place, owned.astype(jnp.int32)])
+    flat = integrals.reshape(mu_dev * fit_dev, nu)
+
+    halves = []
+    for k in range(CHUNKS):
+        own, send = half_chunk(k, scal, occ_all, pair_mask, flat, fit_dev, share)
+        n = p_chunk * share
+        got = lax.ppermute(send, "basis", CORE_SWAP)
+        to_x = (own[n:] + got[n:].astype(jnp.float32)).astype(jnp.bfloat16)
+        from_x = lax.ppermute(to_x, "basis", X_SWAP)
+        halves.append((own[:n] + got[:n].astype(jnp.float32) + from_x.astype(jnp.float32)).astype(jnp.bfloat16))
+
+    total = nfit * fit_dev * share
+    out = None
+    held = list(halves)
+    for s in range(ZS):
+        for k in range(CHUNKS):
+            src_z = (z - s) % ZS
+            other = lax.ppermute(held[k], "fit", Y_SWAP)
+            idx = jnp.stack([(src_z * YS + y) * CHUNKS + k, (src_z * YS + 1 - y) * CHUNKS + k]).astype(jnp.int32)
+            out = project(out, idx, [held[k], other], vir_coef, total)
+            if s < ZS - 1:
+                held[k] = lax.ppermute(held[k], "fit", Z_RING)
+    return out.reshape(nfit * fit_dev, share, vir_coef.shape[1])
 
 
 def shards(integrals, pair_mask, row_blocks, occ_coef, vir_coef):
@@ -41,6 +210,5 @@
 
 def solution(mesh):
     placed = (P("basis", "fit", None), P(), P(), P("basis", None), P(None, "fit"))
-    return jax.shard_map(
-        shards, mesh=mesh, in_specs=placed, out_specs=P(None, "basis", "fit"), check_vma=False
-    )
+    body = shards_blocked if (mesh.shape["basis"], mesh.shape["fit"]) == (4, ZS * YS) else shards
+    return jax.shard_map(body, mesh=mesh, in_specs=placed, out_specs=P(None, "basis", "fit"), check_vma=False)

time: 166 us -> 96.2 us (0.58)
  waiting for transfers between devices: 120 us -> 31.7 us
  Pallas kernels: 0 us -> 33.1 us
  starting transfers between devices: 0.04 us -> 22.3 us
  between operations: 13.5 us -> 0.11 us
  matrix products: 9.68 us -> 0 us
  local copies, waits for them, and re-layouts: 11.1 us -> 4.53 us
  blocking collectives: 6.48 us -> 0 us
    all_gather x1 -> x0, waiting for transfers between devices: 73.5 us -> none  [shards(): lax.all_gather(half, 'fit', axis=1, tiled=True)]
    reduce_scatter x1 -> x0, waiting for transfers between devices: 46.3 us -> none  [shards(): lax.psum_scatter(lax.dot_general(occ_rows, flat, (((0,), (0,)), ((), ()))...]
    pallas_call x0 -> x10, Pallas kernels: none -> 33.1 us  [the longest x8 22.4 us: project(): pl.pallas_call(functools.partial(project_kernel, n_h), grid_spec=pltpu.Pr...]
    ppermute x0 -> x20, waiting for transfers between devices: none -> 31.7 us  [the longest x6 16.4 us: shards_blocked(): held[k] = lax.ppermute(held[k], 'fit', Z_RING)]
    ppermute x0 -> x20, starting transfers between devices: none -> 22.3 us  [the longest x8 11 us: shards_blocked(): other = lax.ppermute(held[k], 'fit', Y_SWAP)]
    dot_general x2 -> x0, matrix products: 9.68 us -> none  [the longest x1 6.92 us: shards(): jnp.einsum('ipn,na->pia', lax.all_gather(half, 'fit', axis=1, tiled=True)...]
    all_gather x1 -> x0, blocking collectives: 6.48 us -> none  [shards(): panels = lax.all_gather(occ_coef, 'basis', axis=0, tiled=True)]
    convert_element_type x1 -> x0, local copies, waits for them, and re-layouts: 4.34 us -> none  [shards(): return product.astype(jnp.bfloat16)]
  transfers between devices with their start and end apart: 2 -> 20, of which waited for: 2 -> 11; matrix products, arithmetic and copies ran while one was open for 0% -> 5% of each run, Pallas kernels for 0% -> 27%
where the time goes in v1:
time: 96.2 us; the launch traced here: 95.7 us
  Pallas kernels  33.1 us (34%)
  waiting for transfers between devices  31.7 us (33%)
  starting transfers between devices  22.3 us (23%)
  local copies, waits for them, and re-layouts  4.53 us (5%)
  other arithmetic  4.03 us (4%)
    pallas_call x8, Pallas kernels, project(): pl.pallas_call(functools.partial(project_kernel, n_h), grid_spec=pltpu.Pr...  22.4 us
    ppermute x6, waiting for transfers between devices, shards_blocked(): held[k] = lax.ppermute(held[k], 'fit', Z_RING)  16.4 us
    ppermute x8, starting transfers between devices, shards_blocked(): other = lax.ppermute(held[k], 'fit', Y_SWAP)  11 us
    pallas_call x2, Pallas kernels, half_chunk(): pl.pallas_call(functools.partial(half_kernel, chunk, p_chunk, fit_dev, sh...  10.7 us
    ppermute x2, waiting for transfers between devices, shards_blocked(): from_x = lax.ppermute(to_x, 'basis', X_SWAP)  6.77 us
    ppermute x8, waiting for transfers between devices, shards_blocked(): other = lax.ppermute(held[k], 'fit', Y_SWAP)  6.05 us
    ppermute x6, starting transfers between devices, shards_blocked(): held[k] = lax.ppermute(held[k], 'fit', Z_RING)  3.89 us
    unnamed x13, local copies, waits for them, and re-layouts  3.81 us
  transfers between devices with their start and end apart: 20, of which 11 were waited for; matrix products, arithmetic and copies ran while one was open for 5% of the time, Pallas kernels for 27%

profile of v1, /device:TPU:0, one launch (start us, length us, event | category | flops | bytes accessed | tf_op | source)
XLA Modules:
  0.0 95.7 jit_solution(3325435023122030792)
XLA Ops:
  2.2 2.9 %collective-permute-start.1 = (bf16[256,64]{1,0:T(8,128)(2,1)S(1)}, bf16[256,64]{1,0:T(8,128)(2,1)S(1)}, u32[]{:S(2)}, u32[]{:S(2)}) collective-permute-start(bf16[256,64]{1,0:T(8,128)(2,1)S(1)} %maximum_select_fusion.1), channel_id=1, source_target_pairs={{0,16},{16,0},{8,24},{24,8},{1,17},{17,1},{9,25},{25,9},{2,18},{18... | collective-permute-start | bytes 98312 | tf_op jit(solution)/shard_map/ppermute | solution.py:146
  5.2 2.3 %collective-permute-done.1 = bf16[256,64]{1,0:T(8,128)(2,1)S(1)} collective-permute-done((bf16[256,64]{1,0:T(8,128)(2,1)S(1)}, bf16[256,64]{1,0:T(8,128)(2,1)S(1)}, u32[]{:S(2)}, u32[]{:S(2)}) %collective-permute-start.1) | collective-permute-done | bytes 32800 | tf_op jit(solution)/shard_map/ppermute | solution.py:146
  7.6 2.2 %copy-done.2 = bf16[128,16,1024]{2,1,0:T(8,128)(2,1)S(1)} copy-done((bf16[128,16,1024]{2,1,0:T(8,128)(2,1)S(1)}, bf16[128,16,1024]{2,1,0:T(8,128)(2,1)}, u32[]{:S(2)}) %copy-start.2) | copy-done | bytes 4194328
  10.5 5.4 %half_chunk.3 = (f32[256,1024]{1,0:T(8,128)S(1)}, bf16[256,1024]{1,0:T(8,128)(2,1)S(1)}) custom-call(s32[12]{0:T(128)S(1)} %pad_add_fusion.1.scal, bf16[512,64]{1,0:T(8,128)(2,1)S(1)} %maximum_select_fusion.occ_ref, s32[32,64]{1,0:T(8,128)S(1)} %copy-done.3, bf16[2048,1024]{1,0:T(8,128)(2,1)S(1)} %bitcast.18), custom_call_target="tpu_custom_call" | custom-call | flops 2147483648 | bytes 5767168 | tf_op jit(solution)/shard_map/half_chunk/pallas_call | solution.py:64
  15.9 5.4 %half_chunk.2 = (f32[256,1024]{1,0:T(8,128)S(1)}, bf16[256,1024]{1,0:T(8,128)(2,1)S(1)}) custom-call(s32[12]{0:T(128)S(1)} %pad_add_fusion.1.scal, bf16[512,64]{1,0:T(8,128)(2,1)S(1)} %maximum_select_fusion.occ_ref, s32[32,64]{1,0:T(8,128)S(1)} %copy-done.3, bf16[2048,1024]{1,0:T(8,128)(2,1)S(1)} %bitcast.19), custom_call_target="tpu_custom_call" | custom-call | flops 2147483648 | bytes 5767168 | tf_op jit(solution)/shard_map/half_chunk/pallas_call | solution.py:64
  22.0 1.9 %collective-permute-start.9 = (bf16[128,1024]{1,0:T(8,128)(2,1)S(1)}, bf16[128,1024]{1,0:T(8,128)(2,1)}, u32[]{:S(2)}, u32[]{:S(2)}) collective-permute-start(bf16[128,1024]{1,0:T(8,128)(2,1)S(1)} %add_convert_fusion.1), channel_id=1, source_target_pairs={{0,16},{16,0},{8,24},{24,8},{1,17},{17,1},{9,25},{25,9},{2,18},{18... | collective-permute-start | bytes 786440 | tf_op jit(solution)/shard_map/ppermute | solution.py:161
  24.8 1.4 %collective-permute-start.3 = (bf16[128,1024]{1,0:T(8,128)(2,1)}, bf16[128,1024]{1,0:T(8,128)(2,1)}, u32[]{:S(2)}, u32[]{:S(2)}) collective-permute-start(bf16[128,1024]{1,0:T(8,128)(2,1)} %add_convert_fusion.3), channel_id=1, source_target_pairs={{0,16},{16,0},{8,24},{24,8},{1,17},{17,1},{9,25},{25,9},{2,18},{18... | collective-permute-start | bytes 786440 | tf_op jit(solution)/shard_map/ppermute | solution.py:161
  26.2 5.1 %collective-permute-done.9 = bf16[128,1024]{1,0:T(8,128)(2,1)} collective-permute-done((bf16[128,1024]{1,0:T(8,128)(2,1)S(1)}, bf16[128,1024]{1,0:T(8,128)(2,1)}, u32[]{:S(2)}, u32[]{:S(2)}) %collective-permute-start.9) | collective-permute-done | bytes 262176 | tf_op jit(solution)/shard_map/ppermute | solution.py:161
  32.4 2.0 %collective-permute-start.10 = (bf16[128,1024]{1,0:T(8,128)(2,1)S(1)}, bf16[128,1024]{1,0:T(8,128)(2,1)S(1)}, u32[]{:S(2)}, u32[]{:S(2)}) collective-permute-start(bf16[128,1024]{1,0:T(8,128)(2,1)S(1)} %add_convert_fusion.refs_0_), channel_id=1, source_target_pairs={{0,2},{1,3},{2,4},{3,5},{4,6},{5,7},{6,0},{7,1},{8,10},{9,11},{10,... | collective-permute-start | bytes 786440 | tf_op jit(solution)/shard_map/ppermute | solution.py:174
  34.4 1.7 %collective-permute-done.3 = bf16[128,1024]{1,0:T(8,128)(2,1)} collective-permute-done((bf16[128,1024]{1,0:T(8,128)(2,1)}, bf16[128,1024]{1,0:T(8,128)(2,1)}, u32[]{:S(2)}, u32[]{:S(2)}) %collective-permute-start.3) | collective-permute-done | bytes 262176 | tf_op jit(solution)/shard_map/ppermute | solution.py:161
  36.1 1.3 %add_convert_fusion.2.refs_0_ = bf16[128,1024]{1,0:T(8,128)(2,1)S(1)} fusion(bf16[128,1024]{1,0:T(8,128)(2,1)} %collective-permute-done.3, f32[256,1024]{1,0:T(8,128)} %copy-done.1, bf16[256,1024]{1,0:T(8,128)(2,1)} %copy-done.4), kind=kLoop, calls=%fused_computation.2 | loop fusion | flops 655360 | bytes 1310720 | tf_op jit(solution)/shard_map/convert_element_type | solution.py:162
  37.4 1.9 %collective-permute-start.4 = (bf16[128,1024]{1,0:T(8,128)(2,1)S(1)}, bf16[128,1024]{1,0:T(8,128)(2,1)S(1)}, u32[]{:S(2)}, u32[]{:S(2)}) collective-permute-start(bf16[128,1024]{1,0:T(8,128)(2,1)S(1)} %add_convert_fusion.2.refs_0_), channel_id=1, source_target_pairs={{0,2},{1,3},{2,4},{3,5},{4,6},{5,7},{6,0},{7,1},{8,10},{9,11},{10,... | collective-permute-start | bytes 786440 | tf_op jit(solution)/shard_map/ppermute | solution.py:174
  39.4 1.8 %collective-permute-done.10.refs_0_ = bf16[128,1024]{1,0:T(8,128)(2,1)S(1)} collective-permute-done((bf16[128,1024]{1,0:T(8,128)(2,1)S(1)}, bf16[128,1024]{1,0:T(8,128)(2,1)S(1)}, u32[]{:S(2)}, u32[]{:S(2)}) %collective-permute-start.10) | collective-permute-done | bytes 262176 | tf_op jit(solution)/shard_map/ppermute | solution.py:174
  41.3 7.3 %collective-permute-done.4.refs_0_ = bf16[128,1024]{1,0:T(8,128)(2,1)S(1)} collective-permute-done((bf16[128,1024]{1,0:T(8,128)(2,1)S(1)}, bf16[128,1024]{1,0:T(8,128)(2,1)S(1)}, u32[]{:S(2)}, u32[]{:S(2)}) %collective-permute-start.4) | collective-permute-done | bytes 262176 | tf_op jit(solution)/shard_map/ppermute | solution.py:174
  48.6 1.8 %collective-permute-start.19 = (bf16[128,1024]{1,0:T(8,128)(2,1)S(1)}, bf16[128,1024]{1,0:T(8,128)(2,1)}, u32[]{:S(2)}, u32[]{:S(2)}) collective-permute-start(bf16[128,1024]{1,0:T(8,128)(2,1)S(1)} %add_convert_fusion.refs_0_), channel_id=1, source_target_pairs={{0,1},{1,0},{2,3},{3,2},{4,5},{5,4},{6,7},{7,6},{8,9},{9,8},{10,11... | collective-permute-start | bytes 786440 | tf_op jit(solution)/shard_map/ppermute | solution.py:170
  50.7 1.7 %collective-permute-start.17 = (bf16[128,1024]{1,0:T(8,128)(2,1)S(1)}, bf16[128,1024]{1,0:T(8,128)(2,1)}, u32[]{:S(2)}, u32[]{:S(2)}) collective-permute-start(bf16[128,1024]{1,0:T(8,128)(2,1)S(1)} %collective-permute-done.10.refs_0_), channel_id=1, source_target_pairs={{0,1},{1,0},{2,3},{3,2},{4,5},{5,4},{6,7},{7,6},{8,9},{9,8},{10,11... | collective-permute-start | bytes 786440 | tf_op jit(solution)/shard_map/ppermute | solution.py:170
  52.5 1.7 %collective-permute-done.11.refs_0_ = bf16[128,1024]{1,0:T(8,128)(2,1)S(1)} collective-permute-done((bf16[128,1024]{1,0:T(8,128)(2,1)S(1)}, bf16[128,1024]{1,0:T(8,128)(2,1)S(1)}, u32[]{:S(2)}, u32[]{:S(2)}) %collective-permute-start.11) | collective-permute-done | bytes 262176 | tf_op jit(solution)/shard_map/ppermute | solution.py:174
  54.2 5.6 %collective-permute-done.5.refs_0_ = bf16[128,1024]{1,0:T(8,128)(2,1)} collective-permute-done((bf16[128,1024]{1,0:T(8,128)(2,1)S(1)}, bf16[128,1024]{1,0:T(8,128)(2,1)}, u32[]{:S(2)}, u32[]{:S(2)}) %collective-permute-start.5) | collective-permute-done | bytes 262176 | tf_op jit(solution)/shard_map/ppermute | solution.py:174
  59.9 1.8 %collective-permute-start.16 = (bf16[128,1024]{1,0:T(8,128)(2,1)S(1)}, bf16[128,1024]{1,0:T(8,128)(2,1)S(1)}, u32[]{:S(2)}, u32[]{:S(2)}) collective-permute-start(bf16[128,1024]{1,0:T(8,128)(2,1)S(1)} %collective-permute-done.4.refs_0_), channel_id=1, source_target_pairs={{0,1},{1,0},{2,3},{3,2},{4,5},{5,4},{6,7},{7,6},{8,9},{9,8},{10,11... | collective-permute-start | bytes 786440 | tf_op jit(solution)/shard_map/ppermute | solution.py:170
  61.7 1.9 %collective-permute-done.18.refs_1_ = bf16[128,1024]{1,0:T(8,128)(2,1)} collective-permute-done((bf16[128,1024]{1,0:T(8,128)(2,1)S(1)}, bf16[128,1024]{1,0:T(8,128)(2,1)}, u32[]{:S(2)}, u32[]{:S(2)}) %collective-permute-start.18) | collective-permute-done | bytes 262176 | tf_op jit(solution)/shard_map/ppermute | solution.py:170
  63.6 1.7 %collective-permute-start.15 = (bf16[128,1024]{1,0:T(8,128)(2,1)S(1)}, bf16[128,1024]{1,0:T(8,128)(2,1)S(1)}, u32[]{:S(2)}, u32[]{:S(2)}) collective-permute-start(bf16[128,1024]{1,0:T(8,128)(2,1)S(1)} %collective-permute-done.11.refs_0_), channel_id=1, source_target_pairs={{0,1},{1,0},{2,3},{3,2},{4,5},{5,4},{6,7},{7,6},{8,9},{9,8},{10,11... | collective-permute-start | bytes 786440 | tf_op jit(solution)/shard_map/ppermute | solution.py:170
  65.3 3.9 %collective-permute-done.17.refs_1_ = bf16[128,1024]{1,0:T(8,128)(2,1)} collective-permute-done((bf16[128,1024]{1,0:T(8,128)(2,1)S(1)}, bf16[128,1024]{1,0:T(8,128)(2,1)}, u32[]{:S(2)}, u32[]{:S(2)}) %collective-permute-start.17) | collective-permute-done | bytes 262176 | tf_op jit(solution)/shard_map/ppermute | solution.py:170
  69.2 1.7 %collective-permute-start.14 = (bf16[128,1024]{1,0:T(8,128)(2,1)}, bf16[128,1024]{1,0:T(8,128)(2,1)S(1)}, u32[]{:S(2)}, u32[]{:S(2)}) collective-permute-start(bf16[128,1024]{1,0:T(8,128)(2,1)} %collective-permute-done.5.refs_0_), channel_id=1, source_target_pairs={{0,1},{1,0},{2,3},{3,2},{4,5},{5,4},{6,7},{7,6},{8,9},{9,8},{10,11... | collective-permute-start | bytes 786440 | tf_op jit(solution)/shard_map/ppermute | solution.py:170
  71.3 3.1 %project.8.refs_3_ = bf16[2048,1024]{1,0:T(8,128)(2,1)} custom-call(s32[2]{0:T(128)S(1)} %pad_add_fusion.8.idx, bf16[128,1024]{1,0:T(8,128)(2,1)S(1)} %add_convert_fusion.refs_0_, bf16[128,1024]{1,0:T(8,128)(2,1)} %collective-permute-done.19.refs_1_, bf16[1024,1024]{1,0:T(8,128)(2,1)S(1)} %copy-done), custom_call_target="tpu_custom_call" | custom-call | flops 536870912 | bytes 3145728 | tf_op jit(solution)/shard_map/project/pallas_call | solution.py:112
  74.5 1.7 %collective-permute-start.7 = (bf16[128,1024]{1,0:T(8,128)(2,1)S(1)}, bf16[128,1024]{1,0:T(8,128)(2,1)S(1)}, u32[]{:S(2)}, u32[]{:S(2)}) collective-permute-start(bf16[128,1024]{1,0:T(8,128)(2,1)S(1)} %collective-permute-done.6.refs_0_), channel_id=1, source_target_pairs={{0,1},{1,0},{2,3},{3,2},{4,5},{5,4},{6,7},{7,6},{8,9},{9,8},{10,11... | collective-permute-start | bytes 786440 | tf_op jit(solution)/shard_map/ppermute | solution.py:170
  76.2 3.2 %project.9.refs_3_ = bf16[2048,1024]{1,0:T(8,128)(2,1)} custom-call(s32[2]{0:T(128)S(1)} %pad_add_fusion.7.idx, bf16[128,1024]{1,0:T(8,128)(2,1)S(1)} %add_convert_fusion.2.refs_0_, bf16[128,1024]{1,0:T(8,128)(2,1)} %collective-permute-done.18.refs_1_, bf16[1024,1024]{1,0:T(8,128)(2,1)S(1)} %copy-done, ...), custom_call_target="tpu_custom_call", output_to_operand_aliasing={{}: (4, {})} | custom-call | flops 536870912 | bytes 3145728 | tf_op jit(solution)/shard_map/project/pallas_call | solution.py:112
  79.3 3.1 %project.10.refs_3_ = bf16[2048,1024]{1,0:T(8,128)(2,1)} custom-call(s32[2]{0:T(128)S(1)} %pad_add_fusion.6.idx, bf16[128,1024]{1,0:T(8,128)(2,1)S(1)} %collective-permute-done.10.refs_0_, bf16[128,1024]{1,0:T(8,128)(2,1)} %collective-permute-done.17.refs_1_, bf16[1024,1024]{1,0:T(8,128)(2,1)S(1)} %copy-done, ...), custom_call_target="tpu_custom_call", output_to_operand_aliasing={{}: (4, {})} | custom-call | flops 536870912 | bytes 3145728 | tf_op jit(solution)/shard_map/project/pallas_call | solution.py:112
  82.5 2.2 %project.11.refs_3_ = bf16[2048,1024]{1,0:T(8,128)(2,1)} custom-call(s32[2]{0:T(128)S(1)} %pad_add_fusion.5.idx, bf16[128,1024]{1,0:T(8,128)(2,1)S(1)} %collective-permute-done.4.refs_0_, bf16[128,1024]{1,0:T(8,128)(2,1)S(1)} %collective-permute-done.16.refs_1_, bf16[1024,1024]{1,0:T(8,128)(2,1)S(1)} %copy-done, ...), custom_call_target="tpu_custom_call", output_to_operand_aliasing={{}: (4, {})} | custom-call | flops 536870912 | bytes 3145728 | tf_op jit(solution)/shard_map/project/pallas_call | solution.py:112
  84.7 2.2 %project.12.refs_3_ = bf16[2048,1024]{1,0:T(8,128)(2,1)} custom-call(s32[2]{0:T(128)S(1)} %pad_add_fusion.4.idx, bf16[128,1024]{1,0:T(8,128)(2,1)S(1)} %collective-permute-done.11.refs_0_, bf16[128,1024]{1,0:T(8,128)(2,1)S(1)} %collective-permute-done.15.refs_1_, bf16[1024,1024]{1,0:T(8,128)(2,1)S(1)} %copy-done, ...), custom_call_target="tpu_custom_call", output_to_operand_aliasing={{}: (4, {})} | custom-call | flops 536870912 | bytes 3145728 | tf_op jit(solution)/shard_map/project/pallas_call | solution.py:112
  86.9 3.2 %project.13.refs_3_ = bf16[2048,1024]{1,0:T(8,128)(2,1)} custom-call(s32[2]{0:T(128)S(1)} %pad_add_fusion.3.idx, bf16[128,1024]{1,0:T(8,128)(2,1)} %collective-permute-done.5.refs_0_, bf16[128,1024]{1,0:T(8,128)(2,1)S(1)} %collective-permute-done.14.refs_1_, bf16[1024,1024]{1,0:T(8,128)(2,1)S(1)} %copy-done, ...), custom_call_target="tpu_custom_call", output_to_operand_aliasing={{}: (4, {})} | custom-call | flops 536870912 | bytes 3145728 | tf_op jit(solution)/shard_map/project/pallas_call | solution.py:112
  90.3 3.1 %project.14.refs_3_ = bf16[2048,1024]{1,0:T(8,128)(2,1)} custom-call(s32[2]{0:T(128)S(1)} %pad_add_fusion.2.idx, bf16[128,1024]{1,0:T(8,128)(2,1)} %collective-permute-done.12.refs_0_, bf16[128,1024]{1,0:T(8,128)(2,1)S(1)} %collective-permute-done.13.refs_1_, bf16[1024,1024]{1,0:T(8,128)(2,1)S(1)} %copy-done, ...), custom_call_target="tpu_custom_call", output_to_operand_aliasing={{}: (4, {})} | custom-call | flops 536870912 | bytes 3145728 | tf_op jit(solution)/shard_map/project/pallas_call | solution.py:112
  93.5 2.2 %project.15 = bf16[2048,1024]{1,0:T(8,128)(2,1)} custom-call(s32[2]{0:T(128)S(1)} %pad_add_fusion.idx, bf16[128,1024]{1,0:T(8,128)(2,1)S(1)} %collective-permute-done.6.refs_0_, bf16[128,1024]{1,0:T(8,128)(2,1)S(1)} %collective-permute-done.7.refs_1_, bf16[1024,1024]{1,0:T(8,128)(2,1)S(1)} %copy-done, ...), custom_call_target="tpu_custom_call", output_to_operand_aliasing={{}: (4, {})} | custom-call | flops 536870912 | bytes 3145728 | tf_op jit(solution)/shard_map/project/pallas_call | solution.py:112
  (48 shorter events, 7.3 us)
Async XLA Ops:
  0.8 1.4 %collective-permute-start = (bf16[128,64]{1,0:T(8,128)(2,1)S(1)}, bf16[128,64]{1,0:T(8,128)(2,1)S(1)}, u32[]{:S(2)}, u32[]{:S(2)}) collective-permute-start(bf16[128,64]{1,0:T(8,128)(2,1)S(1)} %copy.14), channel_id=1, source_target_pairs={{0,8},{8,0},{16,24},{24,16},{1,9},{9,1},{17,25},{25,17},{2,10},{10... | collective-permute-start | bytes 49160 | tf_op jit(solution)/shard_map/ppermute | solution.py:144
  2.2 5.3 %collective-permute-start.1 = (bf16[256,64]{1,0:T(8,128)(2,1)S(1)}, bf16[256,64]{1,0:T(8,128)(2,1)S(1)}, u32[]{:S(2)}, u32[]{:S(2)}) collective-permute-start(bf16[256,64]{1,0:T(8,128)(2,1)S(1)} %maximum_select_fusion.1), channel_id=1, source_target_pairs={{0,16},{16,0},{8,24},{24,8},{1,17},{17,1},{9,25},{25,9},{2,18},{18... | collective-permute-start | bytes 98312 | tf_op jit(solution)/shard_map/ppermute | solution.py:146
  7.6 2.2 %copy-start.2 = (bf16[128,16,1024]{2,1,0:T(8,128)(2,1)S(1)}, bf16[128,16,1024]{2,1,0:T(8,128)(2,1)}, u32[]{:S(2)}) copy-start(bf16[128,16,1024]{2,1,0:T(8,128)(2,1)} %param.5) | copy-start | bytes 12582916
  9.8 0.7 copy-start.3
  15.9 6.0 %collective-permute-start.8 = (bf16[256,1024]{1,0:T(8,128)(2,1)S(1)}, bf16[256,1024]{1,0:T(8,128)(2,1)S(1)}, u32[]{:S(2)}, u32[]{:S(2)}) collective-permute-start(bf16[256,1024]{1,0:T(8,128)(2,1)S(1)} %get-tuple-element.12), channel_id=1, source_target_pairs={{0,8},{8,0},{16,24},{24,16},{1,9},{9,1},{17,25},{25,17},{2,10},{10... | collective-permute-start | bytes 1572872 | tf_op jit(solution)/shard_map/ppermute | solution.py:159
  21.3 2.6 %copy-start.1 = (f32[256,1024]{1,0:T(8,128)}, f32[256,1024]{1,0:T(8,128)S(1)}, u32[]{:S(2)}) copy-start(f32[256,1024]{1,0:T(8,128)S(1)} %get-tuple-element.9) | copy-start | bytes 3145732
  21.3 50.0 %copy-start = (bf16[1024,1024]{1,0:T(8,128)(2,1)S(1)}, bf16[1024,1024]{1,0:T(8,128)(2,1)}, u32[]{:S(2)}) copy-start(bf16[1024,1024]{1,0:T(8,128)(2,1)} %refs_2_.15) | copy-start | bytes 6291460
  21.3 2.5 %collective-permute-start.2 = (bf16[256,1024]{1,0:T(8,128)(2,1)S(1)}, bf16[256,1024]{1,0:T(8,128)(2,1)S(1)}, u32[]{:S(2)}, u32[]{:S(2)}) collective-permute-start(bf16[256,1024]{1,0:T(8,128)(2,1)S(1)} %get-tuple-element.10), channel_id=1, source_target_pairs={{0,8},{8,0},{16,24},{24,16},{1,9},{9,1},{17,25},{25,17},{2,10},{10... | collective-permute-start | bytes 1572872 | tf_op jit(solution)/shard_map/ppermute | solution.py:159
  21.9 2.8 %copy-start.5 = (bf16[256,1024]{1,0:T(8,128)(2,1)}, bf16[256,1024]{1,0:T(8,128)(2,1)S(1)}, u32[]{:S(2)}) copy-start(bf16[256,1024]{1,0:T(8,128)(2,1)S(1)} %collective-permute-done.8) | copy-start | bytes 1572868
  22.0 9.3 %collective-permute-start.9 = (bf16[128,1024]{1,0:T(8,128)(2,1)S(1)}, bf16[128,1024]{1,0:T(8,128)(2,1)}, u32[]{:S(2)}, u32[]{:S(2)}) collective-permute-start(bf16[128,1024]{1,0:T(8,128)(2,1)S(1)} %add_convert_fusion.1), channel_id=1, source_target_pairs={{0,16},{16,0},{8,24},{24,8},{1,17},{17,1},{9,25},{25,9},{2,18},{18... | collective-permute-start | bytes 786440 | tf_op jit(solution)/shard_map/ppermute | solution.py:161
  23.9 0.9 copy-start.4
  24.8 11.3 %collective-permute-start.3 = (bf16[128,1024]{1,0:T(8,128)(2,1)}, bf16[128,1024]{1,0:T(8,128)(2,1)}, u32[]{:S(2)}, u32[]{:S(2)}) collective-permute-start(bf16[128,1024]{1,0:T(8,128)(2,1)} %add_convert_fusion.3), channel_id=1, source_target_pairs={{0,16},{16,0},{8,24},{24,8},{1,17},{17,1},{9,25},{25,9},{2,18},{18... | collective-permute-start | bytes 786440 | tf_op jit(solution)/shard_map/ppermute | solution.py:161
  32.4 8.8 %collective-permute-start.10 = (bf16[128,1024]{1,0:T(8,128)(2,1)S(1)}, bf16[128,1024]{1,0:T(8,128)(2,1)S(1)}, u32[]{:S(2)}, u32[]{:S(2)}) collective-permute-start(bf16[128,1024]{1,0:T(8,128)(2,1)S(1)} %add_convert_fusion.refs_0_), channel_id=1, source_target_pairs={{0,2},{1,3},{2,4},{3,5},{4,6},{5,7},{6,0},{7,1},{8,10},{9,11},{10,... | collective-permute-start | bytes 786440 | tf_op jit(solution)/shard_map/ppermute | solution.py:174
  37.4 11.1 %collective-permute-start.4 = (bf16[128,1024]{1,0:T(8,128)(2,1)S(1)}, bf16[128,1024]{1,0:T(8,128)(2,1)S(1)}, u32[]{:S(2)}, u32[]{:S(2)}) collective-permute-start(bf16[128,1024]{1,0:T(8,128)(2,1)S(1)} %add_convert_fusion.2.refs_0_), channel_id=1, source_target_pairs={{0,2},{1,3},{2,4},{3,5},{4,6},{5,7},{6,0},{7,1},{8,10},{9,11},{10,... | collective-permute-start | bytes 786440 | tf_op jit(solution)/shard_map/ppermute | solution.py:174
  41.2 13.0 %collective-permute-start.11 = (bf16[128,1024]{1,0:T(8,128)(2,1)S(1)}, bf16[128,1024]{1,0:T(8,128)(2,1)S(1)}, u32[]{:S(2)}, u32[]{:S(2)}) collective-permute-start(bf16[128,1024]{1,0:T(8,128)(2,1)S(1)} %collective-permute-done.10.refs_0_), channel_id=1, source_target_pairs={{0,2},{1,3},{2,4},{3,5},{4,6},{5,7},{6,0},{7,1},{8,10},{9,11},{10,... | collective-permute-start | bytes 786440 | tf_op jit(solution)/shard_map/ppermute | solution.py:174
  48.5 11.3 %collective-permute-start.5 = (bf16[128,1024]{1,0:T(8,128)(2,1)S(1)}, bf16[128,1024]{1,0:T(8,128)(2,1)}, u32[]{:S(2)}, u32[]{:S(2)}) collective-permute-start(bf16[128,1024]{1,0:T(8,128)(2,1)S(1)} %collective-permute-done.4.refs_0_), channel_id=1, source_target_pairs={{0,2},{1,3},{2,4},{3,5},{4,6},{5,7},{6,0},{7,1},{8,10},{9,11},{10,... | collective-permute-start | bytes 786440 | tf_op jit(solution)/shard_map/ppermute | solution.py:174
  48.6 11.3 %collective-permute-start.19 = (bf16[128,1024]{1,0:T(8,128)(2,1)S(1)}, bf16[128,1024]{1,0:T(8,128)(2,1)}, u32[]{:S(2)}, u32[]{:S(2)}) collective-permute-start(bf16[128,1024]{1,0:T(8,128)(2,1)S(1)} %add_convert_fusion.refs_0_), channel_id=1, source_target_pairs={{0,1},{1,0},{2,3},{3,2},{4,5},{5,4},{6,7},{7,6},{8,9},{9,8},{10,11... | collective-permute-start | bytes 786440 | tf_op jit(solution)/shard_map/ppermute | solution.py:170
  50.4 13.2 %collective-permute-start.18 = (bf16[128,1024]{1,0:T(8,128)(2,1)S(1)}, bf16[128,1024]{1,0:T(8,128)(2,1)}, u32[]{:S(2)}, u32[]{:S(2)}) collective-permute-start(bf16[128,1024]{1,0:T(8,128)(2,1)S(1)} %add_convert_fusion.2.refs_0_), channel_id=1, source_target_pairs={{0,1},{1,0},{2,3},{3,2},{4,5},{5,4},{6,7},{7,6},{8,9},{9,8},{10,11... | collective-permute-start | bytes 786440 | tf_op jit(solution)/shard_map/ppermute | solution.py:170
  50.7 18.6 %collective-permute-start.17 = (bf16[128,1024]{1,0:T(8,128)(2,1)S(1)}, bf16[128,1024]{1,0:T(8,128)(2,1)}, u32[]{:S(2)}, u32[]{:S(2)}) collective-permute-start(bf16[128,1024]{1,0:T(8,128)(2,1)S(1)} %collective-permute-done.10.refs_0_), channel_id=1, source_target_pairs={{0,1},{1,0},{2,3},{3,2},{4,5},{5,4},{6,7},{7,6},{8,9},{9,8},{10,11... | collective-permute-start | bytes 786440 | tf_op jit(solution)/shard_map/ppermute | solution.py:170
  54.1 16.9 %collective-permute-start.12 = (bf16[128,1024]{1,0:T(8,128)(2,1)S(1)}, bf16[128,1024]{1,0:T(8,128)(2,1)}, u32[]{:S(2)}, u32[]{:S(2)}) collective-permute-start(bf16[128,1024]{1,0:T(8,128)(2,1)S(1)} %collective-permute-done.11.refs_0_), channel_id=1, source_target_pairs={{0,2},{1,3},{2,4},{3,5},{4,6},{5,7},{6,0},{7,1},{8,10},{9,11},{10,... | collective-permute-start | bytes 786440 | tf_op jit(solution)/shard_map/ppermute | solution.py:174
  59.9 14.6 %collective-permute-start.6 = (bf16[128,1024]{1,0:T(8,128)(2,1)}, bf16[128,1024]{1,0:T(8,128)(2,1)S(1)}, u32[]{:S(2)}, u32[]{:S(2)}) collective-permute-start(bf16[128,1024]{1,0:T(8,128)(2,1)} %collective-permute-done.5.refs_0_), channel_id=1, source_target_pairs={{0,2},{1,3},{2,4},{3,5},{4,6},{5,7},{6,0},{7,1},{8,10},{9,11},{10,... | collective-permute-start | bytes 786440 | tf_op jit(solution)/shard_map/ppermute | solution.py:174
  59.9 22.6 %collective-permute-start.16 = (bf16[128,1024]{1,0:T(8,128)(2,1)S(1)}, bf16[128,1024]{1,0:T(8,128)(2,1)S(1)}, u32[]{:S(2)}, u32[]{:S(2)}) collective-permute-start(bf16[128,1024]{1,0:T(8,128)(2,1)S(1)} %collective-permute-done.4.refs_0_), channel_id=1, source_target_pairs={{0,1},{1,0},{2,3},{3,2},{4,5},{5,4},{6,7},{7,6},{8,9},{9,8},{10,11... | collective-permute-start | bytes 786440 | tf_op jit(solution)/shard_map/ppermute | solution.py:170
  63.6 21.1 %collective-permute-start.15 = (bf16[128,1024]{1,0:T(8,128)(2,1)S(1)}, bf16[128,1024]{1,0:T(8,128)(2,1)S(1)}, u32[]{:S(2)}, u32[]{:S(2)}) collective-permute-start(bf16[128,1024]{1,0:T(8,128)(2,1)S(1)} %collective-permute-done.11.refs_0_), channel_id=1, source_target_pairs={{0,1},{1,0},{2,3},{3,2},{4,5},{5,4},{6,7},{7,6},{8,9},{9,8},{10,11... | collective-permute-start | bytes 786440 | tf_op jit(solution)/shard_map/ppermute | solution.py:170
  69.2 17.7 %collective-permute-start.14 = (bf16[128,1024]{1,0:T(8,128)(2,1)}, bf16[128,1024]{1,0:T(8,128)(2,1)S(1)}, u32[]{:S(2)}, u32[]{:S(2)}) collective-permute-start(bf16[128,1024]{1,0:T(8,128)(2,1)} %collective-permute-done.5.refs_0_), channel_id=1, source_target_pairs={{0,1},{1,0},{2,3},{3,2},{4,5},{5,4},{6,7},{7,6},{8,9},{9,8},{10,11... | collective-permute-start | bytes 786440 | tf_op jit(solution)/shard_map/ppermute | solution.py:170
  71.0 19.3 %collective-permute-start.13 = (bf16[128,1024]{1,0:T(8,128)(2,1)}, bf16[128,1024]{1,0:T(8,128)(2,1)S(1)}, u32[]{:S(2)}, u32[]{:S(2)}) collective-permute-start(bf16[128,1024]{1,0:T(8,128)(2,1)} %collective-permute-done.12.refs_0_), channel_id=1, source_target_pairs={{0,1},{1,0},{2,3},{3,2},{4,5},{5,4},{6,7},{7,6},{8,9},{9,8},{10,11... | collective-permute-start | bytes 786440 | tf_op jit(solution)/shard_map/ppermute | solution.py:170
  74.5 19.0 %collective-permute-start.7 = (bf16[128,1024]{1,0:T(8,128)(2,1)S(1)}, bf16[128,1024]{1,0:T(8,128)(2,1)S(1)}, u32[]{:S(2)}, u32[]{:S(2)}) collective-permute-start(bf16[128,1024]{1,0:T(8,128)(2,1)S(1)} %collective-permute-done.6.refs_0_), channel_id=1, source_target_pairs={{0,1},{1,0},{2,3},{3,2},{4,5},{5,4},{6,7},{7,6},{8,9},{9,8},{10,11... | collective-permute-start | bytes 786440 | tf_op jit(solution)/shard_map/ppermute | solution.py:170

commit v2 on v0

--- a/solution.py
+++ b/solution.py
@@ -1,9 +1,210 @@
+import functools
+
 import jax
 import jax.numpy as jnp
 from jax import lax
+from jax.experimental import pallas as pl
+from jax.experimental.pallas import tpu as pltpu
 from jax.sharding import PartitionSpec as P
 
 BLK = 16
+CHUNKS = 2
+ZS, YS = 4, 2
+
+CORE_SWAP = [(0, 1), (1, 0), (2, 3), (3, 2)]
+X_SWAP = [(0, 2), (2, 0), (1, 3), (3, 1)]
+DIAGONAL = [(0, 3), (3, 0), (1, 2), (2, 1)]
+Y_SWAP = [(f, f ^ 1) for f in range(ZS * YS)]
+Z_RING = [(f, (f + YS) % (ZS * YS)) for f in range(ZS * YS)]
+
+IN_ANY = pl.BlockSpec(memory_space=pl.ANY)
+IN_VMEM = pl.BlockSpec(memory_space=pltpu.VMEM)
+IN_SMEM = pl.BlockSpec(memory_space=pltpu.SMEM)
+
+
+def params():
+    return pltpu.CompilerParams(vmem_limit_bytes=16 * 2**20)
+
+
+def vmem(value):
+    return pltpu.with_memory_space_constraint(value, pltpu.VMEM)
+
+
+def order_kernel(me, row_blocks, mask_ref, flat_ref, out_ref, x_ref, sems):
+    rows, nu = x_ref.shape
+    fit_dev = out_ref.shape[0]
+    depth = BLK * fit_dev
+    nblk = rows // depth
+    nnb = mask_ref.shape[1]
+    copies = [
+        pltpu.make_async_copy(
+            flat_ref.at[pl.ds(b * depth, depth)], x_ref.at[pl.ds(b * depth, depth)], sems.at[b]
+        )
+        for b in range(nblk)
+    ]
+    for copy in copies:
+        copy.start()
+    to = lax.broadcasted_iota(jnp.int32, (depth, depth), 0)
+    at = lax.broadcasted_iota(jnp.int32, (depth, depth), 1)
+    turn = jnp.where((to // BLK == at % fit_dev) & (to % BLK == at // fit_dev), 1.0, 0.0).astype(jnp.bfloat16)
+    column = lax.broadcasted_iota(jnp.int32, (nnb, nu), 1) // BLK
+    block = lax.broadcasted_iota(jnp.int32, (nnb, nu), 0)
+    widen = jnp.where(column == block, 1.0, 0.0).astype(jnp.bfloat16)
+    owned = jnp.concatenate(
+        [mask_ref[pl.ds(row_blocks[me[0] * nblk + b], 1), :] for b in range(nblk)], axis=0
+    )
+    mask = jnp.dot(owned.astype(jnp.float32).astype(jnp.bfloat16), widen, preferred_element_type=jnp.float32)
+    for b in range(nblk):
+        copies[b].wait()
+        masked = x_ref[b * depth : (b + 1) * depth, :] * mask[b : b + 1, :].astype(jnp.bfloat16)
+        turned = jnp.dot(turn, masked, preferred_element_type=jnp.float32).astype(jnp.bfloat16)
+        out_ref[:, b * BLK : (b + 1) * BLK, :] = turned.reshape(fit_dev, BLK, nu)
+
+
+def order(me, row_blocks, pair_mask, integrals):
+    mu_dev, fit_dev, nu = integrals.shape
+    rows = mu_dev * fit_dev
+    nblk = mu_dev // BLK
+    return pl.pallas_call(
+        order_kernel,
+        in_specs=[IN_SMEM, IN_SMEM, IN_VMEM, IN_ANY],
+        out_specs=IN_VMEM,
+        scratch_shapes=[pltpu.VMEM((rows, nu), jnp.bfloat16), pltpu.SemaphoreType.DMA((nblk,))],
+        out_shape=pltpu.VMEM((fit_dev, mu_dev, nu), jnp.bfloat16),
+        compiler_params=params(),
+        cost_estimate=pl.CostEstimate(
+            flops=2 * rows * BLK * fit_dev * nu, bytes_accessed=rows * nu * 4, transcendentals=0
+        ),
+        name="order",
+    )(me, row_blocks, pair_mask, pltpu.with_memory_space_constraint(integrals.reshape(rows, nu), pltpu.HBM))
+
+
+def half_kernel(start, me_ref, row_blocks, own_occ, far_occ, core_occ, diag_occ, x_ref, own_ref, send_ref, occ_ref):
+    me = me_ref[0]
+    rows, nocc = own_occ.shape
+    nblk = rows // BLK
+    share = nocc // 4
+    x, c = me // 2, me % 2
+    device = [me, 2 * (1 - x) + c, 2 * x + 1 - c, 2 * (1 - x) + 1 - c]
+    for k, occ in enumerate((own_occ, far_occ, core_occ, diag_occ)):
+        occ_ref[pl.ds(pl.multiple_of(device[k] * rows, rows), rows), :] = occ[...]
+    to = lax.broadcasted_iota(jnp.int32, (nocc, nocc), 0)
+    at = lax.broadcasted_iota(jnp.int32, (nocc, nocc), 1)
+    dest = jnp.full((nocc, nocc), device[3], jnp.int32)
+    for k in range(3):
+        dest = jnp.where(to // share == k, device[k], dest)
+    pick = jnp.where((at // share == dest) & (at % share == to % share), 1.0, 0.0).astype(jnp.bfloat16)
+    mine = jnp.concatenate(
+        [occ_ref[pl.ds(pl.multiple_of(row_blocks[me * nblk + b] * BLK, BLK), BLK), :] for b in range(nblk)], axis=0
+    )
+    turned = lax.dot_general(pick, mine, (((1,), (1,)), ((), ())), preferred_element_type=jnp.float32)
+    turned = turned.astype(jnp.bfloat16)
+    zero = jnp.zeros_like(turned)
+    pair = jnp.concatenate(
+        [jnp.concatenate([turned, zero], axis=1), jnp.concatenate([zero, turned], axis=1)], axis=0
+    )
+    for u in range(0, own_ref.shape[1], 2):
+        both = x_ref[start + u : start + u + 2].reshape(2 * rows, x_ref.shape[2])
+        out = jnp.dot(pair, both, preferred_element_type=jnp.float32)
+        for v in range(2):
+            for k in range(2):
+                at_own, at_send = v * nocc + k * share, v * nocc + (2 + k) * share
+                own_ref[k, u + v] = out[at_own : at_own + share]
+                send_ref[k, u + v] = out[at_send : at_send + share].astype(jnp.bfloat16)
+
+
+def half_terms(me, row_blocks, occs, turned, start, count):
+    _, rows, nu = turned.shape
+    nocc = occs[0].shape[1]
+    share = nocc // 4
+    return pl.pallas_call(
+        functools.partial(half_kernel, start),
+        in_specs=[IN_SMEM, IN_SMEM] + [IN_VMEM] * 5,
+        out_specs=[IN_VMEM] * 2,
+        scratch_shapes=[pltpu.VMEM((4 * rows, nocc), jnp.bfloat16)],
+        out_shape=[
+            pltpu.VMEM((2, count, share, nu), jnp.float32),
+            pltpu.VMEM((2, count, share, nu), jnp.bfloat16),
+        ],
+        compiler_params=params(),
+        cost_estimate=pl.CostEstimate(
+            flops=4 * count * nocc * rows * nu, bytes_accessed=count * nu * (2 * rows + 3 * nocc), transcendentals=0
+        ),
+        name="half",
+    )(me, row_blocks, *[vmem(occ) for occ in occs], vmem(turned))
+
+
+def project_kernel(chunk, place, a_ref, b_ref, vir_ref, *refs):
+    out_ref, buf, sems = refs[-4], refs[-2], refs[-1]
+    rows, nv = a_ref.shape[0], vir_ref.shape[1]
+    z, y = place[0], place[1]
+    both = jnp.concatenate([a_ref[...], b_ref[...]], axis=0)
+    copies = []
+    for j in range(2):
+        cols = pl.ds(j * (nv // 2), nv // 2)
+        buf[:, cols] = jnp.dot(both, vir_ref[:, cols], preferred_element_type=jnp.float32).astype(jnp.bfloat16)
+        for v, to in enumerate((y, 1 - y)):
+            copies.append(
+                pltpu.make_async_copy(
+                    buf.at[pl.ds(v * rows, rows), cols], out_ref.at[z, to, chunk, :, cols], sems.at[2 * j + v]
+                )
+            )
+            copies[-1].start()
+    for copy in copies:
+        copy.wait()
+
+
+def project(out, place, chunk, own, other, vir, passing):
+    rows, nu = own.shape
+    nv = vir.shape[1]
+    first = out is None
+    ops = [place, vmem(own), vmem(other), vmem(vir)] + ([] if first else [out]) + [passing]
+    where = len(ops) - 1
+    out_type = jax.ShapeDtypeStruct((ZS, YS, CHUNKS, rows, nv), jnp.bfloat16)
+    return pl.pallas_call(
+        functools.partial(project_kernel, chunk),
+        in_specs=[IN_SMEM] + [IN_VMEM] * 3 + [IN_ANY] * (1 if first else 2),
+        out_specs=[IN_ANY] * 2,
+        scratch_shapes=[pltpu.VMEM((2 * rows, nv), jnp.bfloat16), pltpu.SemaphoreType.DMA((4,))],
+        out_shape=[out_type, jax.ShapeDtypeStruct(passing.shape, passing.dtype)],
+        input_output_aliases={where: 1} if first else {where - 1: 0, where: 1},
+        compiler_params=params(),
+        cost_estimate=pl.CostEstimate(
+            flops=4 * rows * nu * nv, bytes_accessed=4 * rows * (nu + nv) + nu * nv * 2, transcendentals=0
+        ),
+        name="project",
+    )(*ops)
+
+
+def shards_blocked(integrals, pair_mask, row_blocks, occ_coef, vir_coef):
+    mu_dev, fit_dev, nu = integrals.shape
+    nocc = occ_coef.shape[1]
+    share = nocc // 4
+    count = fit_dev // CHUNKS
+    me = lax.axis_index("basis").astype(jnp.int32).reshape(1)
+    f = lax.axis_index("fit")
+    z, y = f // YS, f % YS
+
+    occs = [occ_coef] + [lax.ppermute(occ_coef, "basis", swap) for swap in (X_SWAP, CORE_SWAP, DIAGONAL)]
+    turned = order(me, row_blocks, pair_mask, integrals)
+
+    held = []
+    for k in range(CHUNKS):
+        own, send = half_terms(me, row_blocks, occs, turned, k * count, count)
+        got = lax.ppermute(send, "basis", CORE_SWAP)
+        to_x = (own[1] + got[1].astype(jnp.float32)).astype(jnp.bfloat16)
+        from_x = lax.ppermute(to_x, "basis", X_SWAP)
+        total = own[0] + got[0].astype(jnp.float32) + from_x.astype(jnp.float32)
+        held.append(total.astype(jnp.bfloat16).reshape(count * share, nu))
+
+    out = None
+    for s in range(ZS):
+        for k in range(CHUNKS):
+            other = lax.ppermute(held[k], "fit", Y_SWAP)
+            coming = lax.ppermute(held[k], "fit", Z_RING) if s < ZS - 1 else me
+            place = jnp.stack([(z - s) % ZS, y]).astype(jnp.int32)
+            out, held[k] = project(out, place, k, held[k], other, vir_coef, coming)
+    return out.reshape(ZS * YS * fit_dev, share, vir_coef.shape[1])
 
 
 def shards(integrals, pair_mask, row_blocks, occ_coef, vir_coef):
@@ -41,6 +242,5 @@
 
 def solution(mesh):
     placed = (P("basis", "fit", None), P(), P(), P("basis", None), P(None, "fit"))
-    return jax.shard_map(
-        shards, mesh=mesh, in_specs=placed, out_specs=P(None, "basis", "fit"), check_vma=False
-    )
+    body = shards_blocked if (mesh.shape["basis"], mesh.shape["fit"]) == (4, ZS * YS) else shards
+    return jax.shard_map(body, mesh=mesh, in_specs=placed, out_specs=P(None, "basis", "fit"), check_vma=False)

time: 166 us -> 75.3 us (0.45)
  waiting for transfers between devices: 120 us -> 25.7 us
  Pallas kernels: 0 us -> 25 us
  starting transfers between devices: 0.04 us -> 21.2 us
  between operations: 13.5 us -> 0.17 us
  matrix products: 9.68 us -> 0 us
  local copies, waits for them, and re-layouts: 11.1 us -> 2.2 us
  blocking collectives: 6.48 us -> 0 us
  other arithmetic: 4.88 us -> 0.6 us
    all_gather x1 -> x0, waiting for transfers between devices: 73.5 us -> none  [shards(): lax.all_gather(half, 'fit', axis=1, tiled=True)]
    reduce_scatter x1 -> x0, waiting for transfers between devices: 46.3 us -> none  [shards(): lax.psum_scatter(lax.dot_general(occ_rows, flat, (((0,), (0,)), ((), ()))...]
    ppermute x0 -> x21, waiting for transfers between devices: none -> 25.7 us  [the longest x6 13.4 us: shards_blocked(): coming = lax.ppermute(held[k], 'fit', Z_RING) if s < ZS - 1 else me]
    pallas_call x0 -> x11, Pallas kernels: none -> 25 us  [the longest x8 18.6 us: project(): pl.pallas_call(functools.partial(project_kernel, chunk), in_specs=[IN_SME...]
    ppermute x0 -> x21, starting transfers between devices: none -> 21.2 us  [the longest x8 10.4 us: shards_blocked(): other = lax.ppermute(held[k], 'fit', Y_SWAP)]
    dot_general x2 -> x0, matrix products: 9.68 us -> none  [the longest x1 6.92 us: shards(): jnp.einsum('ipn,na->pia', lax.all_gather(half, 'fit', axis=1, tiled=True)...]
    all_gather x1 -> x0, blocking collectives: 6.48 us -> none  [shards(): panels = lax.all_gather(occ_coef, 'basis', axis=0, tiled=True)]
    convert_element_type x1 -> x0, local copies, waits for them, and re-layouts: 4.34 us -> none  [shards(): return product.astype(jnp.bfloat16)]
  transfers between devices with their start and end apart: 2 -> 21, of which waited for: 2 -> 13; matrix products, arithmetic and copies ran while one was open for 0% -> 1% of each run, Pallas kernels for 0% -> 29%
where the time goes in v2:
time: 75.3 us; the launch traced here: 74.9 us
  waiting for transfers between devices  25.7 us (34%)
  Pallas kernels  25 us (33%)
  starting transfers between devices  21.2 us (28%)
  local copies, waits for them, and re-layouts  2.2 us (3%)
    pallas_call x8, Pallas kernels, project(): pl.pallas_call(functools.partial(project_kernel, chunk), in_specs=[IN_SME...  18.6 us
    ppermute x6, waiting for transfers between devices, shards_blocked(): coming = lax.ppermute(held[k], 'fit', Z_RING) if s < ZS - 1 else me  13.4 us
    ppermute x8, starting transfers between devices, shards_blocked(): other = lax.ppermute(held[k], 'fit', Y_SWAP)  10.4 us
    ppermute x2, waiting for transfers between devices, shards_blocked(): from_x = lax.ppermute(to_x, 'basis', X_SWAP)  7.12 us
    ppermute x8, waiting for transfers between devices, shards_blocked(): other = lax.ppermute(held[k], 'fit', Y_SWAP)  4.97 us
    pallas_call x1, Pallas kernels, order(): pl.pallas_call(order_kernel, in_specs=[IN_SMEM, IN_SMEM, IN_VMEM, IN_ANY]...  4.15 us
    ppermute x6, starting transfers between devices, shards_blocked(): coming = lax.ppermute(held[k], 'fit', Z_RING) if s < ZS - 1 else me  3.66 us
    ppermute x2, starting transfers between devices, shards_blocked(): from_x = lax.ppermute(to_x, 'basis', X_SWAP)  3.3 us
  transfers between devices with their start and end apart: 21, of which 13 were waited for; matrix products, arithmetic and copies ran while one was open for 1% of the time, Pallas kernels for 29%

profile of v2, /device:TPU:0, one launch (start us, length us, event | category | flops | bytes accessed | tf_op | source)
XLA Modules:
  0.0 74.9 jit_solution(1305609479966785454)
XLA Ops:
  0.8 3.0 %collective-permute-start = (bf16[128,64]{1,0:T(8,128)(2,1)S(1)}, bf16[128,64]{1,0:T(8,128)(2,1)S(1)}, u32[]{:S(2)}, u32[]{:S(2)}) collective-permute-start(bf16[128,64]{1,0:T(8,128)(2,1)S(1)} %copy.24.own_occ), channel_id=1, source_target_pairs={{0,16},{16,0},{8,24},{24,8},{1,17},{17,1},{9,25},{25,9},{2,18},{18... | collective-permute-start | bytes 49160 | tf_op jit(solution)/shard_map/ppermute | solution.py:188
  5.4 4.1 %order.1.x_ref = bf16[16,128,1024]{2,1,0:T(8,128)(2,1)S(1)} custom-call(s32[1]{0:T(128)} %bitcast.5.me.me_ref.refs_1_, s32[32]{0:T(128)S(1)} %copy-done.2, s32[32,64]{1,0:T(8,128)S(1)} %copy-done.1, bf16[2048,1024]{1,0:T(8,128)(2,1)} %bitcast.28), custom_call_target="tpu_custom_call" | custom-call | flops 1073741824 | bytes 8388608 | tf_op jit(solution)/shard_map/order/pallas_call | solution.py:68
  9.6 1.2 %half.3 = (f32[2,8,16,1024]{3,2,1,0:T(8,128)S(1)}, bf16[2,8,16,1024]{3,2,1,0:T(8,128)(2,1)S(1)}) custom-call(s32[1]{0:T(128)} %bitcast.5.me.me_ref.refs_1_, s32[32]{0:T(128)S(1)} %copy-done.2, bf16[128,64]{1,0:T(8,128)(2,1)S(1)} %copy.24.own_occ, bf16[128,64]{1,0:T(8,128)(2,1)S(1)} %collective-permute-done.far_occ, ...), custom_call_target="tpu_custom_call" | custom-call | flops 268435456 | bytes 3670016 | tf_op jit(solution)/shard_map/half/pallas_call | solution.py:120
  11.1 1.1 %half.2 = (f32[2,8,16,1024]{3,2,1,0:T(8,128)S(1)}, bf16[2,8,16,1024]{3,2,1,0:T(8,128)(2,1)S(1)}) custom-call(s32[1]{0:T(128)} %bitcast.5.me.me_ref.refs_1_, s32[32]{0:T(128)S(1)} %copy-done.2, bf16[128,64]{1,0:T(8,128)(2,1)S(1)} %copy.24.own_occ, bf16[128,64]{1,0:T(8,128)(2,1)S(1)} %collective-permute-done.far_occ, ...), custom_call_target="tpu_custom_call" | custom-call | flops 268435456 | bytes 3670016 | tf_op jit(solution)/shard_map/half/pallas_call | solution.py:120
  12.8 2.0 %collective-permute-start.7 = (bf16[8,16,1024]{2,1,0:T(8,128)(2,1)S(1)}, bf16[8,16,1024]{2,1,0:T(8,128)(2,1)S(1)}, u32[]{:S(2)}, u32[]{:S(2)}) collective-permute-start(bf16[8,16,1024]{2,1,0:T(8,128)(2,1)S(1)} %fusion.3), channel_id=1, source_target_pairs={{0,16},{16,0},{8,24},{24,8},{1,17},{17,1},{9,25},{25,9},{2,18},{18... | collective-permute-start | bytes 786440 | tf_op jit(solution)/shard_map/ppermute | solution.py:196
  14.9 1.3 %collective-permute-start.4 = (bf16[8,16,1024]{2,1,0:T(8,128)(2,1)S(1)}, bf16[8,16,1024]{2,1,0:T(8,128)(2,1)S(1)}, u32[]{:S(2)}, u32[]{:S(2)}) collective-permute-start(bf16[8,16,1024]{2,1,0:T(8,128)(2,1)S(1)} %fusion.2), channel_id=1, source_target_pairs={{0,16},{16,0},{8,24},{24,8},{1,17},{17,1},{9,25},{25,9},{2,18},{18... | collective-permute-start | bytes 786440 | tf_op jit(solution)/shard_map/ppermute | solution.py:196
  16.2 5.8 %collective-permute-done.7 = bf16[8,16,1024]{2,1,0:T(8,128)(2,1)S(1)} collective-permute-done((bf16[8,16,1024]{2,1,0:T(8,128)(2,1)S(1)}, bf16[8,16,1024]{2,1,0:T(8,128)(2,1)S(1)}, u32[]{:S(2)}, u32[]{:S(2)}) %collective-permute-start.7) | collective-permute-done | bytes 262176 | tf_op jit(solution)/shard_map/ppermute | solution.py:196
  22.1 2.1 %collective-permute-start.8 = (bf16[128,1024]{1,0:T(8,128)(2,1)S(1)}, bf16[128,1024]{1,0:T(8,128)(2,1)}, u32[]{:S(2)}, u32[]{:S(2)}) collective-permute-start(bf16[128,1024]{1,0:T(8,128)(2,1)S(1)} %bitcast.25), channel_id=1, source_target_pairs={{0,1},{1,0},{2,3},{3,2},{4,5},{5,4},{6,7},{7,6},{8,9},{9,8},{10,11... | collective-permute-start | bytes 786440 | tf_op jit(solution)/shard_map/ppermute | solution.py:203
  24.2 1.6 %collective-permute-start.9 = (bf16[128,1024]{1,0:T(8,128)(2,1)S(1)}, bf16[128,1024]{1,0:T(8,128)(2,1)S(1)}, u32[]{:S(2)}, u32[]{:S(2)}) collective-permute-start(bf16[128,1024]{1,0:T(8,128)(2,1)S(1)} %bitcast.26), channel_id=1, source_target_pairs={{0,2},{1,3},{2,4},{3,5},{4,6},{5,7},{6,0},{7,1},{8,10},{9,11},{10,... | collective-permute-start | bytes 786440 | tf_op jit(solution)/shard_map/ppermute | solution.py:204
  25.7 1.3 %collective-permute-done.4 = bf16[8,16,1024]{2,1,0:T(8,128)(2,1)S(1)} collective-permute-done((bf16[8,16,1024]{2,1,0:T(8,128)(2,1)S(1)}, bf16[8,16,1024]{2,1,0:T(8,128)(2,1)S(1)}, u32[]{:S(2)}, u32[]{:S(2)}) %collective-permute-start.4) | collective-permute-done | bytes 262176 | tf_op jit(solution)/shard_map/ppermute | solution.py:196
  27.1 1.8 %collective-permute-start.5 = (bf16[128,1024]{1,0:T(8,128)(2,1)S(1)}, bf16[128,1024]{1,0:T(8,128)(2,1)S(1)}, u32[]{:S(2)}, u32[]{:S(2)}) collective-permute-start(bf16[128,1024]{1,0:T(8,128)(2,1)S(1)} %bitcast.22), channel_id=1, source_target_pairs={{0,1},{1,0},{2,3},{3,2},{4,5},{5,4},{6,7},{7,6},{8,9},{9,8},{10,11... | collective-permute-start | bytes 786440 | tf_op jit(solution)/shard_map/ppermute | solution.py:203
  29.0 1.6 %collective-permute-start.10 = (bf16[128,1024]{1,0:T(8,128)(2,1)S(1)}, bf16[128,1024]{1,0:T(8,128)(2,1)S(1)}, u32[]{:S(2)}, u32[]{:S(2)}) collective-permute-start(bf16[128,1024]{1,0:T(8,128)(2,1)S(1)} %bitcast.23), channel_id=1, source_target_pairs={{0,2},{1,3},{2,4},{3,5},{4,6},{5,7},{6,0},{7,1},{8,10},{9,11},{10,... | collective-permute-start | bytes 786440 | tf_op jit(solution)/shard_map/ppermute | solution.py:204
  30.6 1.8 %collective-permute-done.9.refs_0_ = bf16[128,1024]{1,0:T(8,128)(2,1)S(1)} collective-permute-done((bf16[128,1024]{1,0:T(8,128)(2,1)S(1)}, bf16[128,1024]{1,0:T(8,128)(2,1)S(1)}, u32[]{:S(2)}, u32[]{:S(2)}) %collective-permute-start.9) | collective-permute-done | bytes 262176 | tf_op jit(solution)/shard_map/ppermute | solution.py:204
  32.4 2.4 %project.8 = (bf16[4,2,2,128,1024]{4,3,2,1,0:T(8,128)(2,1)}, bf16[128,1024]{1,0:T(8,128)(2,1)S(1)}) custom-call(s32[2]{0:T(128)S(1)} %pad_add_fusion.3.place, bf16[128,1024]{1,0:T(8,128)(2,1)S(1)} %bitcast.27, bf16[128,1024]{1,0:T(8,128)(2,1)} %collective-permute-done.8.b_ref, bf16[1024,1024]{1,0:T(8,128)(2,1)S(1)} %copy-done, ...), custom_call_target="tpu_custom_call", output_to_operand_aliasing={{1}: (4, {})} | custom-call | flops 536870912 | bytes 3145728 | tf_op jit(solution)/shard_map/project/pallas_call | solution.py:164
  35.4 3.7 %collective-permute-done.10.refs_1_ = bf16[128,1024]{1,0:T(8,128)(2,1)S(1)} collective-permute-done((bf16[128,1024]{1,0:T(8,128)(2,1)S(1)}, bf16[128,1024]{1,0:T(8,128)(2,1)S(1)}, u32[]{:S(2)}, u32[]{:S(2)}) %collective-permute-start.10) | collective-permute-done | bytes 262176 | tf_op jit(solution)/shard_map/ppermute | solution.py:204
  39.1 2.0 %project.9 = (bf16[4,2,2,128,1024]{4,3,2,1,0:T(8,128)(2,1)}, bf16[128,1024]{1,0:T(8,128)(2,1)S(1)}) custom-call(s32[2]{0:T(128)S(1)} %pad_add_fusion.3.place, bf16[128,1024]{1,0:T(8,128)(2,1)S(1)} %bitcast.24, bf16[128,1024]{1,0:T(8,128)(2,1)S(1)} %collective-permute-done.5.b_ref, ...), custom_call_target="tpu_custom_call", output_to_operand_aliasing={{0}: (4, {}), {1}: (5, {})} | custom-call | flops 536870912 | bytes 3145728 | tf_op jit(solution)/shard_map/project/pallas_call | solution.py:164
  41.8 2.4 %collective-permute-done.13.refs_1_ = bf16[128,1024]{1,0:T(8,128)(2,1)S(1)} collective-permute-done((bf16[128,1024]{1,0:T(8,128)(2,1)S(1)}, bf16[128,1024]{1,0:T(8,128)(2,1)S(1)}, u32[]{:S(2)}, u32[]{:S(2)}) %collective-permute-start.13) | collective-permute-done | bytes 262176 | tf_op jit(solution)/shard_map/ppermute | solution.py:204
  44.2 2.4 %project.10 = (bf16[4,2,2,128,1024]{4,3,2,1,0:T(8,128)(2,1)}, bf16[128,1024]{1,0:T(8,128)(2,1)S(1)}) custom-call(s32[2]{0:T(128)S(1)} %pad_add_fusion.2.place, bf16[128,1024]{1,0:T(8,128)(2,1)S(1)} %get-tuple-element.29.a_ref, bf16[128,1024]{1,0:T(8,128)(2,1)} %collective-permute-done.12.b_ref, ...), custom_call_target="tpu_custom_call", output_to_operand_aliasing={{0}: (4, {}), {1}: (5, {})} | custom-call | flops 536870912 | bytes 3145728 | tf_op jit(solution)/shard_map/project/pallas_call | solution.py:164
  46.6 1.4 %collective-permute-start.16 = (bf16[128,1024]{1,0:T(8,128)(2,1)S(1)}, bf16[128,1024]{1,0:T(8,128)(2,1)S(1)}, u32[]{:S(2)}, u32[]{:S(2)}) collective-permute-start(bf16[128,1024]{1,0:T(8,128)(2,1)S(1)} %get-tuple-element.33.a_ref), channel_id=1, source_target_pairs={{0,1},{1,0},{2,3},{3,2},{4,5},{5,4},{6,7},{7,6},{8,9},{9,8},{10,11... | collective-permute-start | bytes 786440 | tf_op jit(solution)/shard_map/ppermute | solution.py:203
  48.9 1.8 %collective-permute-done.14.refs_1_ = bf16[128,1024]{1,0:T(8,128)(2,1)S(1)} collective-permute-done((bf16[128,1024]{1,0:T(8,128)(2,1)S(1)}, bf16[128,1024]{1,0:T(8,128)(2,1)S(1)}, u32[]{:S(2)}, u32[]{:S(2)}) %collective-permute-start.14) | collective-permute-done | bytes 262176 | tf_op jit(solution)/shard_map/ppermute | solution.py:204
  50.6 2.4 %project.11 = (bf16[4,2,2,128,1024]{4,3,2,1,0:T(8,128)(2,1)}, bf16[128,1024]{1,0:T(8,128)(2,1)S(1)}) custom-call(s32[2]{0:T(128)S(1)} %pad_add_fusion.2.place, bf16[128,1024]{1,0:T(8,128)(2,1)S(1)} %get-tuple-element.28.a_ref, bf16[128,1024]{1,0:T(8,128)(2,1)} %collective-permute-done.11.b_ref, ...), custom_call_target="tpu_custom_call", output_to_operand_aliasing={{0}: (4, {}), {1}: (5, {})} | custom-call | flops 536870912 | bytes 3145728 | tf_op jit(solution)/shard_map/project/pallas_call | solution.py:164
  53.0 2.3 %collective-permute-start.15 = (bf16[128,1024]{1,0:T(8,128)(2,1)S(1)}, bf16[128,1024]{1,0:T(8,128)(2,1)}, u32[]{:S(2)}, u32[]{:S(2)}) collective-permute-start(bf16[128,1024]{1,0:T(8,128)(2,1)S(1)} %get-tuple-element.32.a_ref), channel_id=1, source_target_pairs={{0,1},{1,0},{2,3},{3,2},{4,5},{5,4},{6,7},{7,6},{8,9},{9,8},{10,11... | collective-permute-start | bytes 786440 | tf_op jit(solution)/shard_map/ppermute | solution.py:203
  55.5 2.6 %collective-permute-done.17.refs_1_ = bf16[128,1024]{1,0:T(8,128)(2,1)S(1)} collective-permute-done((bf16[128,1024]{1,0:T(8,128)(2,1)S(1)}, bf16[128,1024]{1,0:T(8,128)(2,1)S(1)}, u32[]{:S(2)}, u32[]{:S(2)}) %collective-permute-start.17) | collective-permute-done | bytes 262176 | tf_op jit(solution)/shard_map/ppermute | solution.py:204
  58.0 2.0 %project.12 = (bf16[4,2,2,128,1024]{4,3,2,1,0:T(8,128)(2,1)}, bf16[128,1024]{1,0:T(8,128)(2,1)S(1)}) custom-call(s32[2]{0:T(128)S(1)} %pad_add_fusion.1.place, bf16[128,1024]{1,0:T(8,128)(2,1)S(1)} %get-tuple-element.33.a_ref, bf16[128,1024]{1,0:T(8,128)(2,1)S(1)} %collective-permute-done.16.b_ref, ...), custom_call_target="tpu_custom_call", output_to_operand_aliasing={{0}: (4, {}), {1}: (5, {})} | custom-call | flops 536870912 | bytes 3145728 | tf_op jit(solution)/shard_map/project/pallas_call | solution.py:164
  60.0 1.0 %collective-permute-start.20 = (bf16[128,1024]{1,0:T(8,128)(2,1)S(1)}, bf16[128,1024]{1,0:T(8,128)(2,1)S(1)}, u32[]{:S(2)}, u32[]{:S(2)}) collective-permute-start(bf16[128,1024]{1,0:T(8,128)(2,1)S(1)} %get-tuple-element.37.a_ref), channel_id=1, source_target_pairs={{0,1},{1,0},{2,3},{3,2},{4,5},{5,4},{6,7},{7,6},{8,9},{9,8},{10,11... | collective-permute-start | bytes 786440 | tf_op jit(solution)/shard_map/ppermute | solution.py:203
  61.0 1.3 %collective-permute-done.15.b_ref = bf16[128,1024]{1,0:T(8,128)(2,1)} collective-permute-done((bf16[128,1024]{1,0:T(8,128)(2,1)S(1)}, bf16[128,1024]{1,0:T(8,128)(2,1)}, u32[]{:S(2)}, u32[]{:S(2)}) %collective-permute-start.15) | collective-permute-done | bytes 262176 | tf_op jit(solution)/shard_map/ppermute | solution.py:203
  62.4 1.2 %collective-permute-done.18.refs_1_ = bf16[128,1024]{1,0:T(8,128)(2,1)S(1)} collective-permute-done((bf16[128,1024]{1,0:T(8,128)(2,1)S(1)}, bf16[128,1024]{1,0:T(8,128)(2,1)S(1)}, u32[]{:S(2)}, u32[]{:S(2)}) %collective-permute-start.18) | collective-permute-done | bytes 262176 | tf_op jit(solution)/shard_map/ppermute | solution.py:204
  63.6 2.4 %project.13 = (bf16[4,2,2,128,1024]{4,3,2,1,0:T(8,128)(2,1)}, bf16[128,1024]{1,0:T(8,128)(2,1)S(1)}) custom-call(s32[2]{0:T(128)S(1)} %pad_add_fusion.1.place, bf16[128,1024]{1,0:T(8,128)(2,1)S(1)} %get-tuple-element.32.a_ref, bf16[128,1024]{1,0:T(8,128)(2,1)} %collective-permute-done.15.b_ref, ...), custom_call_target="tpu_custom_call", output_to_operand_aliasing={{0}: (4, {}), {1}: (5, {})} | custom-call | flops 536870912 | bytes 3145728 | tf_op jit(solution)/shard_map/project/pallas_call | solution.py:164
  66.0 1.1 %collective-permute-start.19 = (bf16[128,1024]{1,0:T(8,128)(2,1)S(1)}, bf16[128,1024]{1,0:T(8,128)(2,1)S(1)}, u32[]{:S(2)}, u32[]{:S(2)}) collective-permute-start(bf16[128,1024]{1,0:T(8,128)(2,1)S(1)} %get-tuple-element.36.a_ref), channel_id=1, source_target_pairs={{0,1},{1,0},{2,3},{3,2},{4,5},{5,4},{6,7},{7,6},{8,9},{9,8},{10,11... | collective-permute-start | bytes 786440 | tf_op jit(solution)/shard_map/ppermute | solution.py:203
  67.1 1.9 %collective-permute-done.20.b_ref = bf16[128,1024]{1,0:T(8,128)(2,1)S(1)} collective-permute-done((bf16[128,1024]{1,0:T(8,128)(2,1)S(1)}, bf16[128,1024]{1,0:T(8,128)(2,1)S(1)}, u32[]{:S(2)}, u32[]{:S(2)}) %collective-permute-start.20) | collective-permute-done | bytes 262176 | tf_op jit(solution)/shard_map/ppermute | solution.py:203
  69.1 2.5 %project.14 = (bf16[4,2,2,128,1024]{4,3,2,1,0:T(8,128)(2,1)}, s32[1]{0:T(128)}) custom-call(s32[2]{0:T(128)S(1)} %pad_add_fusion.place, bf16[128,1024]{1,0:T(8,128)(2,1)S(1)} %get-tuple-element.37.a_ref, bf16[128,1024]{1,0:T(8,128)(2,1)S(1)} %collective-permute-done.20.b_ref, ...), custom_call_target="tpu_custom_call", output_to_operand_aliasing={{0}: (4, {}), {1}: (5, {})} | custom-call | flops 536870912 | bytes 3145728 | tf_op jit(solution)/shard_map/project/pallas_call | solution.py:164
  72.4 2.5 %project.15 = (bf16[4,2,2,128,1024]{4,3,2,1,0:T(8,128)(2,1)}, s32[1]{0:T(128)}) custom-call(s32[2]{0:T(128)S(1)} %pad_add_fusion.place, bf16[128,1024]{1,0:T(8,128)(2,1)S(1)} %get-tuple-element.36.a_ref, bf16[128,1024]{1,0:T(8,128)(2,1)S(1)} %collective-permute-done.19.b_ref, ...), custom_call_target="tpu_custom_call", output_to_operand_aliasing={{0}: (4, {}), {1}: (5, {})} | custom-call | flops 536870912 | bytes 3145728 | tf_op jit(solution)/shard_map/project/pallas_call | solution.py:164
  (36 shorter events, 6.7 us)
Async XLA Ops:
  0.8 8.7 %collective-permute-start = (bf16[128,64]{1,0:T(8,128)(2,1)S(1)}, bf16[128,64]{1,0:T(8,128)(2,1)S(1)}, u32[]{:S(2)}, u32[]{:S(2)}) collective-permute-start(bf16[128,64]{1,0:T(8,128)(2,1)S(1)} %copy.24.own_occ), channel_id=1, source_target_pairs={{0,16},{16,0},{8,24},{24,8},{1,17},{17,1},{9,25},{25,9},{2,18},{18... | collective-permute-start | bytes 49160 | tf_op jit(solution)/shard_map/ppermute | solution.py:188
  3.8 5.7 %collective-permute-start.1 = (bf16[128,64]{1,0:T(8,128)(2,1)S(1)}, bf16[128,64]{1,0:T(8,128)(2,1)S(1)}, u32[]{:S(2)}, u32[]{:S(2)}) collective-permute-start(bf16[128,64]{1,0:T(8,128)(2,1)S(1)} %copy.24.own_occ), channel_id=1, source_target_pairs={{0,8},{8,0},{16,24},{24,16},{1,9},{9,1},{17,25},{25,17},{2,10},{10... | collective-permute-start | bytes 49160 | tf_op jit(solution)/shard_map/ppermute | solution.py:188
  3.8 5.8 %collective-permute-start.2 = (bf16[128,64]{1,0:T(8,128)(2,1)S(1)}, bf16[128,64]{1,0:T(8,128)(2,1)S(1)}, u32[]{:S(2)}, u32[]{:S(2)}) collective-permute-start(bf16[128,64]{1,0:T(8,128)(2,1)S(1)} %copy.24.own_occ), channel_id=1, source_target_pairs={{0,24},{24,0},{8,16},{16,8},{1,25},{25,1},{9,17},{17,9},{2,26},{26... | collective-permute-start | bytes 49160 | tf_op jit(solution)/shard_map/ppermute | solution.py:188
  4.0 0.7 copy-start.1
  4.8 0.7 copy-start.2
  10.8 21.7 %copy-start = (bf16[1024,1024]{1,0:T(8,128)(2,1)S(1)}, bf16[1024,1024]{1,0:T(8,128)(2,1)}, u32[]{:S(2)}) copy-start(bf16[1024,1024]{1,0:T(8,128)(2,1)} %vir_ref.15) | copy-start | bytes 6291460
  10.8 2.0 %collective-permute-start.6 = (bf16[2,8,16,1024]{3,2,1,0:T(8,128)(2,1)S(1)}, bf16[2,8,16,1024]{3,2,1,0:T(8,128)(2,1)S(1)}, u32[]{:S(2)}, u32[]{:S(2)}) collective-permute-start(bf16[2,8,16,1024]{3,2,1,0:T(8,128)(2,1)S(1)} %get-tuple-element.26), channel_id=1, source_target_pairs={{0,8},{8,0},{16,24},{24,16},{1,9},{9,1},{17,25},{25,17},{2,10},{10... | collective-permute-start | bytes 1572872 | tf_op jit(solution)/shard_map/ppermute | solution.py:194
  12.3 2.5 %collective-permute-start.3 = (bf16[2,8,16,1024]{3,2,1,0:T(8,128)(2,1)S(1)}, bf16[2,8,16,1024]{3,2,1,0:T(8,128)(2,1)S(1)}, u32[]{:S(2)}, u32[]{:S(2)}) collective-permute-start(bf16[2,8,16,1024]{3,2,1,0:T(8,128)(2,1)S(1)} %get-tuple-element.24), channel_id=1, source_target_pairs={{0,8},{8,0},{16,24},{24,16},{1,9},{9,1},{17,25},{25,17},{2,10},{10... | collective-permute-start | bytes 1572872 | tf_op jit(solution)/shard_map/ppermute | solution.py:194
  12.8 9.2 %collective-permute-start.7 = (bf16[8,16,1024]{2,1,0:T(8,128)(2,1)S(1)}, bf16[8,16,1024]{2,1,0:T(8,128)(2,1)S(1)}, u32[]{:S(2)}, u32[]{:S(2)}) collective-permute-start(bf16[8,16,1024]{2,1,0:T(8,128)(2,1)S(1)} %fusion.3), channel_id=1, source_target_pairs={{0,16},{16,0},{8,24},{24,8},{1,17},{17,1},{9,25},{25,9},{2,18},{18... | collective-permute-start | bytes 786440 | tf_op jit(solution)/shard_map/ppermute | solution.py:196
  14.9 12.2 %collective-permute-start.4 = (bf16[8,16,1024]{2,1,0:T(8,128)(2,1)S(1)}, bf16[8,16,1024]{2,1,0:T(8,128)(2,1)S(1)}, u32[]{:S(2)}, u32[]{:S(2)}) collective-permute-start(bf16[8,16,1024]{2,1,0:T(8,128)(2,1)S(1)} %fusion.2), channel_id=1, source_target_pairs={{0,16},{16,0},{8,24},{24,8},{1,17},{17,1},{9,25},{25,9},{2,18},{18... | collective-permute-start | bytes 786440 | tf_op jit(solution)/shard_map/ppermute | solution.py:196
  22.1 8.5 %collective-permute-start.8 = (bf16[128,1024]{1,0:T(8,128)(2,1)S(1)}, bf16[128,1024]{1,0:T(8,128)(2,1)}, u32[]{:S(2)}, u32[]{:S(2)}) collective-permute-start(bf16[128,1024]{1,0:T(8,128)(2,1)S(1)} %bitcast.25), channel_id=1, source_target_pairs={{0,1},{1,0},{2,3},{3,2},{4,5},{5,4},{6,7},{7,6},{8,9},{9,8},{10,11... | collective-permute-start | bytes 786440 | tf_op jit(solution)/shard_map/ppermute | solution.py:203
  24.2 8.3 %collective-permute-start.9 = (bf16[128,1024]{1,0:T(8,128)(2,1)S(1)}, bf16[128,1024]{1,0:T(8,128)(2,1)S(1)}, u32[]{:S(2)}, u32[]{:S(2)}) collective-permute-start(bf16[128,1024]{1,0:T(8,128)(2,1)S(1)} %bitcast.26), channel_id=1, source_target_pairs={{0,2},{1,3},{2,4},{3,5},{4,6},{5,7},{6,0},{7,1},{8,10},{9,11},{10,... | collective-permute-start | bytes 786440 | tf_op jit(solution)/shard_map/ppermute | solution.py:204
  27.1 8.3 %collective-permute-start.5 = (bf16[128,1024]{1,0:T(8,128)(2,1)S(1)}, bf16[128,1024]{1,0:T(8,128)(2,1)S(1)}, u32[]{:S(2)}, u32[]{:S(2)}) collective-permute-start(bf16[128,1024]{1,0:T(8,128)(2,1)S(1)} %bitcast.22), channel_id=1, source_target_pairs={{0,1},{1,0},{2,3},{3,2},{4,5},{5,4},{6,7},{7,6},{8,9},{9,8},{10,11... | collective-permute-start | bytes 786440 | tf_op jit(solution)/shard_map/ppermute | solution.py:203
  29.0 10.2 %collective-permute-start.10 = (bf16[128,1024]{1,0:T(8,128)(2,1)S(1)}, bf16[128,1024]{1,0:T(8,128)(2,1)S(1)}, u32[]{:S(2)}, u32[]{:S(2)}) collective-permute-start(bf16[128,1024]{1,0:T(8,128)(2,1)S(1)} %bitcast.23), channel_id=1, source_target_pairs={{0,2},{1,3},{2,4},{3,5},{4,6},{5,7},{6,0},{7,1},{8,10},{9,11},{10,... | collective-permute-start | bytes 786440 | tf_op jit(solution)/shard_map/ppermute | solution.py:204
  34.9 6.9 %collective-permute-start.12 = (bf16[128,1024]{1,0:T(8,128)(2,1)S(1)}, bf16[128,1024]{1,0:T(8,128)(2,1)}, u32[]{:S(2)}, u32[]{:S(2)}) collective-permute-start(bf16[128,1024]{1,0:T(8,128)(2,1)S(1)} %get-tuple-element.29.a_ref), channel_id=1, source_target_pairs={{0,1},{1,0},{2,3},{3,2},{4,5},{5,4},{6,7},{7,6},{8,9},{9,8},{10,11... | collective-permute-start | bytes 786440 | tf_op jit(solution)/shard_map/ppermute | solution.py:203
  35.4 8.7 %collective-permute-start.13 = (bf16[128,1024]{1,0:T(8,128)(2,1)S(1)}, bf16[128,1024]{1,0:T(8,128)(2,1)S(1)}, u32[]{:S(2)}, u32[]{:S(2)}) collective-permute-start(bf16[128,1024]{1,0:T(8,128)(2,1)S(1)} %get-tuple-element.29.a_ref), channel_id=1, source_target_pairs={{0,2},{1,3},{2,4},{3,5},{4,6},{5,7},{6,0},{7,1},{8,10},{9,11},{10,... | collective-permute-start | bytes 786440 | tf_op jit(solution)/shard_map/ppermute | solution.py:204
  41.1 7.8 %collective-permute-start.11 = (bf16[128,1024]{1,0:T(8,128)(2,1)S(1)}, bf16[128,1024]{1,0:T(8,128)(2,1)}, u32[]{:S(2)}, u32[]{:S(2)}) collective-permute-start(bf16[128,1024]{1,0:T(8,128)(2,1)S(1)} %get-tuple-element.28.a_ref), channel_id=1, source_target_pairs={{0,1},{1,0},{2,3},{3,2},{4,5},{5,4},{6,7},{7,6},{8,9},{9,8},{10,11... | collective-permute-start | bytes 786440 | tf_op jit(solution)/shard_map/ppermute | solution.py:203
  41.2 9.4 %collective-permute-start.14 = (bf16[128,1024]{1,0:T(8,128)(2,1)S(1)}, bf16[128,1024]{1,0:T(8,128)(2,1)S(1)}, u32[]{:S(2)}, u32[]{:S(2)}) collective-permute-start(bf16[128,1024]{1,0:T(8,128)(2,1)S(1)} %get-tuple-element.28.a_ref), channel_id=1, source_target_pairs={{0,2},{1,3},{2,4},{3,5},{4,6},{5,7},{6,0},{7,1},{8,10},{9,11},{10,... | collective-permute-start | bytes 786440 | tf_op jit(solution)/shard_map/ppermute | solution.py:204
  46.6 8.9 %collective-permute-start.16 = (bf16[128,1024]{1,0:T(8,128)(2,1)S(1)}, bf16[128,1024]{1,0:T(8,128)(2,1)S(1)}, u32[]{:S(2)}, u32[]{:S(2)}) collective-permute-start(bf16[128,1024]{1,0:T(8,128)(2,1)S(1)} %get-tuple-element.33.a_ref), channel_id=1, source_target_pairs={{0,1},{1,0},{2,3},{3,2},{4,5},{5,4},{6,7},{7,6},{8,9},{9,8},{10,11... | collective-permute-start | bytes 786440 | tf_op jit(solution)/shard_map/ppermute | solution.py:203
  48.0 10.0 %collective-permute-start.17 = (bf16[128,1024]{1,0:T(8,128)(2,1)S(1)}, bf16[128,1024]{1,0:T(8,128)(2,1)S(1)}, u32[]{:S(2)}, u32[]{:S(2)}) collective-permute-start(bf16[128,1024]{1,0:T(8,128)(2,1)S(1)} %get-tuple-element.33.a_ref), channel_id=1, source_target_pairs={{0,2},{1,3},{2,4},{3,5},{4,6},{5,7},{6,0},{7,1},{8,10},{9,11},{10,... | collective-permute-start | bytes 786440 | tf_op jit(solution)/shard_map/ppermute | solution.py:204
  53.0 9.3 %collective-permute-start.15 = (bf16[128,1024]{1,0:T(8,128)(2,1)S(1)}, bf16[128,1024]{1,0:T(8,128)(2,1)}, u32[]{:S(2)}, u32[]{:S(2)}) collective-permute-start(bf16[128,1024]{1,0:T(8,128)(2,1)S(1)} %get-tuple-element.32.a_ref), channel_id=1, source_target_pairs={{0,1},{1,0},{2,3},{3,2},{4,5},{5,4},{6,7},{7,6},{8,9},{9,8},{10,11... | collective-permute-start | bytes 786440 | tf_op jit(solution)/shard_map/ppermute | solution.py:203
  55.4 8.2 %collective-permute-start.18 = (bf16[128,1024]{1,0:T(8,128)(2,1)S(1)}, bf16[128,1024]{1,0:T(8,128)(2,1)S(1)}, u32[]{:S(2)}, u32[]{:S(2)}) collective-permute-start(bf16[128,1024]{1,0:T(8,128)(2,1)S(1)} %get-tuple-element.32.a_ref), channel_id=1, source_target_pairs={{0,2},{1,3},{2,4},{3,5},{4,6},{5,7},{6,0},{7,1},{8,10},{9,11},{10,... | collective-permute-start | bytes 786440 | tf_op jit(solution)/shard_map/ppermute | solution.py:204
  60.0 9.0 %collective-permute-start.20 = (bf16[128,1024]{1,0:T(8,128)(2,1)S(1)}, bf16[128,1024]{1,0:T(8,128)(2,1)S(1)}, u32[]{:S(2)}, u32[]{:S(2)}) collective-permute-start(bf16[128,1024]{1,0:T(8,128)(2,1)S(1)} %get-tuple-element.37.a_ref), channel_id=1, source_target_pairs={{0,1},{1,0},{2,3},{3,2},{4,5},{5,4},{6,7},{7,6},{8,9},{9,8},{10,11... | collective-permute-start | bytes 786440 | tf_op jit(solution)/shard_map/ppermute | solution.py:203
  66.0 6.4 %collective-permute-start.19 = (bf16[128,1024]{1,0:T(8,128)(2,1)S(1)}, bf16[128,1024]{1,0:T(8,128)(2,1)S(1)}, u32[]{:S(2)}, u32[]{:S(2)}) collective-permute-start(bf16[128,1024]{1,0:T(8,128)(2,1)S(1)} %get-tuple-element.36.a_ref), channel_id=1, source_target_pairs={{0,1},{1,0},{2,3},{3,2},{4,5},{5,4},{6,7},{7,6},{8,9},{9,8},{10,11... | collective-permute-start | bytes 786440 | tf_op jit(solution)/shard_map/ppermute | solution.py:203

commit v3 on v0

--- a/solution.py
+++ b/solution.py
@@ -1,9 +1,333 @@
+import functools
+
 import jax
 import jax.numpy as jnp
 from jax import lax
+from jax.experimental import pallas as pl
+from jax.experimental.pallas import tpu as pltpu
 from jax.sharding import PartitionSpec as P
 
 BLK = 16
+GROUPS = 2
+PARTS = (8, 8)
+ZS, YS = 4, 2
+PROJ_FLOPS = 1000
+PROJ_BYTES = 1000
+
+CORE_SWAP = [(0, 1), (1, 0), (2, 3), (3, 2)]
+X_SWAP = [(0, 2), (2, 0), (1, 3), (3, 1)]
+DIAGONAL = [(0, 3), (3, 0), (1, 2), (2, 1)]
+Y_SWAP = [(f, f ^ 1) for f in range(ZS * YS)]
+Z_RING = [(f, (f + YS) % (ZS * YS)) for f in range(ZS * YS)]
+Z_BACK = [(to, f) for f, to in Z_RING]
+
+IN_ANY = pl.BlockSpec(memory_space=pl.ANY)
+IN_VMEM = pl.BlockSpec(memory_space=pltpu.VMEM)
+IN_SMEM = pl.BlockSpec(memory_space=pltpu.SMEM)
+
+
+def params():
+    return pltpu.CompilerParams(vmem_limit_bytes=16 * 2**20)
+
+
+def vmem(value):
+    return pltpu.with_memory_space_constraint(value, pltpu.VMEM)
+
+
+def hbm(value):
+    return pltpu.with_memory_space_constraint(value, pltpu.HBM)
+
+
+def turn_blocks(x_ref, out_ref, first_p, blocks):
+    count, mu_dev, nu = out_ref.shape
+    depth = x_ref.shape[0] // (mu_dev // BLK)
+    fit_dev = depth // BLK
+    to = lax.broadcasted_iota(jnp.int32, (count * BLK, depth), 0)
+    at = lax.broadcasted_iota(jnp.int32, (count * BLK, depth), 1)
+    same = (to // BLK + first_p == at % fit_dev) & (to % BLK == at // fit_dev)
+    turn = jnp.where(same, 1.0, 0.0).astype(jnp.bfloat16)
+    for b in blocks:
+        block = x_ref[b * depth : (b + 1) * depth, :]
+        turned = jnp.dot(turn, block, preferred_element_type=jnp.float32).astype(jnp.bfloat16)
+        out_ref[:, b * BLK : (b + 1) * BLK, :] = turned.reshape(count, BLK, nu)
+
+
+def first_kernel(me, row_blocks_hbm, mask_hbm, flat_hbm, vir_hbm, out_ref, row_blocks, vir_ref, x_ref, mask_ref, sems):
+    rows, nu = x_ref.shape
+    nblk = out_ref.shape[1] // BLK
+    depth = rows // nblk
+    nnb = mask_ref.shape[1]
+    small = [
+        pltpu.make_async_copy(row_blocks_hbm, row_blocks, sems.at[GROUPS]),
+        pltpu.make_async_copy(mask_hbm, mask_ref, sems.at[GROUPS + 1]),
+    ]
+    part = rows // GROUPS
+    copies = [
+        pltpu.make_async_copy(flat_hbm.at[pl.ds(g * part, part)], x_ref.at[pl.ds(g * part, part)], sems.at[g])
+        for g in range(GROUPS)
+    ]
+    vir_copy = pltpu.make_async_copy(vir_hbm, vir_ref, sems.at[GROUPS + 2])
+    for copy in (*small, *copies, vir_copy):
+        copy.start()
+    column = lax.broadcasted_iota(jnp.int32, (nnb, nu), 1) // BLK
+    block = lax.broadcasted_iota(jnp.int32, (nnb, nu), 0)
+    widen = jnp.where(column == block, 1.0, 0.0).astype(jnp.bfloat16)
+    for copy in small:
+        copy.wait()
+    owned = jnp.concatenate(
+        [mask_ref[pl.ds(row_blocks[me[0] * nblk + b], 1), :] for b in range(nblk)], axis=0
+    )
+    mask = jnp.dot(owned.astype(jnp.float32).astype(jnp.bfloat16), widen, preferred_element_type=jnp.float32)
+    mask = mask.astype(jnp.bfloat16)
+    for g in range(GROUPS):
+        copies[g].wait()
+        blocks = range(g * nblk // GROUPS, (g + 1) * nblk // GROUPS)
+        for b in blocks:
+            x_ref[b * depth : (b + 1) * depth, :] *= mask[b : b + 1, :]
+        turn_blocks(x_ref, out_ref, 0, blocks)
+    vir_copy.wait()
+
+
+def first_order(me, row_blocks, pair_mask, integrals, vir, count):
+    mu_dev, fit_dev, nu = integrals.shape
+    rows = mu_dev * fit_dev
+    return pl.pallas_call(
+        first_kernel,
+        in_specs=[IN_SMEM] + [IN_ANY] * 4,
+        out_specs=[IN_VMEM, IN_SMEM, IN_VMEM, IN_VMEM],
+        scratch_shapes=[
+            pltpu.VMEM(pair_mask.shape, jnp.int32),
+            pltpu.SemaphoreType.DMA((GROUPS + 3,)),
+        ],
+        out_shape=[
+            pltpu.VMEM((count, mu_dev, nu), jnp.bfloat16),
+            pltpu.SMEM(row_blocks.shape, jnp.int32),
+            pltpu.VMEM(vir.shape, vir.dtype),
+            pltpu.VMEM((rows, nu), jnp.bfloat16),
+        ],
+        compiler_params=params(),
+        cost_estimate=pl.CostEstimate(
+            flops=2 * rows * BLK * count * nu, bytes_accessed=rows * nu * 4, transcendentals=0
+        ),
+        name="order",
+    )(me, hbm(row_blocks), hbm(pair_mask), hbm(integrals.reshape(rows, nu)), hbm(vir))
+
+
+def next_kernel(first_p, x_ref, out_ref):
+    turn_blocks(x_ref, out_ref, first_p, range(out_ref.shape[1] // BLK))
+
+
+def next_order(masked, first_p, count, mu_dev):
+    rows, nu = masked.shape
+    return pl.pallas_call(
+        functools.partial(next_kernel, first_p),
+        in_specs=[IN_VMEM],
+        out_specs=IN_VMEM,
+        out_shape=pltpu.VMEM((count, mu_dev, nu), jnp.bfloat16),
+        compiler_params=params(),
+        cost_estimate=pl.CostEstimate(
+            flops=2 * rows * BLK * count * nu, bytes_accessed=rows * nu * 4, transcendentals=0
+        ),
+        name="order",
+    )(vmem(masked))
+
+
+def half_kernel(me_ref, row_blocks, own_occ, far_occ, core_occ, diag_occ, x_ref, here_ref, far_ref, send_ref):
+    me = me_ref[0]
+    nocc, rows = own_occ.shape
+    nblk = rows // BLK
+    share = nocc // 4
+    x, c = me // 2, me % 2
+    device = [me, 2 * (1 - x) + c, 2 * x + 1 - c, 2 * (1 - x) + 1 - c]
+    lane = lax.broadcasted_iota(jnp.int32, (rows, rows), 1)
+    wanted = jnp.zeros((rows, rows), jnp.int32)
+    for b in range(nblk):
+        wanted = jnp.where(lane // BLK == b, row_blocks[me * nblk + b] * BLK + lane % BLK, wanted)
+    held = lax.broadcasted_iota(jnp.int32, (rows, rows), 0)
+    mine = jnp.zeros((nocc, rows), jnp.float32)
+    for k, occ in enumerate((own_occ, far_occ, core_occ, diag_occ)):
+        take = jnp.where(held + device[k] * rows == wanted, 1.0, 0.0).astype(jnp.bfloat16)
+        mine += jnp.dot(occ[...], take, preferred_element_type=jnp.float32)
+    to = lax.broadcasted_iota(jnp.int32, (nocc, nocc), 0)
+    at = lax.broadcasted_iota(jnp.int32, (nocc, nocc), 1)
+    dest = jnp.full((nocc, nocc), device[3], jnp.int32)
+    for k in range(3):
+        dest = jnp.where(to // share == k, device[k], dest)
+    pick = jnp.where((at // share == dest) & (at % share == to % share), 1.0, 0.0).astype(jnp.bfloat16)
+    turned = jnp.dot(pick, mine.astype(jnp.bfloat16), preferred_element_type=jnp.float32).astype(jnp.bfloat16)
+    zero = jnp.zeros_like(turned)
+    pair = jnp.concatenate(
+        [jnp.concatenate([turned, zero], axis=1), jnp.concatenate([zero, turned], axis=1)], axis=0
+    )
+    for u in range(0, here_ref.shape[0], 2):
+        both = x_ref[u : u + 2].reshape(2 * rows, x_ref.shape[2])
+        out = jnp.dot(pair, both, preferred_element_type=jnp.float32)
+        for v in range(2):
+            for k, own_ref in enumerate((here_ref, far_ref)):
+                at_own, at_send = v * nocc + k * share, v * nocc + (2 + k) * share
+                own_ref[u + v] = out[at_own : at_own + share]
+                send_ref[k, u + v] = out[at_send : at_send + share].astype(jnp.bfloat16)
+
+
+def half_terms(me, row_blocks, occs, turned):
+    count, rows, nu = turned.shape
+    nocc = occs[0].shape[0]
+    share = nocc // 4
+    return pl.pallas_call(
+        half_kernel,
+        in_specs=[IN_SMEM, IN_SMEM] + [IN_VMEM] * 5,
+        out_specs=[IN_VMEM] * 3,
+        out_shape=[
+            pltpu.VMEM((count, share, nu), jnp.float32),
+            pltpu.VMEM((count, share, nu), jnp.float32),
+            pltpu.VMEM((2, count, share, nu), jnp.bfloat16),
+        ],
+        compiler_params=params(),
+        cost_estimate=pl.CostEstimate(
+            flops=4 * count * nocc * rows * nu, bytes_accessed=count * nu * (2 * rows + 3 * nocc), transcendentals=0
+        ),
+        name="half",
+    )(me, row_blocks, *[vmem(occ) for occ in occs], vmem(turned))
+
+
+def add_kernel(k, own_ref, core_ref, *refs):
+    out_ref = refs[-1]
+    total = own_ref[...] + core_ref[k].astype(jnp.float32)
+    for ref in refs[:-1]:
+        total += ref[...].astype(jnp.float32)
+    out_ref[...] = total.astype(jnp.bfloat16).reshape(out_ref.shape)
+
+
+def add(own, core, k, others, shape):
+    return pl.pallas_call(
+        functools.partial(add_kernel, k),
+        in_specs=[IN_VMEM] * (2 + len(others)),
+        out_specs=IN_VMEM,
+        out_shape=pltpu.VMEM(shape, jnp.bfloat16),
+        compiler_params=params(),
+        cost_estimate=pl.CostEstimate(flops=2 * own.size, bytes_accessed=8 * own.size, transcendentals=0),
+        name="add",
+    )(*[vmem(value) for value in (own, core, *others)])
+
+
+def work_kernel(moved, made, n_copy, n_after, last, *refs):
+    refs = list(refs)
+    place, vir_ref = refs[:2]
+    at = 2 + n_copy
+    next_refs, h_refs = refs[2:at], refs[at : at + len(made)]
+    prev_ref = refs[at + len(made)] if moved else None
+    sems = refs[-1]
+    copy_refs = refs[len(refs) - 1 - n_copy : -1]
+    buf_ref, out_ref = refs[-2 - n_copy], refs[-3 - n_copy]
+    if last:
+        buf_ref, out_ref = refs[-2], refs[-3]
+    y = place[ZS]
+
+    def copies(buf, blocks, base):
+        rows = buf.shape[0] // len(blocks)
+        return [
+            pltpu.make_async_copy(
+                buf.at[pl.ds(v * rows, rows)],
+                out_ref.at[place[step], 1 - y if side else y, pl.ds(first_row, rows)],
+                sems.at[base + v],
+            )
+            for v, (step, first_row, side) in enumerate(blocks)
+        ]
+
+    going = copies(prev_ref, moved, 0) if moved else []
+    for copy in going:
+        copy.start()
+    for next_ref, copy_ref in zip(next_refs, copy_refs):
+        copy_ref[...] = next_ref[...]
+    rows = jnp.concatenate([h[...] for h in h_refs], axis=0)
+    buf_ref[...] = jnp.dot(rows, vir_ref[...], preferred_element_type=jnp.float32).astype(jnp.bfloat16)
+    if last:
+        final = copies(buf_ref, made, 2)
+        for copy in final:
+            copy.start()
+        going += final
+    for copy in going:
+        copy.wait()
+
+
+def work(state, place, vir, made, hs, out_type, sent=(), after=(), last=False):
+    out, buf, moved = state
+    rows, nv = hs[0].shape[0], vir.shape[1]
+    inside = [vir, *sent, *hs] + ([buf] if moved else [])
+    ops = [place, *map(vmem, inside), *after] + ([] if out is None else [out])
+    block = pltpu.VMEM((len(hs) * rows, nv), jnp.bfloat16)
+    results = [] if last else [block] + [pltpu.VMEM(value.shape, value.dtype) for value in sent]
+    got = pl.pallas_call(
+        functools.partial(work_kernel, moved, made, len(sent), len(after), last),
+        in_specs=[IN_SMEM] + [IN_VMEM] * len(inside) + [IN_ANY] * (len(after) + (out is not None)),
+        out_specs=[IN_ANY] + [IN_VMEM] * len(results),
+        scratch_shapes=([block] if last else []) + [pltpu.SemaphoreType.DMA((4,))],
+        out_shape=[out_type] + results,
+        input_output_aliases={} if out is None else {len(ops) - 1: 0},
+        compiler_params=params(),
+        cost_estimate=pl.CostEstimate(flops=PROJ_FLOPS, bytes_accessed=PROJ_BYTES, transcendentals=0),
+        name="project",
+    )(*ops)
+    return (got[0], None if last else got[1], made), *got[2:]
+
+
+def shards_blocked(integrals, pair_mask, row_blocks, occ_coef, vir_coef):
+    mu_dev, fit_dev, nu = integrals.shape
+    nocc, nv = occ_coef.shape[1], vir_coef.shape[1]
+    share = nocc // 4
+    me = lax.axis_index("basis").astype(jnp.int32).reshape(1)
+    f = lax.axis_index("fit")
+    z, y = f // YS, f % YS
+    counts = [fit_dev * part // 16 for part in PARTS]
+    starts = [0, counts[0]]
+
+    occ = occ_coef.T
+    occs = [occ] + [lax.ppermute(occ, "basis", swap) for swap in (X_SWAP, CORE_SWAP, DIAGONAL)]
+    turned, row_blocks, vir, masked = first_order(me, row_blocks, pair_mask, integrals, vir_coef, counts[0])
+
+    held = []
+    for k in range(2):
+        here, far, send = half_terms(me, row_blocks, occs, turned)
+        got = lax.ppermute(send, "basis", CORE_SWAP)
+        to_x = add(far, got, 1, [], far.shape)
+        from_x = lax.ppermute(to_x, "basis", X_SWAP)
+        held.append(add(here, got, 0, [from_x], (counts[k] * share, nu)))
+        if k == 0:
+            turned = next_order(masked, starts[1], counts[1], mu_dev)
+
+    place = jnp.concatenate([(z - jnp.arange(ZS)) % ZS, y.reshape(1)]).astype(jnp.int32)
+    run = functools.partial(
+        work, place=place, vir=vir, out_type=jax.ShapeDtypeStruct((ZS, YS, fit_dev * share, nv), jnp.bfloat16)
+    )
+    up, down, swap = [functools.partial(lax.ppermute, axis_name="fit", perm=p) for p in (Z_RING, Z_BACK, Y_SWAP)]
+    a0, b0 = held
+    row_a, row_b = [start * share for start in starts]
+
+    def pair(step, row):
+        return [(step, row, 0), (step, row, 1)]
+
+    a1, a0_y = up(a0), swap(a0)
+    b1, b0_y = up(b0), swap(b0)
+    a2 = up(a1)
+    state, a1_copy = run((None, None, None), made=pair(0, row_a), hs=[a0, a0_y], sent=[a1])
+    a1_y = swap(a1_copy)
+    b2 = up(b1)
+    state, b1_copy = run(state, made=pair(0, row_b), hs=[b0, b0_y], sent=[b1])
+    b1_y = swap(b1_copy)
+    a3 = up(a2)
+    state, a2_copy = run(state, made=pair(1, row_a), hs=[a1, a1_y], sent=[a2])
+    a2_y = swap(a2_copy)
+    b3 = up(b2)
+    state, b2_copy, b0_y_copy = run(state, made=pair(1, row_b), hs=[b1, b1_y], sent=[b2, b0_y])
+    b2_y = swap(b2_copy)
+    b3_y = down(b0_y_copy)
+    state, a3_copy = run(state, made=pair(2, row_a), hs=[a2, a2_y], sent=[a3])
+    a3_y = swap(a3_copy)
+    state, = run(state, made=pair(2, row_b), hs=[b2, b2_y], after=[b3])
+    state, = run(state, made=[(3, row_a, 0), (3, row_b, 0)], hs=[a3, b3])
+    state, = run(state, made=[(3, row_a, 1)], hs=[a3_y])
+    state, = run(state, made=[(3, row_b, 1)], hs=[b3_y], last=True)
+    return state[0].reshape(ZS * YS * fit_dev, share, nv)
 
 
 def shards(integrals, pair_mask, row_blocks, occ_coef, vir_coef):
@@ -41,6 +365,5 @@
 
 def solution(mesh):
     placed = (P("basis", "fit", None), P(), P(), P("basis", None), P(None, "fit"))
-    return jax.shard_map(
-        shards, mesh=mesh, in_specs=placed, out_specs=P(None, "basis", "fit"), check_vma=False
-    )
+    body = shards_blocked if (mesh.shape["basis"], mesh.shape["fit"]) == (4, ZS * YS) else shards
+    return jax.shard_map(body, mesh=mesh, in_specs=placed, out_specs=P(None, "basis", "fit"), check_vma=False)

time: 166 us -> 66.7 us (0.40)
  waiting for transfers between devices: 120 us -> 18.1 us
  starting transfers between devices: 0.04 us -> 24.2 us
  Pallas kernels: 0 us -> 22.9 us
  between operations: 13.5 us -> 0.18 us
  local copies, waits for them, and re-layouts: 11.1 us -> 1.05 us
  matrix products: 9.68 us -> 0 us
  blocking collectives: 6.48 us -> 0 us
  other arithmetic: 4.88 us -> 0.08 us
    all_gather x1 -> x0, waiting for transfers between devices: 73.5 us -> none  [shards(): lax.all_gather(half, 'fit', axis=1, tiled=True)]
    reduce_scatter x1 -> x0, waiting for transfers between devices: 46.3 us -> none  [shards(): lax.psum_scatter(lax.dot_general(occ_rows, flat, (((0,), (0,)), ((), ()))...]
    ppermute x0 -> x21, starting transfers between devices: none -> 24.2 us  [the longest x2 3.4 us: shards_blocked(): a1, a0_y = (up(a0), swap(a0))]
    pallas_call x0 -> x17, Pallas kernels: none -> 22.9 us  [the longest x9 15.8 us: work(): pl.pallas_call(functools.partial(work_kernel, moved, made, len(sent), len...]
    ppermute x0 -> x21, waiting for transfers between devices: none -> 18.1 us  [the longest x2 7.02 us: shards_blocked(): from_x = lax.ppermute(to_x, 'basis', X_SWAP)]
    dot_general x2 -> x0, matrix products: 9.68 us -> none  [the longest x1 6.92 us: shards(): jnp.einsum('ipn,na->pia', lax.all_gather(half, 'fit', axis=1, tiled=True)...]
    all_gather x1 -> x0, blocking collectives: 6.48 us -> none  [shards(): panels = lax.all_gather(occ_coef, 'basis', axis=0, tiled=True)]
    convert_element_type x1 -> x0, local copies, waits for them, and re-layouts: 4.34 us -> none  [shards(): return product.astype(jnp.bfloat16)]
  transfers between devices with their start and end apart: 2 -> 21, of which waited for: 2 -> 8; matrix products, arithmetic and copies ran while one was open for 0% -> 0% of each run, Pallas kernels for 0% -> 31%
where the time goes in v3:
time: 66.7 us; the launch traced here: 66.5 us
  starting transfers between devices  24.2 us (36%)
  Pallas kernels  22.9 us (34%)
  waiting for transfers between devices  18.1 us (27%)
  local copies, waits for them, and re-layouts  1.05 us (2%)
    pallas_call x9, Pallas kernels, work(): pl.pallas_call(functools.partial(work_kernel, moved, made, len(sent), len...  15.8 us
    ppermute x2, waiting for transfers between devices, shards_blocked(): from_x = lax.ppermute(to_x, 'basis', X_SWAP)  7.02 us
    ppermute x2, waiting for transfers between devices, shards_blocked(): b1, b0_y = (up(b0), swap(b0))  4.37 us
    ppermute x2, starting transfers between devices, shards_blocked(): a1, a0_y = (up(a0), swap(a0))  3.4 us
    ppermute x2, starting transfers between devices, shards_blocked(): from_x = lax.ppermute(to_x, 'basis', X_SWAP)  3.16 us
    ppermute x2, starting transfers between devices, shards_blocked(): b1, b0_y = (up(b0), swap(b0))  3.15 us
    ppermute x3, starting transfers between devices, shards_blocked(): lax.ppermute(occ, 'basis', swap)  3.13 us
    pallas_call x1, Pallas kernels, first_order(): pl.pallas_call(first_kernel, in_specs=[IN_SMEM] + [IN_ANY] * 4, out_specs...  2.92 us
  transfers between devices with their start and end apart: 21, of which 8 were waited for; matrix products, arithmetic and copies ran while one was open for 0% of the time, Pallas kernels for 31%

profile of v3, /device:TPU:0, one launch (start us, length us, event | category | flops | bytes accessed | tf_op | source)
XLA Modules:
  0.0 66.5 jit_solution(16384095680625257360)
XLA Ops:
  0.0 2.9 %collective-permute-start = (bf16[64,128]{1,0:T(8,128)(2,1)}, bf16[64,128]{1,0:T(8,128)(2,1)S(1)}, u32[]{:S(2)}, u32[]{:S(2)}) collective-permute-start(bf16[64,128]{1,0:T(8,128)(2,1)} %bitcast.5), channel_id=1, source_target_pairs={{0,16},{16,0},{8,24},{24,8},{1,17},{17,1},{9,25},{25,9},{2,18},{18... | collective-permute-start | bytes 49160 | tf_op jit(solution)/shard_map/ppermute | solution.py:285
  3.1 2.9 %order.2 = (bf16[8,128,1024]{2,1,0:T(8,128)(2,1)S(1)}, s32[32]{0:T(128)S(4)}, bf16[1024,1024]{1,0:T(8,128)(2,1)S(1)}, bf16[2048,1024]{1,0:T(8,128)(2,1)S(1)}) custom-call(s32[1]{0:T(128)} %bitcast.1.me.me_ref, s32[32]{0:T(128)} %row_blocks_hbm.1, s32[32,64]{1,0:T(8,128)} %mask_hbm.1, bf16[2048,1024]{1,0:T(8,128)(2,1)} %bitcast.10, bf16[1024,1024]{1,0:T(8,128)(2,1)} %vir_hbm.1), custom_call_target="tpu_custom_call" | custom-call | flops 536870912 | bytes 8388608 | tf_op jit(solution)/shard_map/order/pallas_call | solution.py:94
  8.4 0.8 %half.2 = (f32[8,16,1024]{2,1,0:T(8,128)S(1)}, f32[8,16,1024]{2,1,0:T(8,128)S(1)}, bf16[2,8,16,1024]{3,2,1,0:T(8,128)(2,1)S(1)}) custom-call(s32[1]{0:T(128)} %bitcast.1.me.me_ref, s32[32]{0:T(128)S(4)} %get-tuple-element.38.row_blocks, bf16[64,128]{1,0:T(8,128)(2,1)S(1)} %bitcast.9, bf16[64,128]{1,0:T(8,128)(2,1)S(1)} %collective-permute-done.far_occ, ...), custom_call_target="tpu_custom_call" | custom-call | flops 268435456 | bytes 3670016 | tf_op jit(solution)/shard_map/half/pallas_call | solution.py:176
  9.3 1.8 %collective-permute-start.9 = (bf16[8,16,1024]{2,1,0:T(8,128)(2,1)S(1)}, bf16[8,16,1024]{2,1,0:T(8,128)(2,1)S(1)}, u32[]{:S(2)}, u32[]{:S(2)}) collective-permute-start(bf16[8,16,1024]{2,1,0:T(8,128)(2,1)S(1)} %add.22), channel_id=1, source_target_pairs={{0,16},{16,0},{8,24},{24,8},{1,17},{17,1},{9,25},{25,9},{2,18},{18... | collective-permute-start | bytes 786440 | tf_op jit(solution)/shard_map/ppermute | solution.py:293
  11.9 1.4 %collective-permute-start.4 = (bf16[8,16,1024]{2,1,0:T(8,128)(2,1)}, bf16[8,16,1024]{2,1,0:T(8,128)(2,1)}, u32[]{:S(2)}, u32[]{:S(2)}) collective-permute-start(bf16[8,16,1024]{2,1,0:T(8,128)(2,1)} %add.20), channel_id=1, source_target_pairs={{0,16},{16,0},{8,24},{24,8},{1,17},{17,1},{9,25},{25,9},{2,18},{18... | collective-permute-start | bytes 786440 | tf_op jit(solution)/shard_map/ppermute | solution.py:293
  13.3 5.2 %collective-permute-done.9.refs_0_ = bf16[8,16,1024]{2,1,0:T(8,128)(2,1)S(1)} collective-permute-done((bf16[8,16,1024]{2,1,0:T(8,128)(2,1)S(1)}, bf16[8,16,1024]{2,1,0:T(8,128)(2,1)S(1)}, u32[]{:S(2)}, u32[]{:S(2)}) %collective-permute-start.9) | collective-permute-done | bytes 262176 | tf_op jit(solution)/shard_map/ppermute | solution.py:293
  18.6 1.9 %collective-permute-start.10 = (bf16[128,1024]{1,0:T(8,128)(2,1)S(1)}, bf16[128,1024]{1,0:T(8,128)(2,1)S(1)}, u32[]{:S(2)}, u32[]{:S(2)}) collective-permute-start(bf16[128,1024]{1,0:T(8,128)(2,1)S(1)} %add.23.refs_3_), channel_id=1, source_target_pairs={{0,2},{1,3},{2,4},{3,5},{4,6},{5,7},{6,0},{7,1},{8,10},{9,11},{10,... | collective-permute-start | bytes 786440 | tf_op jit(solution)/shard_map/ppermute | solution.py:309
  20.5 1.5 %collective-permute-start.11 = (bf16[128,1024]{1,0:T(8,128)(2,1)S(1)}, bf16[128,1024]{1,0:T(8,128)(2,1)S(1)}, u32[]{:S(2)}, u32[]{:S(2)}) collective-permute-start(bf16[128,1024]{1,0:T(8,128)(2,1)S(1)} %add.23.refs_3_), channel_id=1, source_target_pairs={{0,1},{1,0},{2,3},{3,2},{4,5},{5,4},{6,7},{7,6},{8,9},{9,8},{10,11... | collective-permute-start | bytes 786440 | tf_op jit(solution)/shard_map/ppermute | solution.py:309
  22.0 1.8 %collective-permute-done.4.refs_0_ = bf16[8,16,1024]{2,1,0:T(8,128)(2,1)} collective-permute-done((bf16[8,16,1024]{2,1,0:T(8,128)(2,1)}, bf16[8,16,1024]{2,1,0:T(8,128)(2,1)}, u32[]{:S(2)}, u32[]{:S(2)}) %collective-permute-start.4) | collective-permute-done | bytes 262176 | tf_op jit(solution)/shard_map/ppermute | solution.py:293
  23.8 1.0 %copy-done.1 = f32[8,16,1024]{2,1,0:T(8,128)S(1)} copy-done((f32[8,16,1024]{2,1,0:T(8,128)S(1)}, f32[8,16,1024]{2,1,0:T(8,128)}, u32[]{:S(2)}) %copy-start.1) | copy-done | bytes 524312
  24.8 1.0 %add.21.refs_3_ = bf16[128,1024]{1,0:T(8,128)(2,1)S(1)} custom-call(f32[8,16,1024]{2,1,0:T(8,128)S(1)} %copy-done.1, bf16[2,8,16,1024]{3,2,1,0:T(8,128)(2,1)S(1)} %collective-permute-done.3.core_ref, bf16[8,16,1024]{2,1,0:T(8,128)(2,1)} %collective-permute-done.4.refs_0_), custom_call_target="tpu_custom_call" | custom-call | flops 262144 | bytes 1048576 | tf_op jit(solution)/shard_map/add/pallas_call | solution.py:202
  25.9 1.6 %collective-permute-start.5 = (bf16[128,1024]{1,0:T(8,128)(2,1)S(1)}, bf16[128,1024]{1,0:T(8,128)(2,1)S(1)}, u32[]{:S(2)}, u32[]{:S(2)}) collective-permute-start(bf16[128,1024]{1,0:T(8,128)(2,1)S(1)} %add.21.refs_3_), channel_id=1, source_target_pairs={{0,2},{1,3},{2,4},{3,5},{4,6},{5,7},{6,0},{7,1},{8,10},{9,11},{10,... | collective-permute-start | bytes 786440 | tf_op jit(solution)/shard_map/ppermute | solution.py:310
  27.5 1.5 %collective-permute-start.7 = (bf16[128,1024]{1,0:T(8,128)(2,1)S(1)}, bf16[128,1024]{1,0:T(8,128)(2,1)S(1)}, u32[]{:S(2)}, u32[]{:S(2)}) collective-permute-start(bf16[128,1024]{1,0:T(8,128)(2,1)S(1)} %add.21.refs_3_), channel_id=1, source_target_pairs={{0,1},{1,0},{2,3},{3,2},{4,5},{5,4},{6,7},{7,6},{8,9},{9,8},{10,11... | collective-permute-start | bytes 786440 | tf_op jit(solution)/shard_map/ppermute | solution.py:310
  29.1 1.6 %collective-permute-start.13 = (bf16[128,1024]{1,0:T(8,128)(2,1)S(1)}, bf16[128,1024]{1,0:T(8,128)(2,1)S(1)}, u32[]{:S(2)}, u32[]{:S(2)}) collective-permute-start(bf16[128,1024]{1,0:T(8,128)(2,1)S(1)} %collective-permute-done.10.refs_2_.refs_3_), channel_id=1, source_target_pairs={{0,2},{1,3},{2,4},{3,5},{4,6},{5,7},{6,0},{7,1},{8,10},{9,11},{10,... | collective-permute-start | bytes 786440 | tf_op jit(solution)/shard_map/ppermute | solution.py:311
  30.7 1.3 %project.9 = (bf16[4,2,256,1024]{3,2,1,0:T(8,128)(2,1)}, bf16[256,1024]{1,0:T(8,128)(2,1)S(1)}, bf16[128,1024]{1,0:T(8,128)(2,1)S(1)}) custom-call(s32[5]{0:T(128)S(1)} %pad_add_fusion.refs_0_, bf16[1024,1024]{1,0:T(8,128)(2,1)S(1)} %get-tuple-element.37.refs_1_, bf16[128,1024]{1,0:T(8,128)(2,1)S(1)} %collective-permute-done.10.refs_2_.refs_3_, ...), custom_call_target="tpu_custom_call" | custom-call | flops 1000 | bytes 1000 | tf_op jit(solution)/shard_map/project/pallas_call | solution.py:260
  32.6 4.4 %collective-permute-done.5.refs_2_.refs_4_ = bf16[128,1024]{1,0:T(8,128)(2,1)S(1)} collective-permute-done((bf16[128,1024]{1,0:T(8,128)(2,1)S(1)}, bf16[128,1024]{1,0:T(8,128)(2,1)S(1)}, u32[]{:S(2)}, u32[]{:S(2)}) %collective-permute-start.5) | collective-permute-done | bytes 262176 | tf_op jit(solution)/shard_map/ppermute | solution.py:310
  36.9 1.9 %project.10 = (bf16[4,2,256,1024]{3,2,1,0:T(8,128)(2,1)}, bf16[256,1024]{1,0:T(8,128)(2,1)S(1)}, bf16[128,1024]{1,0:T(8,128)(2,1)S(1)}) custom-call(s32[5]{0:T(128)S(1)} %pad_add_fusion.refs_0_, bf16[1024,1024]{1,0:T(8,128)(2,1)S(1)} %get-tuple-element.37.refs_1_, ...), custom_call_target="tpu_custom_call", output_to_operand_aliasing={{0}: (6, {})} | custom-call | flops 1000 | bytes 1000 | tf_op jit(solution)/shard_map/project/pallas_call | solution.py:260
  38.8 1.6 %collective-permute-start.12 = (bf16[128,1024]{1,0:T(8,128)(2,1)S(1)}, bf16[128,1024]{1,0:T(8,128)(2,1)S(1)}, u32[]{:S(2)}, u32[]{:S(2)}) collective-permute-start(bf16[128,1024]{1,0:T(8,128)(2,1)S(1)} %get-tuple-element.49), channel_id=1, source_target_pairs={{0,1},{1,0},{2,3},{3,2},{4,5},{5,4},{6,7},{7,6},{8,9},{9,8},{10,11... | collective-permute-start | bytes 786440 | tf_op jit(solution)/shard_map/ppermute | solution.py:316
  40.4 2.1 %collective-permute-done.13.refs_2_.refs_3_ = bf16[128,1024]{1,0:T(8,128)(2,1)S(1)} collective-permute-done((bf16[128,1024]{1,0:T(8,128)(2,1)S(1)}, bf16[128,1024]{1,0:T(8,128)(2,1)S(1)}, u32[]{:S(2)}, u32[]{:S(2)}) %collective-permute-start.13) | collective-permute-done | bytes 262176 | tf_op jit(solution)/shard_map/ppermute | solution.py:311
  42.6 1.9 %project.11 = (bf16[4,2,256,1024]{3,2,1,0:T(8,128)(2,1)}, bf16[256,1024]{1,0:T(8,128)(2,1)S(1)}, bf16[128,1024]{1,0:T(8,128)(2,1)S(1)}) custom-call(s32[5]{0:T(128)S(1)} %pad_add_fusion.refs_0_, bf16[1024,1024]{1,0:T(8,128)(2,1)S(1)} %get-tuple-element.37.refs_1_, ...), custom_call_target="tpu_custom_call", output_to_operand_aliasing={{0}: (6, {})} | custom-call | flops 1000 | bytes 1000 | tf_op jit(solution)/shard_map/project/pallas_call | solution.py:260
  44.4 1.6 %collective-permute-start.17 = (bf16[128,1024]{1,0:T(8,128)(2,1)S(1)}, bf16[128,1024]{1,0:T(8,128)(2,1)S(1)}, u32[]{:S(2)}, u32[]{:S(2)}) collective-permute-start(bf16[128,1024]{1,0:T(8,128)(2,1)S(1)} %get-tuple-element.56), channel_id=1, source_target_pairs={{0,1},{1,0},{2,3},{3,2},{4,5},{5,4},{6,7},{7,6},{8,9},{9,8},{10,11... | collective-permute-start | bytes 786440 | tf_op jit(solution)/shard_map/ppermute | solution.py:319
  46.1 2.1 %collective-permute-done.6.refs_2_ = bf16[128,1024]{1,0:T(8,128)(2,1)S(1)} collective-permute-done((bf16[128,1024]{1,0:T(8,128)(2,1)S(1)}, bf16[128,1024]{1,0:T(8,128)(2,1)S(1)}, u32[]{:S(2)}, u32[]{:S(2)}) %collective-permute-start.6) | collective-permute-done | bytes 262176 | tf_op jit(solution)/shard_map/ppermute | solution.py:314
  48.2 1.9 %project.12 = (bf16[4,2,256,1024]{3,2,1,0:T(8,128)(2,1)}, bf16[256,1024]{1,0:T(8,128)(2,1)S(1)}, bf16[128,1024]{1,0:T(8,128)(2,1)S(1)}, bf16[128,1024]{1,0:T(8,128)(2,1)S(1)}) custom-call(s32[5]{0:T(128)S(1)} %pad_add_fusion.refs_0_, bf16[1024,1024]{1,0:T(8,128)(2,1)S(1)} %get-tuple-element.37.refs_1_, ...), custom_call_target="tpu_custom_call", output_to_operand_aliasing={{0}: (7, {})} | custom-call | flops 1000 | bytes 1000 | tf_op jit(solution)/shard_map/project/pallas_call | solution.py:260
  50.1 1.6 %collective-permute-start.20 = (bf16[128,1024]{1,0:T(8,128)(2,1)S(1)}, bf16[128,1024]{1,0:T(8,128)(2,1)S(1)}, u32[]{:S(2)}, u32[]{:S(2)}) collective-permute-start(bf16[128,1024]{1,0:T(8,128)(2,1)S(1)} %get-tuple-element.60), channel_id=1, source_target_pairs={{0,1},{1,0},{2,3},{3,2},{4,5},{5,4},{6,7},{7,6},{8,9},{9,8},{10,11... | collective-permute-start | bytes 786440 | tf_op jit(solution)/shard_map/ppermute | solution.py:322
  51.7 2.1 %collective-permute-done.16.refs_2_ = bf16[128,1024]{1,0:T(8,128)(2,1)S(1)} collective-permute-done((bf16[128,1024]{1,0:T(8,128)(2,1)S(1)}, bf16[128,1024]{1,0:T(8,128)(2,1)S(1)}, u32[]{:S(2)}, u32[]{:S(2)}) %collective-permute-start.16) | collective-permute-done | bytes 262176 | tf_op jit(solution)/shard_map/ppermute | solution.py:317
  53.8 1.9 %project.13 = (bf16[4,2,256,1024]{3,2,1,0:T(8,128)(2,1)}, bf16[256,1024]{1,0:T(8,128)(2,1)S(1)}, bf16[128,1024]{1,0:T(8,128)(2,1)S(1)}) custom-call(s32[5]{0:T(128)S(1)} %pad_add_fusion.refs_0_, bf16[1024,1024]{1,0:T(8,128)(2,1)S(1)} %get-tuple-element.37.refs_1_, ...), custom_call_target="tpu_custom_call", output_to_operand_aliasing={{0}: (6, {})} | custom-call | flops 1000 | bytes 1000 | tf_op jit(solution)/shard_map/project/pallas_call | solution.py:260
  55.7 1.6 %collective-permute-start.18 = (bf16[128,1024]{1,0:T(8,128)(2,1)S(1)}, bf16[128,1024]{1,0:T(8,128)(2,1)S(1)}, u32[]{:S(2)}, u32[]{:S(2)}) collective-permute-start(bf16[128,1024]{1,0:T(8,128)(2,1)S(1)} %get-tuple-element.59), channel_id=1, source_target_pairs={{0,1},{1,0},{2,3},{3,2},{4,5},{5,4},{6,7},{7,6},{8,9},{9,8},{10,11... | collective-permute-start | bytes 786440 | tf_op jit(solution)/shard_map/ppermute | solution.py:325
  57.3 2.1 %collective-permute-start.15 = (bf16[128,1024]{1,0:T(8,128)(2,1)S(1)}, bf16[128,1024]{1,0:T(8,128)(2,1)S(1)}, u32[]{:S(2)}, u32[]{:S(2)}) collective-permute-start(bf16[128,1024]{1,0:T(8,128)(2,1)S(1)} %get-tuple-element.55), channel_id=1, source_target_pairs={{2,0},{3,1},{4,2},{5,3},{6,4},{7,5},{0,6},{1,7},{10,8},{11,9},{12,... | collective-permute-start | bytes 786440 | tf_op jit(solution)/shard_map/ppermute | solution.py:323
  59.4 1.8 %project.14 = (bf16[4,2,256,1024]{3,2,1,0:T(8,128)(2,1)}, bf16[256,1024]{1,0:T(8,128)(2,1)S(1)}) custom-call(s32[5]{0:T(128)S(1)} %pad_add_fusion.refs_0_, bf16[1024,1024]{1,0:T(8,128)(2,1)S(1)} %get-tuple-element.37.refs_1_, bf16[128,1024]{1,0:T(8,128)(2,1)S(1)} %collective-permute-done.6.refs_2_, ...), custom_call_target="tpu_custom_call", output_to_operand_aliasing={{0}: (6, {})} | custom-call | flops 1000 | bytes 1000 | tf_op jit(solution)/shard_map/project/pallas_call | solution.py:260
  61.3 1.9 %project.15 = (bf16[4,2,256,1024]{3,2,1,0:T(8,128)(2,1)}, bf16[256,1024]{1,0:T(8,128)(2,1)S(1)}) custom-call(s32[5]{0:T(128)S(1)} %pad_add_fusion.refs_0_, bf16[1024,1024]{1,0:T(8,128)(2,1)S(1)} %get-tuple-element.37.refs_1_, bf16[128,1024]{1,0:T(8,128)(2,1)S(1)} %collective-permute-done.16.refs_2_, ...), custom_call_target="tpu_custom_call", output_to_operand_aliasing={{0}: (5, {})} | custom-call | flops 1000 | bytes 1000 | tf_op jit(solution)/shard_map/project/pallas_call | solution.py:260
  63.2 1.6 %project.16 = (bf16[4,2,256,1024]{3,2,1,0:T(8,128)(2,1)}, bf16[128,1024]{1,0:T(8,128)(2,1)S(1)}) custom-call(s32[5]{0:T(128)S(1)} %pad_add_fusion.refs_0_, bf16[1024,1024]{1,0:T(8,128)(2,1)S(1)} %get-tuple-element.37.refs_1_, bf16[128,1024]{1,0:T(8,128)(2,1)S(1)} %collective-permute-done.18.refs_2_, ...), custom_call_target="tpu_custom_call", output_to_operand_aliasing={{0}: (4, {})} | custom-call | flops 1000 | bytes 1000 | tf_op jit(solution)/shard_map/project/pallas_call | solution.py:260
  64.8 1.7 %project.17 = bf16[4,2,256,1024]{3,2,1,0:T(8,128)(2,1)} custom-call(s32[5]{0:T(128)S(1)} %pad_add_fusion.refs_0_, bf16[1024,1024]{1,0:T(8,128)(2,1)S(1)} %get-tuple-element.37.refs_1_, bf16[128,1024]{1,0:T(8,128)(2,1)S(1)} %collective-permute-done.15.refs_2_, bf16[128,1024]{1,0:T(8,128)(2,1)S(1)} %get-tuple-element.67.refs_3_, ...), custom_call_target="tpu_custom_call", output_to_operand_aliasing={{}: (4, {})} | custom-call | flops 1000 | bytes 1000 | tf_op jit(solution)/shard_map/project/pallas_call | solution.py:260
  (35 shorter events, 4.2 us)
Async XLA Ops:
  0.0 6.3 %copy-start.2 = (bf16[128,64]{0,1:T(8,128)(2,1)S(1)}, bf16[128,64]{0,1:T(8,128)(2,1)}, u32[]{:S(2)}) copy-start(bf16[128,64]{0,1:T(8,128)(2,1)} %param.8) | copy-start | bytes 49156
  0.0 6.1 %collective-permute-start = (bf16[64,128]{1,0:T(8,128)(2,1)}, bf16[64,128]{1,0:T(8,128)(2,1)S(1)}, u32[]{:S(2)}, u32[]{:S(2)}) collective-permute-start(bf16[64,128]{1,0:T(8,128)(2,1)} %bitcast.5), channel_id=1, source_target_pairs={{0,16},{16,0},{8,24},{24,8},{1,17},{17,1},{9,25},{25,9},{2,18},{18... | collective-permute-start | bytes 49160 | tf_op jit(solution)/shard_map/ppermute | solution.py:285
  2.9 3.1 %collective-permute-start.1 = (bf16[64,128]{1,0:T(8,128)(2,1)}, bf16[64,128]{1,0:T(8,128)(2,1)S(1)}, u32[]{:S(2)}, u32[]{:S(2)}) collective-permute-start(bf16[64,128]{1,0:T(8,128)(2,1)} %bitcast.6), channel_id=1, source_target_pairs={{0,8},{8,0},{16,24},{24,16},{1,9},{9,1},{17,25},{25,17},{2,10},{10... | collective-permute-start | bytes 49160 | tf_op jit(solution)/shard_map/ppermute | solution.py:285
  2.9 3.4 %collective-permute-start.2 = (bf16[64,128]{1,0:T(8,128)(2,1)}, bf16[64,128]{1,0:T(8,128)(2,1)S(1)}, u32[]{:S(2)}, u32[]{:S(2)}) collective-permute-start(bf16[64,128]{1,0:T(8,128)(2,1)} %bitcast.7), channel_id=1, source_target_pairs={{0,24},{24,0},{8,16},{16,8},{1,25},{25,1},{9,17},{17,9},{2,26},{26... | collective-permute-start | bytes 49160 | tf_op jit(solution)/shard_map/ppermute | solution.py:285
  7.1 2.2 %collective-permute-start.8 = (bf16[2,8,16,1024]{3,2,1,0:T(8,128)(2,1)S(1)}, bf16[2,8,16,1024]{3,2,1,0:T(8,128)(2,1)S(1)}, u32[]{:S(2)}, u32[]{:S(2)}) collective-permute-start(bf16[2,8,16,1024]{3,2,1,0:T(8,128)(2,1)S(1)} %get-tuple-element.45), channel_id=1, source_target_pairs={{0,8},{8,0},{16,24},{24,16},{1,9},{9,1},{17,25},{25,17},{2,10},{10... | collective-permute-start | bytes 1572872 | tf_op jit(solution)/shard_map/ppermute | solution.py:291
  9.2 9.4 %copy-start = (f32[8,16,1024]{2,1,0:T(8,128)}, f32[8,16,1024]{2,1,0:T(8,128)S(1)}, u32[]{:S(2)}) copy-start(f32[8,16,1024]{2,1,0:T(8,128)S(1)} %get-tuple-element.40.own_ref) | copy-start | bytes 1572868
  9.2 2.0 %collective-permute-start.3 = (bf16[2,8,16,1024]{3,2,1,0:T(8,128)(2,1)S(1)}, bf16[2,8,16,1024]{3,2,1,0:T(8,128)(2,1)S(1)}, u32[]{:S(2)}, u32[]{:S(2)}) collective-permute-start(bf16[2,8,16,1024]{3,2,1,0:T(8,128)(2,1)S(1)} %get-tuple-element.41), channel_id=1, source_target_pairs={{0,8},{8,0},{16,24},{24,16},{1,9},{9,1},{17,25},{25,17},{2,10},{10... | collective-permute-start | bytes 1572872 | tf_op jit(solution)/shard_map/ppermute | solution.py:291
  9.3 9.2 %collective-permute-start.9 = (bf16[8,16,1024]{2,1,0:T(8,128)(2,1)S(1)}, bf16[8,16,1024]{2,1,0:T(8,128)(2,1)S(1)}, u32[]{:S(2)}, u32[]{:S(2)}) collective-permute-start(bf16[8,16,1024]{2,1,0:T(8,128)(2,1)S(1)} %add.22), channel_id=1, source_target_pairs={{0,16},{16,0},{8,24},{24,8},{1,17},{17,1},{9,25},{25,9},{2,18},{18... | collective-permute-start | bytes 786440 | tf_op jit(solution)/shard_map/ppermute | solution.py:293
  11.9 11.9 %collective-permute-start.4 = (bf16[8,16,1024]{2,1,0:T(8,128)(2,1)}, bf16[8,16,1024]{2,1,0:T(8,128)(2,1)}, u32[]{:S(2)}, u32[]{:S(2)}) collective-permute-start(bf16[8,16,1024]{2,1,0:T(8,128)(2,1)} %add.20), channel_id=1, source_target_pairs={{0,16},{16,0},{8,24},{24,8},{1,17},{17,1},{9,25},{25,9},{2,18},{18... | collective-permute-start | bytes 786440 | tf_op jit(solution)/shard_map/ppermute | solution.py:293
  18.6 10.5 %collective-permute-start.10 = (bf16[128,1024]{1,0:T(8,128)(2,1)S(1)}, bf16[128,1024]{1,0:T(8,128)(2,1)S(1)}, u32[]{:S(2)}, u32[]{:S(2)}) collective-permute-start(bf16[128,1024]{1,0:T(8,128)(2,1)S(1)} %add.23.refs_3_), channel_id=1, source_target_pairs={{0,2},{1,3},{2,4},{3,5},{4,6},{5,7},{6,0},{7,1},{8,10},{9,11},{10,... | collective-permute-start | bytes 786440 | tf_op jit(solution)/shard_map/ppermute | solution.py:309
  20.5 10.2 %collective-permute-start.11 = (bf16[128,1024]{1,0:T(8,128)(2,1)S(1)}, bf16[128,1024]{1,0:T(8,128)(2,1)S(1)}, u32[]{:S(2)}, u32[]{:S(2)}) collective-permute-start(bf16[128,1024]{1,0:T(8,128)(2,1)S(1)} %add.23.refs_3_), channel_id=1, source_target_pairs={{0,1},{1,0},{2,3},{3,2},{4,5},{5,4},{6,7},{7,6},{8,9},{9,8},{10,11... | collective-permute-start | bytes 786440 | tf_op jit(solution)/shard_map/ppermute | solution.py:309
  23.8 1.0 %copy-start.1 = (f32[8,16,1024]{2,1,0:T(8,128)S(1)}, f32[8,16,1024]{2,1,0:T(8,128)}, u32[]{:S(2)}) copy-start(f32[8,16,1024]{2,1,0:T(8,128)} %copy-done) | copy-start | bytes 1572868
  25.9 11.1 %collective-permute-start.5 = (bf16[128,1024]{1,0:T(8,128)(2,1)S(1)}, bf16[128,1024]{1,0:T(8,128)(2,1)S(1)}, u32[]{:S(2)}, u32[]{:S(2)}) collective-permute-start(bf16[128,1024]{1,0:T(8,128)(2,1)S(1)} %add.21.refs_3_), channel_id=1, source_target_pairs={{0,2},{1,3},{2,4},{3,5},{4,6},{5,7},{6,0},{7,1},{8,10},{9,11},{10,... | collective-permute-start | bytes 786440 | tf_op jit(solution)/shard_map/ppermute | solution.py:310
  27.5 9.4 %collective-permute-start.7 = (bf16[128,1024]{1,0:T(8,128)(2,1)S(1)}, bf16[128,1024]{1,0:T(8,128)(2,1)S(1)}, u32[]{:S(2)}, u32[]{:S(2)}) collective-permute-start(bf16[128,1024]{1,0:T(8,128)(2,1)S(1)} %add.21.refs_3_), channel_id=1, source_target_pairs={{0,1},{1,0},{2,3},{3,2},{4,5},{5,4},{6,7},{7,6},{8,9},{9,8},{10,11... | collective-permute-start | bytes 786440 | tf_op jit(solution)/shard_map/ppermute | solution.py:310
  29.1 13.4 %collective-permute-start.13 = (bf16[128,1024]{1,0:T(8,128)(2,1)S(1)}, bf16[128,1024]{1,0:T(8,128)(2,1)S(1)}, u32[]{:S(2)}, u32[]{:S(2)}) collective-permute-start(bf16[128,1024]{1,0:T(8,128)(2,1)S(1)} %collective-permute-done.10.refs_2_.refs_3_), channel_id=1, source_target_pairs={{0,2},{1,3},{2,4},{3,5},{4,6},{5,7},{6,0},{7,1},{8,10},{9,11},{10,... | collective-permute-start | bytes 786440 | tf_op jit(solution)/shard_map/ppermute | solution.py:311
  32.0 10.6 %collective-permute-start.14 = (bf16[128,1024]{1,0:T(8,128)(2,1)S(1)}, bf16[128,1024]{1,0:T(8,128)(2,1)S(1)}, u32[]{:S(2)}, u32[]{:S(2)}) collective-permute-start(bf16[128,1024]{1,0:T(8,128)(2,1)S(1)} %get-tuple-element.50), channel_id=1, source_target_pairs={{0,1},{1,0},{2,3},{3,2},{4,5},{5,4},{6,7},{7,6},{8,9},{9,8},{10,11... | collective-permute-start | bytes 786440 | tf_op jit(solution)/shard_map/ppermute | solution.py:313
  36.9 11.2 %collective-permute-start.6 = (bf16[128,1024]{1,0:T(8,128)(2,1)S(1)}, bf16[128,1024]{1,0:T(8,128)(2,1)S(1)}, u32[]{:S(2)}, u32[]{:S(2)}) collective-permute-start(bf16[128,1024]{1,0:T(8,128)(2,1)S(1)} %collective-permute-done.5.refs_2_.refs_4_), channel_id=1, source_target_pairs={{0,2},{1,3},{2,4},{3,5},{4,6},{5,7},{6,0},{7,1},{8,10},{9,11},{10,... | collective-permute-start | bytes 786440 | tf_op jit(solution)/shard_map/ppermute | solution.py:314
  38.8 9.4 %collective-permute-start.12 = (bf16[128,1024]{1,0:T(8,128)(2,1)S(1)}, bf16[128,1024]{1,0:T(8,128)(2,1)S(1)}, u32[]{:S(2)}, u32[]{:S(2)}) collective-permute-start(bf16[128,1024]{1,0:T(8,128)(2,1)S(1)} %get-tuple-element.49), channel_id=1, source_target_pairs={{0,1},{1,0},{2,3},{3,2},{4,5},{5,4},{6,7},{7,6},{8,9},{9,8},{10,11... | collective-permute-start | bytes 786440 | tf_op jit(solution)/shard_map/ppermute | solution.py:316
  42.6 11.2 %collective-permute-start.16 = (bf16[128,1024]{1,0:T(8,128)(2,1)S(1)}, bf16[128,1024]{1,0:T(8,128)(2,1)S(1)}, u32[]{:S(2)}, u32[]{:S(2)}) collective-permute-start(bf16[128,1024]{1,0:T(8,128)(2,1)S(1)} %collective-permute-done.13.refs_2_.refs_3_), channel_id=1, source_target_pairs={{0,2},{1,3},{2,4},{3,5},{4,6},{5,7},{6,0},{7,1},{8,10},{9,11},{10,... | collective-permute-start | bytes 786440 | tf_op jit(solution)/shard_map/ppermute | solution.py:317
  44.4 9.4 %collective-permute-start.17 = (bf16[128,1024]{1,0:T(8,128)(2,1)S(1)}, bf16[128,1024]{1,0:T(8,128)(2,1)S(1)}, u32[]{:S(2)}, u32[]{:S(2)}) collective-permute-start(bf16[128,1024]{1,0:T(8,128)(2,1)S(1)} %get-tuple-element.56), channel_id=1, source_target_pairs={{0,1},{1,0},{2,3},{3,2},{4,5},{5,4},{6,7},{7,6},{8,9},{9,8},{10,11... | collective-permute-start | bytes 786440 | tf_op jit(solution)/shard_map/ppermute | solution.py:319
  48.2 11.3 %collective-permute-start.19 = (bf16[128,1024]{1,0:T(8,128)(2,1)S(1)}, bf16[128,1024]{1,0:T(8,128)(2,1)S(1)}, u32[]{:S(2)}, u32[]{:S(2)}) collective-permute-start(bf16[128,1024]{1,0:T(8,128)(2,1)S(1)} %collective-permute-done.6.refs_2_), channel_id=1, source_target_pairs={{0,2},{1,3},{2,4},{3,5},{4,6},{5,7},{6,0},{7,1},{8,10},{9,11},{10,... | collective-permute-start | bytes 786440 | tf_op jit(solution)/shard_map/ppermute | solution.py:320
  50.1 9.4 %collective-permute-start.20 = (bf16[128,1024]{1,0:T(8,128)(2,1)S(1)}, bf16[128,1024]{1,0:T(8,128)(2,1)S(1)}, u32[]{:S(2)}, u32[]{:S(2)}) collective-permute-start(bf16[128,1024]{1,0:T(8,128)(2,1)S(1)} %get-tuple-element.60), channel_id=1, source_target_pairs={{0,1},{1,0},{2,3},{3,2},{4,5},{5,4},{6,7},{7,6},{8,9},{9,8},{10,11... | collective-permute-start | bytes 786440 | tf_op jit(solution)/shard_map/ppermute | solution.py:322
  55.7 7.5 %collective-permute-start.18 = (bf16[128,1024]{1,0:T(8,128)(2,1)S(1)}, bf16[128,1024]{1,0:T(8,128)(2,1)S(1)}, u32[]{:S(2)}, u32[]{:S(2)}) collective-permute-start(bf16[128,1024]{1,0:T(8,128)(2,1)S(1)} %get-tuple-element.59), channel_id=1, source_target_pairs={{0,1},{1,0},{2,3},{3,2},{4,5},{5,4},{6,7},{7,6},{8,9},{9,8},{10,11... | collective-permute-start | bytes 786440 | tf_op jit(solution)/shard_map/ppermute | solution.py:325
  57.3 7.5 %collective-permute-start.15 = (bf16[128,1024]{1,0:T(8,128)(2,1)S(1)}, bf16[128,1024]{1,0:T(8,128)(2,1)S(1)}, u32[]{:S(2)}, u32[]{:S(2)}) collective-permute-start(bf16[128,1024]{1,0:T(8,128)(2,1)S(1)} %get-tuple-element.55), channel_id=1, source_target_pairs={{2,0},{3,1},{4,2},{5,3},{6,4},{7,5},{0,6},{1,7},{10,8},{11,9},{12,... | collective-permute-start | bytes 786440 | tf_op jit(solution)/shard_map/ppermute | solution.py:323

commit v4 on v3

--- a/solution.py
+++ b/solution.py
@@ -190,24 +190,39 @@
     )(me, row_blocks, *[vmem(occ) for occ in occs], vmem(turned))
 
 
-def add_kernel(k, own_ref, core_ref, *refs):
-    out_ref = refs[-1]
-    total = own_ref[...] + core_ref[k].astype(jnp.float32)
-    for ref in refs[:-1]:
-        total += ref[...].astype(jnp.float32)
+def meet_kernel(here_ref, far_ref, core_ref, sum_ref, send_ref):
+    sum_ref[...] = here_ref[...] + core_ref[0].astype(jnp.float32)
+    send_ref[...] = (far_ref[...] + core_ref[1].astype(jnp.float32)).astype(jnp.bfloat16)
+
+
+def meet(here, far, core):
+    return pl.pallas_call(
+        meet_kernel,
+        in_specs=[IN_VMEM] * 3,
+        out_specs=[IN_VMEM] * 2,
+        out_shape=[pltpu.VMEM(here.shape, jnp.float32), pltpu.VMEM(here.shape, jnp.bfloat16)],
+        compiler_params=params(),
+        cost_estimate=pl.CostEstimate(flops=2 * here.size, bytes_accessed=8 * here.size, transcendentals=0),
+        name="meet",
+    )(*map(vmem, (here, far, core)))
+
+
+def finish_kernel(sum_ref, chip_ref, out_ref):
+    total = sum_ref[...] + chip_ref[...].astype(jnp.float32)
     out_ref[...] = total.astype(jnp.bfloat16).reshape(out_ref.shape)
 
 
-def add(own, core, k, others, shape):
-    return pl.pallas_call(
-        functools.partial(add_kernel, k),
-        in_specs=[IN_VMEM] * (2 + len(others)),
+def finish(total, chip):
+    count, share, nu = total.shape
+    return pl.pallas_call(
+        finish_kernel,
+        in_specs=[IN_VMEM] * 2,
         out_specs=IN_VMEM,
-        out_shape=pltpu.VMEM(shape, jnp.bfloat16),
-        compiler_params=params(),
-        cost_estimate=pl.CostEstimate(flops=2 * own.size, bytes_accessed=8 * own.size, transcendentals=0),
-        name="add",
-    )(*[vmem(value) for value in (own, core, *others)])
+        out_shape=pltpu.VMEM((count * share, nu), jnp.bfloat16),
+        compiler_params=params(),
+        cost_estimate=pl.CostEstimate(flops=2 * total.size, bytes_accessed=8 * total.size, transcendentals=0),
+        name="finish",
+    )(vmem(total), vmem(chip))
 
 
 def work_kernel(moved, made, n_copy, n_after, last, *refs):
@@ -288,10 +303,8 @@
     held = []
     for k in range(2):
         here, far, send = half_terms(me, row_blocks, occs, turned)
-        got = lax.ppermute(send, "basis", CORE_SWAP)
-        to_x = add(far, got, 1, [], far.shape)
-        from_x = lax.ppermute(to_x, "basis", X_SWAP)
-        held.append(add(here, got, 0, [from_x], (counts[k] * share, nu)))
+        total, to_x = meet(here, far, lax.ppermute(send, "basis", CORE_SWAP))
+        held.append(finish(total, lax.ppermute(to_x, "basis", X_SWAP)))
         if k == 0:
             turned = next_order(masked, starts[1], counts[1], mu_dev)
 

time: 66.7 us -> 65.6 us (0.984)
  local copies, waits for them, and re-layouts: 1.05 us -> 0.01 us
    unnamed x6 -> x2, local copies, waits for them, and re-layouts: 1.05 us -> 0.01 us
  transfers between devices with their start and end apart: 21 -> 21, of which waited for: 8 -> 7; matrix products, arithmetic and copies ran while one was open for 0% -> 0% of each run, Pallas kernels for 31% -> 31%
where the time goes in v4:
time: 65.6 us; the launch traced here: 65.5 us
  starting transfers between devices  24.2 us (37%)
  Pallas kernels  22.9 us (35%)
  waiting for transfers between devices  18.1 us (28%)
    pallas_call x9, Pallas kernels, work(): pl.pallas_call(functools.partial(work_kernel, moved, made, len(sent), len...  15.8 us
    ppermute x2, waiting for transfers between devices, shards_blocked(): held.append(finish(total, lax.ppermute(to_x, 'basis', X_SWAP)))  7.1 us
    ppermute x2, waiting for transfers between devices, shards_blocked(): b1, b0_y = (up(b0), swap(b0))  4.37 us
    ppermute x2, starting transfers between devices, shards_blocked(): a1, a0_y = (up(a0), swap(a0))  3.4 us
    ppermute x2, starting transfers between devices, shards_blocked(): b1, b0_y = (up(b0), swap(b0))  3.15 us
    ppermute x2, starting transfers between devices, shards_blocked(): held.append(finish(total, lax.ppermute(to_x, 'basis', X_SWAP)))  3.15 us
    ppermute x3, starting transfers between devices, shards_blocked(): lax.ppermute(occ, 'basis', swap)  3.13 us
    pallas_call x1, Pallas kernels, first_order(): pl.pallas_call(first_kernel, in_specs=[IN_SMEM] + [IN_ANY] * 4, out_specs...  2.92 us
  transfers between devices with their start and end apart: 21, of which 7 were waited for; matrix products, arithmetic and copies ran while one was open for 0% of the time, Pallas kernels for 31%

profile of v4, /device:TPU:0, one launch (start us, length us, event | category | flops | bytes accessed | tf_op | source)
XLA Modules:
  0.0 65.5 jit_solution(7369791491018786138)
XLA Ops:
  0.0 2.9 %collective-permute-start = (bf16[64,128]{1,0:T(8,128)(2,1)}, bf16[64,128]{1,0:T(8,128)(2,1)S(1)}, u32[]{:S(2)}, u32[]{:S(2)}) collective-permute-start(bf16[64,128]{1,0:T(8,128)(2,1)} %bitcast.5), channel_id=1, source_target_pairs={{0,16},{16,0},{8,24},{24,8},{1,17},{17,1},{9,25},{25,9},{2,18},{18... | collective-permute-start | bytes 49160 | tf_op jit(solution)/shard_map/ppermute | solution.py:300
  3.1 2.9 %order.2 = (bf16[8,128,1024]{2,1,0:T(8,128)(2,1)S(1)}, s32[32]{0:T(128)S(4)}, bf16[1024,1024]{1,0:T(8,128)(2,1)S(1)}, bf16[2048,1024]{1,0:T(8,128)(2,1)S(1)}) custom-call(s32[1]{0:T(128)} %bitcast.1.me.me_ref, s32[32]{0:T(128)} %row_blocks_hbm.1, s32[32,64]{1,0:T(8,128)} %mask_hbm.1, bf16[2048,1024]{1,0:T(8,128)(2,1)} %bitcast.10, bf16[1024,1024]{1,0:T(8,128)(2,1)} %vir_hbm.1), custom_call_target="tpu_custom_call" | custom-call | flops 536870912 | bytes 8388608 | tf_op jit(solution)/shard_map/order/pallas_call | solution.py:94
  8.4 0.8 %half.2 = (f32[8,16,1024]{2,1,0:T(8,128)S(1)}, f32[8,16,1024]{2,1,0:T(8,128)S(1)}, bf16[2,8,16,1024]{3,2,1,0:T(8,128)(2,1)S(1)}) custom-call(s32[1]{0:T(128)} %bitcast.1.me.me_ref, s32[32]{0:T(128)S(4)} %get-tuple-element.42.row_blocks, bf16[64,128]{1,0:T(8,128)(2,1)S(1)} %bitcast.9, bf16[64,128]{1,0:T(8,128)(2,1)S(1)} %collective-permute-done.far_occ, ...), custom_call_target="tpu_custom_call" | custom-call | flops 268435456 | bytes 3670016 | tf_op jit(solution)/shard_map/half/pallas_call | solution.py:176
  9.4 1.8 %collective-permute-start.9 = (bf16[8,16,1024]{2,1,0:T(8,128)(2,1)S(1)}, bf16[8,16,1024]{2,1,0:T(8,128)(2,1)S(1)}, u32[]{:S(2)}, u32[]{:S(2)}) collective-permute-start(bf16[8,16,1024]{2,1,0:T(8,128)(2,1)S(1)} %get-tuple-element.54), channel_id=1, source_target_pairs={{0,16},{16,0},{8,24},{24,8},{1,17},{17,1},{9,25},{25,9},{2,18},{18... | collective-permute-start | bytes 786440 | tf_op jit(solution)/shard_map/ppermute | solution.py:307
  11.2 0.8 %meet.2 = (f32[8,16,1024]{2,1,0:T(8,128)S(1)}, bf16[8,16,1024]{2,1,0:T(8,128)(2,1)}) custom-call(f32[8,16,1024]{2,1,0:T(8,128)S(1)} %get-tuple-element.44.here_ref, f32[8,16,1024]{2,1,0:T(8,128)S(1)} %get-tuple-element.45.far_ref, bf16[2,8,16,1024]{3,2,1,0:T(8,128)(2,1)S(1)} %collective-permute-done.3.core_ref), custom_call_target="tpu_custom_call" | custom-call | flops 262144 | bytes 1048576 | tf_op jit(solution)/shard_map/meet/pallas_call | solution.py:199
  11.9 1.4 %collective-permute-start.4 = (bf16[8,16,1024]{2,1,0:T(8,128)(2,1)}, bf16[8,16,1024]{2,1,0:T(8,128)(2,1)}, u32[]{:S(2)}, u32[]{:S(2)}) collective-permute-start(bf16[8,16,1024]{2,1,0:T(8,128)(2,1)} %get-tuple-element.48), channel_id=1, source_target_pairs={{0,16},{16,0},{8,24},{24,8},{1,17},{17,1},{9,25},{25,9},{2,18},{18... | collective-permute-start | bytes 786440 | tf_op jit(solution)/shard_map/ppermute | solution.py:307
  13.3 5.2 %collective-permute-done.9.chip_ref = bf16[8,16,1024]{2,1,0:T(8,128)(2,1)S(1)} collective-permute-done((bf16[8,16,1024]{2,1,0:T(8,128)(2,1)S(1)}, bf16[8,16,1024]{2,1,0:T(8,128)(2,1)S(1)}, u32[]{:S(2)}, u32[]{:S(2)}) %collective-permute-start.9) | collective-permute-done | bytes 262176 | tf_op jit(solution)/shard_map/ppermute | solution.py:307
  18.6 1.9 %collective-permute-start.10 = (bf16[128,1024]{1,0:T(8,128)(2,1)S(1)}, bf16[128,1024]{1,0:T(8,128)(2,1)S(1)}, u32[]{:S(2)}, u32[]{:S(2)}) collective-permute-start(bf16[128,1024]{1,0:T(8,128)(2,1)S(1)} %finish.3.refs_3_), channel_id=1, source_target_pairs={{0,2},{1,3},{2,4},{3,5},{4,6},{5,7},{6,0},{7,1},{8,10},{9,11},{10,... | collective-permute-start | bytes 786440 | tf_op jit(solution)/shard_map/ppermute | solution.py:322
  20.5 1.5 %collective-permute-start.11 = (bf16[128,1024]{1,0:T(8,128)(2,1)S(1)}, bf16[128,1024]{1,0:T(8,128)(2,1)S(1)}, u32[]{:S(2)}, u32[]{:S(2)}) collective-permute-start(bf16[128,1024]{1,0:T(8,128)(2,1)S(1)} %finish.3.refs_3_), channel_id=1, source_target_pairs={{0,1},{1,0},{2,3},{3,2},{4,5},{5,4},{6,7},{7,6},{8,9},{9,8},{10,11... | collective-permute-start | bytes 786440 | tf_op jit(solution)/shard_map/ppermute | solution.py:322
  22.0 1.9 %collective-permute-done.4.chip_ref = bf16[8,16,1024]{2,1,0:T(8,128)(2,1)} collective-permute-done((bf16[8,16,1024]{2,1,0:T(8,128)(2,1)}, bf16[8,16,1024]{2,1,0:T(8,128)(2,1)}, u32[]{:S(2)}, u32[]{:S(2)}) %collective-permute-start.4) | collective-permute-done | bytes 262176 | tf_op jit(solution)/shard_map/ppermute | solution.py:307
  23.9 1.0 %finish.2.refs_3_ = bf16[128,1024]{1,0:T(8,128)(2,1)S(1)} custom-call(f32[8,16,1024]{2,1,0:T(8,128)S(1)} %get-tuple-element.47.sum_ref, bf16[8,16,1024]{2,1,0:T(8,128)(2,1)} %collective-permute-done.4.chip_ref), custom_call_target="tpu_custom_call" | custom-call | flops 262144 | bytes 1048576 | tf_op jit(solution)/shard_map/finish/pallas_call | solution.py:217
  24.9 1.6 %collective-permute-start.5 = (bf16[128,1024]{1,0:T(8,128)(2,1)S(1)}, bf16[128,1024]{1,0:T(8,128)(2,1)S(1)}, u32[]{:S(2)}, u32[]{:S(2)}) collective-permute-start(bf16[128,1024]{1,0:T(8,128)(2,1)S(1)} %finish.2.refs_3_), channel_id=1, source_target_pairs={{0,2},{1,3},{2,4},{3,5},{4,6},{5,7},{6,0},{7,1},{8,10},{9,11},{10,... | collective-permute-start | bytes 786440 | tf_op jit(solution)/shard_map/ppermute | solution.py:323
  26.5 1.5 %collective-permute-start.7 = (bf16[128,1024]{1,0:T(8,128)(2,1)S(1)}, bf16[128,1024]{1,0:T(8,128)(2,1)S(1)}, u32[]{:S(2)}, u32[]{:S(2)}) collective-permute-start(bf16[128,1024]{1,0:T(8,128)(2,1)S(1)} %finish.2.refs_3_), channel_id=1, source_target_pairs={{0,1},{1,0},{2,3},{3,2},{4,5},{5,4},{6,7},{7,6},{8,9},{9,8},{10,11... | collective-permute-start | bytes 786440 | tf_op jit(solution)/shard_map/ppermute | solution.py:323
  28.1 1.6 %collective-permute-start.13 = (bf16[128,1024]{1,0:T(8,128)(2,1)S(1)}, bf16[128,1024]{1,0:T(8,128)(2,1)S(1)}, u32[]{:S(2)}, u32[]{:S(2)}) collective-permute-start(bf16[128,1024]{1,0:T(8,128)(2,1)S(1)} %collective-permute-done.10.refs_2_.refs_3_), channel_id=1, source_target_pairs={{0,2},{1,3},{2,4},{3,5},{4,6},{5,7},{6,0},{7,1},{8,10},{9,11},{10,... | collective-permute-start | bytes 786440 | tf_op jit(solution)/shard_map/ppermute | solution.py:324
  29.7 1.3 %project.9 = (bf16[4,2,256,1024]{3,2,1,0:T(8,128)(2,1)}, bf16[256,1024]{1,0:T(8,128)(2,1)S(1)}, bf16[128,1024]{1,0:T(8,128)(2,1)S(1)}) custom-call(s32[5]{0:T(128)S(1)} %pad_add_fusion.refs_0_, bf16[1024,1024]{1,0:T(8,128)(2,1)S(1)} %get-tuple-element.41.refs_1_, bf16[128,1024]{1,0:T(8,128)(2,1)S(1)} %collective-permute-done.10.refs_2_.refs_3_, ...), custom_call_target="tpu_custom_call" | custom-call | flops 1000 | bytes 1000 | tf_op jit(solution)/shard_map/project/pallas_call | solution.py:275
  31.6 4.4 %collective-permute-done.5.refs_2_.refs_4_ = bf16[128,1024]{1,0:T(8,128)(2,1)S(1)} collective-permute-done((bf16[128,1024]{1,0:T(8,128)(2,1)S(1)}, bf16[128,1024]{1,0:T(8,128)(2,1)S(1)}, u32[]{:S(2)}, u32[]{:S(2)}) %collective-permute-start.5) | collective-permute-done | bytes 262176 | tf_op jit(solution)/shard_map/ppermute | solution.py:323
  35.9 1.9 %project.10 = (bf16[4,2,256,1024]{3,2,1,0:T(8,128)(2,1)}, bf16[256,1024]{1,0:T(8,128)(2,1)S(1)}, bf16[128,1024]{1,0:T(8,128)(2,1)S(1)}) custom-call(s32[5]{0:T(128)S(1)} %pad_add_fusion.refs_0_, bf16[1024,1024]{1,0:T(8,128)(2,1)S(1)} %get-tuple-element.41.refs_1_, ...), custom_call_target="tpu_custom_call", output_to_operand_aliasing={{0}: (6, {})} | custom-call | flops 1000 | bytes 1000 | tf_op jit(solution)/shard_map/project/pallas_call | solution.py:275
  37.8 1.6 %collective-permute-start.12 = (bf16[128,1024]{1,0:T(8,128)(2,1)S(1)}, bf16[128,1024]{1,0:T(8,128)(2,1)S(1)}, u32[]{:S(2)}, u32[]{:S(2)}) collective-permute-start(bf16[128,1024]{1,0:T(8,128)(2,1)S(1)} %get-tuple-element.57), channel_id=1, source_target_pairs={{0,1},{1,0},{2,3},{3,2},{4,5},{5,4},{6,7},{7,6},{8,9},{9,8},{10,11... | collective-permute-start | bytes 786440 | tf_op jit(solution)/shard_map/ppermute | solution.py:329
  39.4 2.1 %collective-permute-done.13.refs_2_.refs_3_ = bf16[128,1024]{1,0:T(8,128)(2,1)S(1)} collective-permute-done((bf16[128,1024]{1,0:T(8,128)(2,1)S(1)}, bf16[128,1024]{1,0:T(8,128)(2,1)S(1)}, u32[]{:S(2)}, u32[]{:S(2)}) %collective-permute-start.13) | collective-permute-done | bytes 262176 | tf_op jit(solution)/shard_map/ppermute | solution.py:324
  41.5 1.9 %project.11 = (bf16[4,2,256,1024]{3,2,1,0:T(8,128)(2,1)}, bf16[256,1024]{1,0:T(8,128)(2,1)S(1)}, bf16[128,1024]{1,0:T(8,128)(2,1)S(1)}) custom-call(s32[5]{0:T(128)S(1)} %pad_add_fusion.refs_0_, bf16[1024,1024]{1,0:T(8,128)(2,1)S(1)} %get-tuple-element.41.refs_1_, ...), custom_call_target="tpu_custom_call", output_to_operand_aliasing={{0}: (6, {})} | custom-call | flops 1000 | bytes 1000 | tf_op jit(solution)/shard_map/project/pallas_call | solution.py:275
  43.4 1.6 %collective-permute-start.17 = (bf16[128,1024]{1,0:T(8,128)(2,1)S(1)}, bf16[128,1024]{1,0:T(8,128)(2,1)S(1)}, u32[]{:S(2)}, u32[]{:S(2)}) collective-permute-start(bf16[128,1024]{1,0:T(8,128)(2,1)S(1)} %get-tuple-element.64), channel_id=1, source_target_pairs={{0,1},{1,0},{2,3},{3,2},{4,5},{5,4},{6,7},{7,6},{8,9},{9,8},{10,11... | collective-permute-start | bytes 786440 | tf_op jit(solution)/shard_map/ppermute | solution.py:332
  45.0 2.1 %collective-permute-done.6.refs_2_ = bf16[128,1024]{1,0:T(8,128)(2,1)S(1)} collective-permute-done((bf16[128,1024]{1,0:T(8,128)(2,1)S(1)}, bf16[128,1024]{1,0:T(8,128)(2,1)S(1)}, u32[]{:S(2)}, u32[]{:S(2)}) %collective-permute-start.6) | collective-permute-done | bytes 262176 | tf_op jit(solution)/shard_map/ppermute | solution.py:327
  47.2 1.9 %project.12 = (bf16[4,2,256,1024]{3,2,1,0:T(8,128)(2,1)}, bf16[256,1024]{1,0:T(8,128)(2,1)S(1)}, bf16[128,1024]{1,0:T(8,128)(2,1)S(1)}, bf16[128,1024]{1,0:T(8,128)(2,1)S(1)}) custom-call(s32[5]{0:T(128)S(1)} %pad_add_fusion.refs_0_, bf16[1024,1024]{1,0:T(8,128)(2,1)S(1)} %get-tuple-element.41.refs_1_, ...), custom_call_target="tpu_custom_call", output_to_operand_aliasing={{0}: (7, {})} | custom-call | flops 1000 | bytes 1000 | tf_op jit(solution)/shard_map/project/pallas_call | solution.py:275
  49.0 1.6 %collective-permute-start.20 = (bf16[128,1024]{1,0:T(8,128)(2,1)S(1)}, bf16[128,1024]{1,0:T(8,128)(2,1)S(1)}, u32[]{:S(2)}, u32[]{:S(2)}) collective-permute-start(bf16[128,1024]{1,0:T(8,128)(2,1)S(1)} %get-tuple-element.68), channel_id=1, source_target_pairs={{0,1},{1,0},{2,3},{3,2},{4,5},{5,4},{6,7},{7,6},{8,9},{9,8},{10,11... | collective-permute-start | bytes 786440 | tf_op jit(solution)/shard_map/ppermute | solution.py:335
  50.7 2.1 %collective-permute-done.16.refs_2_ = bf16[128,1024]{1,0:T(8,128)(2,1)S(1)} collective-permute-done((bf16[128,1024]{1,0:T(8,128)(2,1)S(1)}, bf16[128,1024]{1,0:T(8,128)(2,1)S(1)}, u32[]{:S(2)}, u32[]{:S(2)}) %collective-permute-start.16) | collective-permute-done | bytes 262176 | tf_op jit(solution)/shard_map/ppermute | solution.py:330
  52.8 1.9 %project.13 = (bf16[4,2,256,1024]{3,2,1,0:T(8,128)(2,1)}, bf16[256,1024]{1,0:T(8,128)(2,1)S(1)}, bf16[128,1024]{1,0:T(8,128)(2,1)S(1)}) custom-call(s32[5]{0:T(128)S(1)} %pad_add_fusion.refs_0_, bf16[1024,1024]{1,0:T(8,128)(2,1)S(1)} %get-tuple-element.41.refs_1_, ...), custom_call_target="tpu_custom_call", output_to_operand_aliasing={{0}: (6, {})} | custom-call | flops 1000 | bytes 1000 | tf_op jit(solution)/shard_map/project/pallas_call | solution.py:275
  54.6 1.6 %collective-permute-start.18 = (bf16[128,1024]{1,0:T(8,128)(2,1)S(1)}, bf16[128,1024]{1,0:T(8,128)(2,1)S(1)}, u32[]{:S(2)}, u32[]{:S(2)}) collective-permute-start(bf16[128,1024]{1,0:T(8,128)(2,1)S(1)} %get-tuple-element.67), channel_id=1, source_target_pairs={{0,1},{1,0},{2,3},{3,2},{4,5},{5,4},{6,7},{7,6},{8,9},{9,8},{10,11... | collective-permute-start | bytes 786440 | tf_op jit(solution)/shard_map/ppermute | solution.py:338
  56.3 2.1 %collective-permute-start.15 = (bf16[128,1024]{1,0:T(8,128)(2,1)S(1)}, bf16[128,1024]{1,0:T(8,128)(2,1)S(1)}, u32[]{:S(2)}, u32[]{:S(2)}) collective-permute-start(bf16[128,1024]{1,0:T(8,128)(2,1)S(1)} %get-tuple-element.63), channel_id=1, source_target_pairs={{2,0},{3,1},{4,2},{5,3},{6,4},{7,5},{0,6},{1,7},{10,8},{11,9},{12,... | collective-permute-start | bytes 786440 | tf_op jit(solution)/shard_map/ppermute | solution.py:336
  58.4 1.9 %project.14 = (bf16[4,2,256,1024]{3,2,1,0:T(8,128)(2,1)}, bf16[256,1024]{1,0:T(8,128)(2,1)S(1)}) custom-call(s32[5]{0:T(128)S(1)} %pad_add_fusion.refs_0_, bf16[1024,1024]{1,0:T(8,128)(2,1)S(1)} %get-tuple-element.41.refs_1_, bf16[128,1024]{1,0:T(8,128)(2,1)S(1)} %collective-permute-done.6.refs_2_, ...), custom_call_target="tpu_custom_call", output_to_operand_aliasing={{0}: (6, {})} | custom-call | flops 1000 | bytes 1000 | tf_op jit(solution)/shard_map/project/pallas_call | solution.py:275
  60.3 1.9 %project.15 = (bf16[4,2,256,1024]{3,2,1,0:T(8,128)(2,1)}, bf16[256,1024]{1,0:T(8,128)(2,1)S(1)}) custom-call(s32[5]{0:T(128)S(1)} %pad_add_fusion.refs_0_, bf16[1024,1024]{1,0:T(8,128)(2,1)S(1)} %get-tuple-element.41.refs_1_, bf16[128,1024]{1,0:T(8,128)(2,1)S(1)} %collective-permute-done.16.refs_2_, ...), custom_call_target="tpu_custom_call", output_to_operand_aliasing={{0}: (5, {})} | custom-call | flops 1000 | bytes 1000 | tf_op jit(solution)/shard_map/project/pallas_call | solution.py:275
  62.1 1.6 %project.16 = (bf16[4,2,256,1024]{3,2,1,0:T(8,128)(2,1)}, bf16[128,1024]{1,0:T(8,128)(2,1)S(1)}) custom-call(s32[5]{0:T(128)S(1)} %pad_add_fusion.refs_0_, bf16[1024,1024]{1,0:T(8,128)(2,1)S(1)} %get-tuple-element.41.refs_1_, bf16[128,1024]{1,0:T(8,128)(2,1)S(1)} %collective-permute-done.18.refs_2_, ...), custom_call_target="tpu_custom_call", output_to_operand_aliasing={{0}: (4, {})} | custom-call | flops 1000 | bytes 1000 | tf_op jit(solution)/shard_map/project/pallas_call | solution.py:275
  63.7 1.7 %project.17 = bf16[4,2,256,1024]{3,2,1,0:T(8,128)(2,1)} custom-call(s32[5]{0:T(128)S(1)} %pad_add_fusion.refs_0_, bf16[1024,1024]{1,0:T(8,128)(2,1)S(1)} %get-tuple-element.41.refs_1_, bf16[128,1024]{1,0:T(8,128)(2,1)S(1)} %collective-permute-done.15.refs_2_, bf16[128,1024]{1,0:T(8,128)(2,1)S(1)} %get-tuple-element.75.refs_3_, ...), custom_call_target="tpu_custom_call", output_to_operand_aliasing={{}: (4, {})} | custom-call | flops 1000 | bytes 1000 | tf_op jit(solution)/shard_map/project/pallas_call | solution.py:275
  (31 shorter events, 3.4 us)
Async XLA Ops:
  0.0 6.3 %copy-start = (bf16[128,64]{0,1:T(8,128)(2,1)S(1)}, bf16[128,64]{0,1:T(8,128)(2,1)}, u32[]{:S(2)}) copy-start(bf16[128,64]{0,1:T(8,128)(2,1)} %param.8) | copy-start | bytes 49156
  0.0 6.1 %collective-permute-start = (bf16[64,128]{1,0:T(8,128)(2,1)}, bf16[64,128]{1,0:T(8,128)(2,1)S(1)}, u32[]{:S(2)}, u32[]{:S(2)}) collective-permute-start(bf16[64,128]{1,0:T(8,128)(2,1)} %bitcast.5), channel_id=1, source_target_pairs={{0,16},{16,0},{8,24},{24,8},{1,17},{17,1},{9,25},{25,9},{2,18},{18... | collective-permute-start | bytes 49160 | tf_op jit(solution)/shard_map/ppermute | solution.py:300
  2.9 3.1 %collective-permute-start.1 = (bf16[64,128]{1,0:T(8,128)(2,1)}, bf16[64,128]{1,0:T(8,128)(2,1)S(1)}, u32[]{:S(2)}, u32[]{:S(2)}) collective-permute-start(bf16[64,128]{1,0:T(8,128)(2,1)} %bitcast.6), channel_id=1, source_target_pairs={{0,8},{8,0},{16,24},{24,16},{1,9},{9,1},{17,25},{25,17},{2,10},{10... | collective-permute-start | bytes 49160 | tf_op jit(solution)/shard_map/ppermute | solution.py:300
  2.9 3.4 %collective-permute-start.2 = (bf16[64,128]{1,0:T(8,128)(2,1)}, bf16[64,128]{1,0:T(8,128)(2,1)S(1)}, u32[]{:S(2)}, u32[]{:S(2)}) collective-permute-start(bf16[64,128]{1,0:T(8,128)(2,1)} %bitcast.7), channel_id=1, source_target_pairs={{0,24},{24,0},{8,16},{16,8},{1,25},{25,1},{9,17},{17,9},{2,26},{26... | collective-permute-start | bytes 49160 | tf_op jit(solution)/shard_map/ppermute | solution.py:300
  7.1 2.2 %collective-permute-start.8 = (bf16[2,8,16,1024]{3,2,1,0:T(8,128)(2,1)S(1)}, bf16[2,8,16,1024]{3,2,1,0:T(8,128)(2,1)S(1)}, u32[]{:S(2)}, u32[]{:S(2)}) collective-permute-start(bf16[2,8,16,1024]{3,2,1,0:T(8,128)(2,1)S(1)} %get-tuple-element.52), channel_id=1, source_target_pairs={{0,8},{8,0},{16,24},{24,16},{1,9},{9,1},{17,25},{25,17},{2,10},{10... | collective-permute-start | bytes 1572872 | tf_op jit(solution)/shard_map/ppermute | solution.py:306
  9.2 2.0 %collective-permute-start.3 = (bf16[2,8,16,1024]{3,2,1,0:T(8,128)(2,1)S(1)}, bf16[2,8,16,1024]{3,2,1,0:T(8,128)(2,1)S(1)}, u32[]{:S(2)}, u32[]{:S(2)}) collective-permute-start(bf16[2,8,16,1024]{3,2,1,0:T(8,128)(2,1)S(1)} %get-tuple-element.46), channel_id=1, source_target_pairs={{0,8},{8,0},{16,24},{24,16},{1,9},{9,1},{17,25},{25,17},{2,10},{10... | collective-permute-start | bytes 1572872 | tf_op jit(solution)/shard_map/ppermute | solution.py:306
  9.4 9.2 %collective-permute-start.9 = (bf16[8,16,1024]{2,1,0:T(8,128)(2,1)S(1)}, bf16[8,16,1024]{2,1,0:T(8,128)(2,1)S(1)}, u32[]{:S(2)}, u32[]{:S(2)}) collective-permute-start(bf16[8,16,1024]{2,1,0:T(8,128)(2,1)S(1)} %get-tuple-element.54), channel_id=1, source_target_pairs={{0,16},{16,0},{8,24},{24,8},{1,17},{17,1},{9,25},{25,9},{2,18},{18... | collective-permute-start | bytes 786440 | tf_op jit(solution)/shard_map/ppermute | solution.py:307
  11.9 11.9 %collective-permute-start.4 = (bf16[8,16,1024]{2,1,0:T(8,128)(2,1)}, bf16[8,16,1024]{2,1,0:T(8,128)(2,1)}, u32[]{:S(2)}, u32[]{:S(2)}) collective-permute-start(bf16[8,16,1024]{2,1,0:T(8,128)(2,1)} %get-tuple-element.48), channel_id=1, source_target_pairs={{0,16},{16,0},{8,24},{24,8},{1,17},{17,1},{9,25},{25,9},{2,18},{18... | collective-permute-start | bytes 786440 | tf_op jit(solution)/shard_map/ppermute | solution.py:307
  18.6 9.5 %collective-permute-start.10 = (bf16[128,1024]{1,0:T(8,128)(2,1)S(1)}, bf16[128,1024]{1,0:T(8,128)(2,1)S(1)}, u32[]{:S(2)}, u32[]{:S(2)}) collective-permute-start(bf16[128,1024]{1,0:T(8,128)(2,1)S(1)} %finish.3.refs_3_), channel_id=1, source_target_pairs={{0,2},{1,3},{2,4},{3,5},{4,6},{5,7},{6,0},{7,1},{8,10},{9,11},{10,... | collective-permute-start | bytes 786440 | tf_op jit(solution)/shard_map/ppermute | solution.py:322
  20.5 9.2 %collective-permute-start.11 = (bf16[128,1024]{1,0:T(8,128)(2,1)S(1)}, bf16[128,1024]{1,0:T(8,128)(2,1)S(1)}, u32[]{:S(2)}, u32[]{:S(2)}) collective-permute-start(bf16[128,1024]{1,0:T(8,128)(2,1)S(1)} %finish.3.refs_3_), channel_id=1, source_target_pairs={{0,1},{1,0},{2,3},{3,2},{4,5},{5,4},{6,7},{7,6},{8,9},{9,8},{10,11... | collective-permute-start | bytes 786440 | tf_op jit(solution)/shard_map/ppermute | solution.py:322
  24.9 11.1 %collective-permute-start.5 = (bf16[128,1024]{1,0:T(8,128)(2,1)S(1)}, bf16[128,1024]{1,0:T(8,128)(2,1)S(1)}, u32[]{:S(2)}, u32[]{:S(2)}) collective-permute-start(bf16[128,1024]{1,0:T(8,128)(2,1)S(1)} %finish.2.refs_3_), channel_id=1, source_target_pairs={{0,2},{1,3},{2,4},{3,5},{4,6},{5,7},{6,0},{7,1},{8,10},{9,11},{10,... | collective-permute-start | bytes 786440 | tf_op jit(solution)/shard_map/ppermute | solution.py:323
  26.5 9.4 %collective-permute-start.7 = (bf16[128,1024]{1,0:T(8,128)(2,1)S(1)}, bf16[128,1024]{1,0:T(8,128)(2,1)S(1)}, u32[]{:S(2)}, u32[]{:S(2)}) collective-permute-start(bf16[128,1024]{1,0:T(8,128)(2,1)S(1)} %finish.2.refs_3_), channel_id=1, source_target_pairs={{0,1},{1,0},{2,3},{3,2},{4,5},{5,4},{6,7},{7,6},{8,9},{9,8},{10,11... | collective-permute-start | bytes 786440 | tf_op jit(solution)/shard_map/ppermute | solution.py:323
  28.1 13.4 %collective-permute-start.13 = (bf16[128,1024]{1,0:T(8,128)(2,1)S(1)}, bf16[128,1024]{1,0:T(8,128)(2,1)S(1)}, u32[]{:S(2)}, u32[]{:S(2)}) collective-permute-start(bf16[128,1024]{1,0:T(8,128)(2,1)S(1)} %collective-permute-done.10.refs_2_.refs_3_), channel_id=1, source_target_pairs={{0,2},{1,3},{2,4},{3,5},{4,6},{5,7},{6,0},{7,1},{8,10},{9,11},{10,... | collective-permute-start | bytes 786440 | tf_op jit(solution)/shard_map/ppermute | solution.py:324
  31.0 10.6 %collective-permute-start.14 = (bf16[128,1024]{1,0:T(8,128)(2,1)S(1)}, bf16[128,1024]{1,0:T(8,128)(2,1)S(1)}, u32[]{:S(2)}, u32[]{:S(2)}) collective-permute-start(bf16[128,1024]{1,0:T(8,128)(2,1)S(1)} %get-tuple-element.58), channel_id=1, source_target_pairs={{0,1},{1,0},{2,3},{3,2},{4,5},{5,4},{6,7},{7,6},{8,9},{9,8},{10,11... | collective-permute-start | bytes 786440 | tf_op jit(solution)/shard_map/ppermute | solution.py:326
  35.9 11.2 %collective-permute-start.6 = (bf16[128,1024]{1,0:T(8,128)(2,1)S(1)}, bf16[128,1024]{1,0:T(8,128)(2,1)S(1)}, u32[]{:S(2)}, u32[]{:S(2)}) collective-permute-start(bf16[128,1024]{1,0:T(8,128)(2,1)S(1)} %collective-permute-done.5.refs_2_.refs_4_), channel_id=1, source_target_pairs={{0,2},{1,3},{2,4},{3,5},{4,6},{5,7},{6,0},{7,1},{8,10},{9,11},{10,... | collective-permute-start | bytes 786440 | tf_op jit(solution)/shard_map/ppermute | solution.py:327
  37.8 9.4 %collective-permute-start.12 = (bf16[128,1024]{1,0:T(8,128)(2,1)S(1)}, bf16[128,1024]{1,0:T(8,128)(2,1)S(1)}, u32[]{:S(2)}, u32[]{:S(2)}) collective-permute-start(bf16[128,1024]{1,0:T(8,128)(2,1)S(1)} %get-tuple-element.57), channel_id=1, source_target_pairs={{0,1},{1,0},{2,3},{3,2},{4,5},{5,4},{6,7},{7,6},{8,9},{9,8},{10,11... | collective-permute-start | bytes 786440 | tf_op jit(solution)/shard_map/ppermute | solution.py:329
  41.5 11.2 %collective-permute-start.16 = (bf16[128,1024]{1,0:T(8,128)(2,1)S(1)}, bf16[128,1024]{1,0:T(8,128)(2,1)S(1)}, u32[]{:S(2)}, u32[]{:S(2)}) collective-permute-start(bf16[128,1024]{1,0:T(8,128)(2,1)S(1)} %collective-permute-done.13.refs_2_.refs_3_), channel_id=1, source_target_pairs={{0,2},{1,3},{2,4},{3,5},{4,6},{5,7},{6,0},{7,1},{8,10},{9,11},{10,... | collective-permute-start | bytes 786440 | tf_op jit(solution)/shard_map/ppermute | solution.py:330
  43.4 9.4 %collective-permute-start.17 = (bf16[128,1024]{1,0:T(8,128)(2,1)S(1)}, bf16[128,1024]{1,0:T(8,128)(2,1)S(1)}, u32[]{:S(2)}, u32[]{:S(2)}) collective-permute-start(bf16[128,1024]{1,0:T(8,128)(2,1)S(1)} %get-tuple-element.64), channel_id=1, source_target_pairs={{0,1},{1,0},{2,3},{3,2},{4,5},{5,4},{6,7},{7,6},{8,9},{9,8},{10,11... | collective-permute-start | bytes 786440 | tf_op jit(solution)/shard_map/ppermute | solution.py:332
  47.2 11.3 %collective-permute-start.19 = (bf16[128,1024]{1,0:T(8,128)(2,1)S(1)}, bf16[128,1024]{1,0:T(8,128)(2,1)S(1)}, u32[]{:S(2)}, u32[]{:S(2)}) collective-permute-start(bf16[128,1024]{1,0:T(8,128)(2,1)S(1)} %collective-permute-done.6.refs_2_), channel_id=1, source_target_pairs={{0,2},{1,3},{2,4},{3,5},{4,6},{5,7},{6,0},{7,1},{8,10},{9,11},{10,... | collective-permute-start | bytes 786440 | tf_op jit(solution)/shard_map/ppermute | solution.py:333
  49.0 9.4 %collective-permute-start.20 = (bf16[128,1024]{1,0:T(8,128)(2,1)S(1)}, bf16[128,1024]{1,0:T(8,128)(2,1)S(1)}, u32[]{:S(2)}, u32[]{:S(2)}) collective-permute-start(bf16[128,1024]{1,0:T(8,128)(2,1)S(1)} %get-tuple-element.68), channel_id=1, source_target_pairs={{0,1},{1,0},{2,3},{3,2},{4,5},{5,4},{6,7},{7,6},{8,9},{9,8},{10,11... | collective-permute-start | bytes 786440 | tf_op jit(solution)/shard_map/ppermute | solution.py:335
  54.6 7.5 %collective-permute-start.18 = (bf16[128,1024]{1,0:T(8,128)(2,1)S(1)}, bf16[128,1024]{1,0:T(8,128)(2,1)S(1)}, u32[]{:S(2)}, u32[]{:S(2)}) collective-permute-start(bf16[128,1024]{1,0:T(8,128)(2,1)S(1)} %get-tuple-element.67), channel_id=1, source_target_pairs={{0,1},{1,0},{2,3},{3,2},{4,5},{5,4},{6,7},{7,6},{8,9},{9,8},{10,11... | collective-permute-start | bytes 786440 | tf_op jit(solution)/shard_map/ppermute | solution.py:338
  56.3 7.5 %collective-permute-start.15 = (bf16[128,1024]{1,0:T(8,128)(2,1)S(1)}, bf16[128,1024]{1,0:T(8,128)(2,1)S(1)}, u32[]{:S(2)}, u32[]{:S(2)}) collective-permute-start(bf16[128,1024]{1,0:T(8,128)(2,1)S(1)} %get-tuple-element.63), channel_id=1, source_target_pairs={{2,0},{3,1},{4,2},{5,3},{6,4},{7,5},{0,6},{1,7},{10,8},{11,9},{12,... | collective-permute-start | bytes 786440 | tf_op jit(solution)/shard_map/ppermute | solution.py:336

commit v5 on v4

--- a/solution.py
+++ b/solution.py
@@ -11,7 +11,7 @@
 GROUPS = 2
 PARTS = (8, 8)
 ZS, YS = 4, 2
-PROJ_FLOPS = 1000
+PROJ_FLOPS = 10**9
 PROJ_BYTES = 1000
 
 CORE_SWAP = [(0, 1), (1, 0), (2, 3), (3, 2)]
@@ -229,7 +229,7 @@
     refs = list(refs)
     place, vir_ref = refs[:2]
     at = 2 + n_copy
-    next_refs, h_refs = refs[2:at], refs[at : at + len(made)]
+    next_refs, h_refs = refs[2:at], refs[at : at + len(made)][::-1]
     prev_ref = refs[at + len(made)] if moved else None
     sems = refs[-1]
     copy_refs = refs[len(refs) - 1 - n_copy : -1]
@@ -257,7 +257,7 @@
     rows = jnp.concatenate([h[...] for h in h_refs], axis=0)
     buf_ref[...] = jnp.dot(rows, vir_ref[...], preferred_element_type=jnp.float32).astype(jnp.bfloat16)
     if last:
-        final = copies(buf_ref, made, 2)
+        final = copies(buf_ref, made, 4)
         for copy in final:
             copy.start()
         going += final
@@ -268,7 +268,7 @@
 def work(state, place, vir, made, hs, out_type, sent=(), after=(), last=False):
     out, buf, moved = state
     rows, nv = hs[0].shape[0], vir.shape[1]
-    inside = [vir, *sent, *hs] + ([buf] if moved else [])
+    inside = [vir, *sent, *hs[::-1]] + ([buf] if moved else [])
     ops = [place, *map(vmem, inside), *after] + ([] if out is None else [out])
     block = pltpu.VMEM((len(hs) * rows, nv), jnp.bfloat16)
     results = [] if last else [block] + [pltpu.VMEM(value.shape, value.dtype) for value in sent]
@@ -276,7 +276,7 @@
         functools.partial(work_kernel, moved, made, len(sent), len(after), last),
         in_specs=[IN_SMEM] + [IN_VMEM] * len(inside) + [IN_ANY] * (len(after) + (out is not None)),
         out_specs=[IN_ANY] + [IN_VMEM] * len(results),
-        scratch_shapes=([block] if last else []) + [pltpu.SemaphoreType.DMA((4,))],
+        scratch_shapes=([block] if last else []) + [pltpu.SemaphoreType.DMA((8,))],
         out_shape=[out_type] + results,
         input_output_aliases={} if out is None else {len(ops) - 1: 0},
         compiler_params=params(),
@@ -336,10 +336,9 @@
     b3_y = down(b0_y_copy)
     state, a3_copy = run(state, made=pair(2, row_a), hs=[a2, a2_y], sent=[a3])
     a3_y = swap(a3_copy)
-    state, = run(state, made=pair(2, row_b), hs=[b2, b2_y], after=[b3])
-    state, = run(state, made=[(3, row_a, 0), (3, row_b, 0)], hs=[a3, b3])
-    state, = run(state, made=[(3, row_a, 1)], hs=[a3_y])
-    state, = run(state, made=[(3, row_b, 1)], hs=[b3_y], last=True)
+    state, = run(state, made=pair(2, row_b) + [(3, row_a, 0)], hs=[b2, b2_y, a3], after=[b3])
+    state, = run(state, made=[(3, row_b, 0)], hs=[b3])
+    state, = run(state, made=[(3, row_a, 1), (3, row_b, 1)], hs=[a3_y, b3_y], last=True)
     return state[0].reshape(ZS * YS * fit_dev, share, nv)
 
 

time: 65.6 us -> 64.1 us (0.977)
  Pallas kernels: 22.9 us -> 21.1 us
    ppermute x1, waiting for transfers between devices: 2.11 us -> 0.01 us  [shards_blocked(): a3 = up(a2)]
    ppermute x1, starting transfers between devices: 2.15 us -> 3.82 us  [shards_blocked(): b3_y = down(b0_y_copy)]
    ppermute x1, waiting for transfers between devices: 0.01 us -> 1.44 us  [shards_blocked(): b3 = up(b2)]
    ppermute x1, starting transfers between devices: 1.61 us -> 0.56 us  [shards_blocked(): a3_y = swap(a3_copy)]
    pallas_call x2, Pallas kernels: 1.04 us -> 0.09 us  [finish(): pl.pallas_call(finish_kernel, in_specs=[IN_VMEM] * 2, out_specs=IN_VMEM,...]
    ppermute x2, waiting for transfers between devices: 0.01 us -> 0.93 us  [shards_blocked(): a1, a0_y = (up(a0), swap(a0))]
    ppermute x1, starting transfers between devices: 1.57 us -> 0.64 us  [shards_blocked(): a2 = up(a1)]
    pallas_call x9 -> x8, Pallas kernels: 15.8 us -> 15 us  [work(): pl.pallas_call(functools.partial(work_kernel, moved, made, len(sent), len...]
  transfers between devices with their start and end apart: 21 -> 21, of which waited for: 7 -> 10; matrix products, arithmetic and copies ran while one was open for 0% -> 0% of each run, Pallas kernels for 31% -> 29%
where the time goes in v5:
time: 64.1 us; the launch traced here: 63.9 us
  starting transfers between devices  24.1 us (38%)
  Pallas kernels  21.1 us (33%)
  waiting for transfers between devices  18.5 us (29%)
    pallas_call x8, Pallas kernels, work(): pl.pallas_call(functools.partial(work_kernel, moved, made, len(sent), len...  15 us
    ppermute x2, waiting for transfers between devices, shards_blocked(): held.append(finish(total, lax.ppermute(to_x, 'basis', X_SWAP)))  6.99 us
    ppermute x1, starting transfers between devices, shards_blocked(): b3_y = down(b0_y_copy)  3.82 us
    ppermute x2, waiting for transfers between devices, shards_blocked(): b1, b0_y = (up(b0), swap(b0))  3.73 us
    ppermute x2, starting transfers between devices, shards_blocked(): a1, a0_y = (up(a0), swap(a0))  3.4 us
    ppermute x2, starting transfers between devices, shards_blocked(): b1, b0_y = (up(b0), swap(b0))  3.15 us
    ppermute x2, starting transfers between devices, shards_blocked(): held.append(finish(total, lax.ppermute(to_x, 'basis', X_SWAP)))  3.15 us
    ppermute x3, starting transfers between devices, shards_blocked(): lax.ppermute(occ, 'basis', swap)  3.13 us
  transfers between devices with their start and end apart: 21, of which 10 were waited for; matrix products, arithmetic and copies ran while one was open for 0% of the time, Pallas kernels for 29%

profile of v5, /device:TPU:0, one launch (start us, length us, event | category | flops | bytes accessed | tf_op | source)
XLA Modules:
  0.0 63.9 jit_solution(14472615214449484155)
XLA Ops:
  0.0 2.9 %collective-permute-start = (bf16[64,128]{1,0:T(8,128)(2,1)}, bf16[64,128]{1,0:T(8,128)(2,1)S(1)}, u32[]{:S(2)}, u32[]{:S(2)}) collective-permute-start(bf16[64,128]{1,0:T(8,128)(2,1)} %bitcast.5), channel_id=1, source_target_pairs={{0,16},{16,0},{8,24},{24,8},{1,17},{17,1},{9,25},{25,9},{2,18},{18... | collective-permute-start | bytes 49160 | tf_op jit(solution)/shard_map/ppermute | solution.py:300
  3.1 2.9 %order.2 = (bf16[8,128,1024]{2,1,0:T(8,128)(2,1)S(1)}, s32[32]{0:T(128)S(4)}, bf16[1024,1024]{1,0:T(8,128)(2,1)S(1)}, bf16[2048,1024]{1,0:T(8,128)(2,1)S(1)}) custom-call(s32[1]{0:T(128)} %bitcast.1.me.me_ref, s32[32]{0:T(128)} %row_blocks_hbm.1, s32[32,64]{1,0:T(8,128)} %mask_hbm.1, bf16[2048,1024]{1,0:T(8,128)(2,1)} %bitcast.10, bf16[1024,1024]{1,0:T(8,128)(2,1)} %vir_hbm.1), custom_call_target="tpu_custom_call" | custom-call | flops 536870912 | bytes 8388608 | tf_op jit(solution)/shard_map/order/pallas_call | solution.py:94
  6.3 0.8 %half.3 = (f32[8,16,1024]{2,1,0:T(8,128)S(1)}, f32[8,16,1024]{2,1,0:T(8,128)S(1)}, bf16[2,8,16,1024]{3,2,1,0:T(8,128)(2,1)S(1)}) custom-call(s32[1]{0:T(128)} %bitcast.1.me.me_ref, s32[32]{0:T(128)S(4)} %get-tuple-element.40.row_blocks, bf16[64,128]{1,0:T(8,128)(2,1)S(1)} %bitcast.8, bf16[64,128]{1,0:T(8,128)(2,1)S(1)} %collective-permute-done.far_occ, ...), custom_call_target="tpu_custom_call" | custom-call | flops 268435456 | bytes 3670016 | tf_op jit(solution)/shard_map/half/pallas_call | solution.py:176
  8.4 0.8 %half.2 = (f32[8,16,1024]{2,1,0:T(8,128)S(1)}, f32[8,16,1024]{2,1,0:T(8,128)S(1)}, bf16[2,8,16,1024]{3,2,1,0:T(8,128)(2,1)S(1)}) custom-call(s32[1]{0:T(128)} %bitcast.1.me.me_ref, s32[32]{0:T(128)S(4)} %get-tuple-element.40.row_blocks, bf16[64,128]{1,0:T(8,128)(2,1)S(1)} %bitcast.9, bf16[64,128]{1,0:T(8,128)(2,1)S(1)} %collective-permute-done.far_occ, ...), custom_call_target="tpu_custom_call" | custom-call | flops 268435456 | bytes 3670016 | tf_op jit(solution)/shard_map/half/pallas_call | solution.py:176
  9.4 1.8 %collective-permute-start.9 = (bf16[8,16,1024]{2,1,0:T(8,128)(2,1)S(1)}, bf16[8,16,1024]{2,1,0:T(8,128)(2,1)S(1)}, u32[]{:S(2)}, u32[]{:S(2)}) collective-permute-start(bf16[8,16,1024]{2,1,0:T(8,128)(2,1)S(1)} %get-tuple-element.52), channel_id=1, source_target_pairs={{0,16},{16,0},{8,24},{24,8},{1,17},{17,1},{9,25},{25,9},{2,18},{18... | collective-permute-start | bytes 786440 | tf_op jit(solution)/shard_map/ppermute | solution.py:307
  11.2 0.8 %meet.2 = (f32[8,16,1024]{2,1,0:T(8,128)S(1)}, bf16[8,16,1024]{2,1,0:T(8,128)(2,1)}) custom-call(f32[8,16,1024]{2,1,0:T(8,128)S(1)} %get-tuple-element.42.here_ref, f32[8,16,1024]{2,1,0:T(8,128)S(1)} %get-tuple-element.43.far_ref, bf16[2,8,16,1024]{3,2,1,0:T(8,128)(2,1)S(1)} %collective-permute-done.3.core_ref), custom_call_target="tpu_custom_call" | custom-call | flops 262144 | bytes 1048576 | tf_op jit(solution)/shard_map/meet/pallas_call | solution.py:199
  11.9 1.4 %collective-permute-start.4 = (bf16[8,16,1024]{2,1,0:T(8,128)(2,1)}, bf16[8,16,1024]{2,1,0:T(8,128)(2,1)S(1)}, u32[]{:S(2)}, u32[]{:S(2)}) collective-permute-start(bf16[8,16,1024]{2,1,0:T(8,128)(2,1)} %get-tuple-element.46), channel_id=1, source_target_pairs={{0,16},{16,0},{8,24},{24,8},{1,17},{17,1},{9,25},{25,9},{2,18},{18... | collective-permute-start | bytes 786440 | tf_op jit(solution)/shard_map/ppermute | solution.py:307
  13.3 5.2 %collective-permute-done.9.chip_ref = bf16[8,16,1024]{2,1,0:T(8,128)(2,1)S(1)} collective-permute-done((bf16[8,16,1024]{2,1,0:T(8,128)(2,1)S(1)}, bf16[8,16,1024]{2,1,0:T(8,128)(2,1)S(1)}, u32[]{:S(2)}, u32[]{:S(2)}) %collective-permute-start.9) | collective-permute-done | bytes 262176 | tf_op jit(solution)/shard_map/ppermute | solution.py:307
  18.6 1.9 %collective-permute-start.10 = (bf16[128,1024]{1,0:T(8,128)(2,1)S(1)}, bf16[128,1024]{1,0:T(8,128)(2,1)S(1)}, u32[]{:S(2)}, u32[]{:S(2)}) collective-permute-start(bf16[128,1024]{1,0:T(8,128)(2,1)S(1)} %finish.3.refs_4_), channel_id=1, source_target_pairs={{0,2},{1,3},{2,4},{3,5},{4,6},{5,7},{6,0},{7,1},{8,10},{9,11},{10,... | collective-permute-start | bytes 786440 | tf_op jit(solution)/shard_map/ppermute | solution.py:322
  20.5 1.5 %collective-permute-start.11 = (bf16[128,1024]{1,0:T(8,128)(2,1)S(1)}, bf16[128,1024]{1,0:T(8,128)(2,1)}, u32[]{:S(2)}, u32[]{:S(2)}) collective-permute-start(bf16[128,1024]{1,0:T(8,128)(2,1)S(1)} %finish.3.refs_4_), channel_id=1, source_target_pairs={{0,1},{1,0},{2,3},{3,2},{4,5},{5,4},{6,7},{7,6},{8,9},{9,8},{10,11... | collective-permute-start | bytes 786440 | tf_op jit(solution)/shard_map/ppermute | solution.py:322
  22.0 1.8 %collective-permute-done.4.chip_ref = bf16[8,16,1024]{2,1,0:T(8,128)(2,1)S(1)} collective-permute-done((bf16[8,16,1024]{2,1,0:T(8,128)(2,1)}, bf16[8,16,1024]{2,1,0:T(8,128)(2,1)S(1)}, u32[]{:S(2)}, u32[]{:S(2)}) %collective-permute-start.4) | collective-permute-done | bytes 262176 | tf_op jit(solution)/shard_map/ppermute | solution.py:307
  23.8 1.6 %collective-permute-start.5 = (bf16[128,1024]{1,0:T(8,128)(2,1)S(1)}, bf16[128,1024]{1,0:T(8,128)(2,1)S(1)}, u32[]{:S(2)}, u32[]{:S(2)}) collective-permute-start(bf16[128,1024]{1,0:T(8,128)(2,1)S(1)} %finish.2.refs_4_), channel_id=1, source_target_pairs={{0,2},{1,3},{2,4},{3,5},{4,6},{5,7},{6,0},{7,1},{8,10},{9,11},{10,... | collective-permute-start | bytes 786440 | tf_op jit(solution)/shard_map/ppermute | solution.py:323
  25.4 1.5 %collective-permute-start.7 = (bf16[128,1024]{1,0:T(8,128)(2,1)S(1)}, bf16[128,1024]{1,0:T(8,128)(2,1)S(1)}, u32[]{:S(2)}, u32[]{:S(2)}) collective-permute-start(bf16[128,1024]{1,0:T(8,128)(2,1)S(1)} %finish.2.refs_4_), channel_id=1, source_target_pairs={{0,1},{1,0},{2,3},{3,2},{4,5},{5,4},{6,7},{7,6},{8,9},{9,8},{10,11... | collective-permute-start | bytes 786440 | tf_op jit(solution)/shard_map/ppermute | solution.py:323
  27.0 0.9 %collective-permute-done.10.refs_2_.refs_4_ = bf16[128,1024]{1,0:T(8,128)(2,1)S(1)} collective-permute-done((bf16[128,1024]{1,0:T(8,128)(2,1)S(1)}, bf16[128,1024]{1,0:T(8,128)(2,1)S(1)}, u32[]{:S(2)}, u32[]{:S(2)}) %collective-permute-start.10) | collective-permute-done | bytes 262176 | tf_op jit(solution)/shard_map/ppermute | solution.py:322
  28.6 1.8 %project.8 = (bf16[4,2,256,1024]{3,2,1,0:T(8,128)(2,1)}, bf16[256,1024]{1,0:T(8,128)(2,1)S(1)}, bf16[128,1024]{1,0:T(8,128)(2,1)S(1)}) custom-call(s32[5]{0:T(128)S(1)} %pad_add_fusion.refs_0_, bf16[1024,1024]{1,0:T(8,128)(2,1)S(1)} %get-tuple-element.39.refs_1_, bf16[128,1024]{1,0:T(8,128)(2,1)S(1)} %collective-permute-done.10.refs_2_.refs_4_, ...), custom_call_target="tpu_custom_call" | custom-call | flops 1000000000 | bytes 1000 | tf_op jit(solution)/shard_map/project/pallas_call | solution.py:275
  30.4 0.8 %collective-permute-start.14 = (bf16[128,1024]{1,0:T(8,128)(2,1)S(1)}, bf16[128,1024]{1,0:T(8,128)(2,1)S(1)}, u32[]{:S(2)}, u32[]{:S(2)}) collective-permute-start(bf16[128,1024]{1,0:T(8,128)(2,1)S(1)} %get-tuple-element.56), channel_id=1, source_target_pairs={{0,1},{1,0},{2,3},{3,2},{4,5},{5,4},{6,7},{7,6},{8,9},{9,8},{10,11... | collective-permute-start | bytes 786440 | tf_op jit(solution)/shard_map/ppermute | solution.py:326
  31.1 3.7 %collective-permute-done.5.refs_2_.refs_5_ = bf16[128,1024]{1,0:T(8,128)(2,1)S(1)} collective-permute-done((bf16[128,1024]{1,0:T(8,128)(2,1)S(1)}, bf16[128,1024]{1,0:T(8,128)(2,1)S(1)}, u32[]{:S(2)}, u32[]{:S(2)}) %collective-permute-start.5) | collective-permute-done | bytes 262176 | tf_op jit(solution)/shard_map/ppermute | solution.py:323
  34.9 1.9 %project.9 = (bf16[4,2,256,1024]{3,2,1,0:T(8,128)(2,1)}, bf16[256,1024]{1,0:T(8,128)(2,1)S(1)}, bf16[128,1024]{1,0:T(8,128)(2,1)S(1)}) custom-call(s32[5]{0:T(128)S(1)} %pad_add_fusion.refs_0_, bf16[1024,1024]{1,0:T(8,128)(2,1)S(1)} %get-tuple-element.39.refs_1_, ...), custom_call_target="tpu_custom_call", output_to_operand_aliasing={{0}: (6, {})} | custom-call | flops 1000000000 | bytes 1000 | tf_op jit(solution)/shard_map/project/pallas_call | solution.py:275
  36.8 1.6 %collective-permute-start.12 = (bf16[128,1024]{1,0:T(8,128)(2,1)S(1)}, bf16[128,1024]{1,0:T(8,128)(2,1)S(1)}, u32[]{:S(2)}, u32[]{:S(2)}) collective-permute-start(bf16[128,1024]{1,0:T(8,128)(2,1)S(1)} %get-tuple-element.55), channel_id=1, source_target_pairs={{0,1},{1,0},{2,3},{3,2},{4,5},{5,4},{6,7},{7,6},{8,9},{9,8},{10,11... | collective-permute-start | bytes 786440 | tf_op jit(solution)/shard_map/ppermute | solution.py:329
  38.4 2.1 %collective-permute-done.13.refs_2_.refs_4_ = bf16[128,1024]{1,0:T(8,128)(2,1)S(1)} collective-permute-done((bf16[128,1024]{1,0:T(8,128)(2,1)S(1)}, bf16[128,1024]{1,0:T(8,128)(2,1)S(1)}, u32[]{:S(2)}, u32[]{:S(2)}) %collective-permute-start.13) | collective-permute-done | bytes 262176 | tf_op jit(solution)/shard_map/ppermute | solution.py:324
  40.5 1.9 %project.10 = (bf16[4,2,256,1024]{3,2,1,0:T(8,128)(2,1)}, bf16[256,1024]{1,0:T(8,128)(2,1)S(1)}, bf16[128,1024]{1,0:T(8,128)(2,1)S(1)}) custom-call(s32[5]{0:T(128)S(1)} %pad_add_fusion.refs_0_, bf16[1024,1024]{1,0:T(8,128)(2,1)S(1)} %get-tuple-element.39.refs_1_, ...), custom_call_target="tpu_custom_call", output_to_operand_aliasing={{0}: (6, {})} | custom-call | flops 1000000000 | bytes 1000 | tf_op jit(solution)/shard_map/project/pallas_call | solution.py:275
  42.4 1.6 %collective-permute-start.17 = (bf16[128,1024]{1,0:T(8,128)(2,1)S(1)}, bf16[128,1024]{1,0:T(8,128)(2,1)S(1)}, u32[]{:S(2)}, u32[]{:S(2)}) collective-permute-start(bf16[128,1024]{1,0:T(8,128)(2,1)S(1)} %get-tuple-element.62), channel_id=1, source_target_pairs={{0,1},{1,0},{2,3},{3,2},{4,5},{5,4},{6,7},{7,6},{8,9},{9,8},{10,11... | collective-permute-start | bytes 786440 | tf_op jit(solution)/shard_map/ppermute | solution.py:332
  44.0 2.1 %collective-permute-done.6.refs_2_.refs_4_ = bf16[128,1024]{1,0:T(8,128)(2,1)S(1)} collective-permute-done((bf16[128,1024]{1,0:T(8,128)(2,1)S(1)}, bf16[128,1024]{1,0:T(8,128)(2,1)S(1)}, u32[]{:S(2)}, u32[]{:S(2)}) %collective-permute-start.6) | collective-permute-done | bytes 262176 | tf_op jit(solution)/shard_map/ppermute | solution.py:327
  46.1 1.9 %project.11 = (bf16[4,2,256,1024]{3,2,1,0:T(8,128)(2,1)}, bf16[256,1024]{1,0:T(8,128)(2,1)S(1)}, bf16[128,1024]{1,0:T(8,128)(2,1)S(1)}, bf16[128,1024]{1,0:T(8,128)(2,1)S(1)}) custom-call(s32[5]{0:T(128)S(1)} %pad_add_fusion.refs_0_, bf16[1024,1024]{1,0:T(8,128)(2,1)S(1)} %get-tuple-element.39.refs_1_, ...), custom_call_target="tpu_custom_call", output_to_operand_aliasing={{0}: (7, {})} | custom-call | flops 1000000000 | bytes 1000 | tf_op jit(solution)/shard_map/project/pallas_call | solution.py:275
  48.0 1.6 %collective-permute-start.20 = (bf16[128,1024]{1,0:T(8,128)(2,1)S(1)}, bf16[128,1024]{1,0:T(8,128)(2,1)S(1)}, u32[]{:S(2)}, u32[]{:S(2)}) collective-permute-start(bf16[128,1024]{1,0:T(8,128)(2,1)S(1)} %get-tuple-element.66), channel_id=1, source_target_pairs={{0,1},{1,0},{2,3},{3,2},{4,5},{5,4},{6,7},{7,6},{8,9},{9,8},{10,11... | collective-permute-start | bytes 786440 | tf_op jit(solution)/shard_map/ppermute | solution.py:335
  49.6 3.8 %collective-permute-start.15 = (bf16[128,1024]{1,0:T(8,128)(2,1)S(1)}, bf16[128,1024]{1,0:T(8,128)(2,1)S(1)}, u32[]{:S(2)}, u32[]{:S(2)}) collective-permute-start(bf16[128,1024]{1,0:T(8,128)(2,1)S(1)} %get-tuple-element.61), channel_id=1, source_target_pairs={{2,0},{3,1},{4,2},{5,3},{6,4},{7,5},{0,6},{1,7},{10,8},{11,9},{12,... | collective-permute-start | bytes 786440 | tf_op jit(solution)/shard_map/ppermute | solution.py:336
  53.5 1.9 %project.12 = (bf16[4,2,256,1024]{3,2,1,0:T(8,128)(2,1)}, bf16[256,1024]{1,0:T(8,128)(2,1)S(1)}, bf16[128,1024]{1,0:T(8,128)(2,1)S(1)}) custom-call(s32[5]{0:T(128)S(1)} %pad_add_fusion.refs_0_, bf16[1024,1024]{1,0:T(8,128)(2,1)S(1)} %get-tuple-element.39.refs_1_, ...), custom_call_target="tpu_custom_call", output_to_operand_aliasing={{0}: (6, {})} | custom-call | flops 1000000000 | bytes 1000 | tf_op jit(solution)/shard_map/project/pallas_call | solution.py:275
  55.9 1.4 %collective-permute-done.19.refs_6_.refs_2_ = bf16[128,1024]{1,0:T(8,128)(2,1)S(1)} collective-permute-done((bf16[128,1024]{1,0:T(8,128)(2,1)S(1)}, bf16[128,1024]{1,0:T(8,128)(2,1)S(1)}, u32[]{:S(2)}, u32[]{:S(2)}) %collective-permute-start.19) | collective-permute-done | bytes 262176 | tf_op jit(solution)/shard_map/ppermute | solution.py:333
  57.4 1.8 %project.13 = (bf16[4,2,256,1024]{3,2,1,0:T(8,128)(2,1)}, bf16[384,1024]{1,0:T(8,128)(2,1)S(1)}) custom-call(s32[5]{0:T(128)S(1)} %pad_add_fusion.refs_0_, bf16[1024,1024]{1,0:T(8,128)(2,1)S(1)} %get-tuple-element.39.refs_1_, bf16[128,1024]{1,0:T(8,128)(2,1)S(1)} %collective-permute-done.16.refs_2_, ...), custom_call_target="tpu_custom_call", output_to_operand_aliasing={{0}: (7, {})} | custom-call | flops 1000000000 | bytes 1000 | tf_op jit(solution)/shard_map/project/pallas_call | solution.py:275
  59.2 1.7 %project.14 = (bf16[4,2,256,1024]{3,2,1,0:T(8,128)(2,1)}, bf16[128,1024]{1,0:T(8,128)(2,1)S(1)}) custom-call(s32[5]{0:T(128)S(1)} %pad_add_fusion.refs_0_, bf16[1024,1024]{1,0:T(8,128)(2,1)S(1)} %get-tuple-element.39.refs_1_, bf16[128,1024]{1,0:T(8,128)(2,1)S(1)} %collective-permute-done.19.refs_6_.refs_2_, ...), custom_call_target="tpu_custom_call", output_to_operand_aliasing={{0}: (4, {})} | custom-call | flops 1000000000 | bytes 1000 | tf_op jit(solution)/shard_map/project/pallas_call | solution.py:275
  60.9 0.8 %collective-permute-done.15.refs_2_ = bf16[128,1024]{1,0:T(8,128)(2,1)S(1)} collective-permute-done((bf16[128,1024]{1,0:T(8,128)(2,1)S(1)}, bf16[128,1024]{1,0:T(8,128)(2,1)S(1)}, u32[]{:S(2)}, u32[]{:S(2)}) %collective-permute-start.15) | collective-permute-done | bytes 262176 | tf_op jit(solution)/shard_map/ppermute | solution.py:336
  61.8 2.1 %project.15 = bf16[4,2,256,1024]{3,2,1,0:T(8,128)(2,1)} custom-call(s32[5]{0:T(128)S(1)} %pad_add_fusion.refs_0_, bf16[1024,1024]{1,0:T(8,128)(2,1)S(1)} %get-tuple-element.39.refs_1_, bf16[128,1024]{1,0:T(8,128)(2,1)S(1)} %collective-permute-done.15.refs_2_, bf16[128,1024]{1,0:T(8,128)(2,1)S(1)} %collective-permute-done.18.refs_3_, ...), custom_call_target="tpu_custom_call", output_to_operand_aliasing={{}: (5, {})} | custom-call | flops 1000000000 | bytes 1000 | tf_op jit(solution)/shard_map/project/pallas_call | solution.py:275
  (30 shorter events, 3.5 us)
Async XLA Ops:
  0.0 6.3 %copy-start = (bf16[128,64]{0,1:T(8,128)(2,1)S(1)}, bf16[128,64]{0,1:T(8,128)(2,1)}, u32[]{:S(2)}) copy-start(bf16[128,64]{0,1:T(8,128)(2,1)} %param.8) | copy-start | bytes 49156
  0.0 6.1 %collective-permute-start = (bf16[64,128]{1,0:T(8,128)(2,1)}, bf16[64,128]{1,0:T(8,128)(2,1)S(1)}, u32[]{:S(2)}, u32[]{:S(2)}) collective-permute-start(bf16[64,128]{1,0:T(8,128)(2,1)} %bitcast.5), channel_id=1, source_target_pairs={{0,16},{16,0},{8,24},{24,8},{1,17},{17,1},{9,25},{25,9},{2,18},{18... | collective-permute-start | bytes 49160 | tf_op jit(solution)/shard_map/ppermute | solution.py:300
  2.9 3.1 %collective-permute-start.1 = (bf16[64,128]{1,0:T(8,128)(2,1)}, bf16[64,128]{1,0:T(8,128)(2,1)S(1)}, u32[]{:S(2)}, u32[]{:S(2)}) collective-permute-start(bf16[64,128]{1,0:T(8,128)(2,1)} %bitcast.6), channel_id=1, source_target_pairs={{0,8},{8,0},{16,24},{24,16},{1,9},{9,1},{17,25},{25,17},{2,10},{10... | collective-permute-start | bytes 49160 | tf_op jit(solution)/shard_map/ppermute | solution.py:300
  2.9 3.4 %collective-permute-start.2 = (bf16[64,128]{1,0:T(8,128)(2,1)}, bf16[64,128]{1,0:T(8,128)(2,1)S(1)}, u32[]{:S(2)}, u32[]{:S(2)}) collective-permute-start(bf16[64,128]{1,0:T(8,128)(2,1)} %bitcast.7), channel_id=1, source_target_pairs={{0,24},{24,0},{8,16},{16,8},{1,25},{25,1},{9,17},{17,9},{2,26},{26... | collective-permute-start | bytes 49160 | tf_op jit(solution)/shard_map/ppermute | solution.py:300
  7.1 2.2 %collective-permute-start.8 = (bf16[2,8,16,1024]{3,2,1,0:T(8,128)(2,1)S(1)}, bf16[2,8,16,1024]{3,2,1,0:T(8,128)(2,1)S(1)}, u32[]{:S(2)}, u32[]{:S(2)}) collective-permute-start(bf16[2,8,16,1024]{3,2,1,0:T(8,128)(2,1)S(1)} %get-tuple-element.50), channel_id=1, source_target_pairs={{0,8},{8,0},{16,24},{24,16},{1,9},{9,1},{17,25},{25,17},{2,10},{10... | collective-permute-start | bytes 1572872 | tf_op jit(solution)/shard_map/ppermute | solution.py:306
  9.2 2.0 %collective-permute-start.3 = (bf16[2,8,16,1024]{3,2,1,0:T(8,128)(2,1)S(1)}, bf16[2,8,16,1024]{3,2,1,0:T(8,128)(2,1)S(1)}, u32[]{:S(2)}, u32[]{:S(2)}) collective-permute-start(bf16[2,8,16,1024]{3,2,1,0:T(8,128)(2,1)S(1)} %get-tuple-element.44), channel_id=1, source_target_pairs={{0,8},{8,0},{16,24},{24,16},{1,9},{9,1},{17,25},{25,17},{2,10},{10... | collective-permute-start | bytes 1572872 | tf_op jit(solution)/shard_map/ppermute | solution.py:306
  9.4 9.2 %collective-permute-start.9 = (bf16[8,16,1024]{2,1,0:T(8,128)(2,1)S(1)}, bf16[8,16,1024]{2,1,0:T(8,128)(2,1)S(1)}, u32[]{:S(2)}, u32[]{:S(2)}) collective-permute-start(bf16[8,16,1024]{2,1,0:T(8,128)(2,1)S(1)} %get-tuple-element.52), channel_id=1, source_target_pairs={{0,16},{16,0},{8,24},{24,8},{1,17},{17,1},{9,25},{25,9},{2,18},{18... | collective-permute-start | bytes 786440 | tf_op jit(solution)/shard_map/ppermute | solution.py:307
  11.9 11.8 %collective-permute-start.4 = (bf16[8,16,1024]{2,1,0:T(8,128)(2,1)}, bf16[8,16,1024]{2,1,0:T(8,128)(2,1)S(1)}, u32[]{:S(2)}, u32[]{:S(2)}) collective-permute-start(bf16[8,16,1024]{2,1,0:T(8,128)(2,1)} %get-tuple-element.46), channel_id=1, source_target_pairs={{0,16},{16,0},{8,24},{24,8},{1,17},{17,1},{9,25},{25,9},{2,18},{18... | collective-permute-start | bytes 786440 | tf_op jit(solution)/shard_map/ppermute | solution.py:307
  18.6 9.4 %collective-permute-start.10 = (bf16[128,1024]{1,0:T(8,128)(2,1)S(1)}, bf16[128,1024]{1,0:T(8,128)(2,1)S(1)}, u32[]{:S(2)}, u32[]{:S(2)}) collective-permute-start(bf16[128,1024]{1,0:T(8,128)(2,1)S(1)} %finish.3.refs_4_), channel_id=1, source_target_pairs={{0,2},{1,3},{2,4},{3,5},{4,6},{5,7},{6,0},{7,1},{8,10},{9,11},{10,... | collective-permute-start | bytes 786440 | tf_op jit(solution)/shard_map/ppermute | solution.py:322
  20.5 8.1 %collective-permute-start.11 = (bf16[128,1024]{1,0:T(8,128)(2,1)S(1)}, bf16[128,1024]{1,0:T(8,128)(2,1)}, u32[]{:S(2)}, u32[]{:S(2)}) collective-permute-start(bf16[128,1024]{1,0:T(8,128)(2,1)S(1)} %finish.3.refs_4_), channel_id=1, source_target_pairs={{0,1},{1,0},{2,3},{3,2},{4,5},{5,4},{6,7},{7,6},{8,9},{9,8},{10,11... | collective-permute-start | bytes 786440 | tf_op jit(solution)/shard_map/ppermute | solution.py:322
  23.8 11.1 %collective-permute-start.5 = (bf16[128,1024]{1,0:T(8,128)(2,1)S(1)}, bf16[128,1024]{1,0:T(8,128)(2,1)S(1)}, u32[]{:S(2)}, u32[]{:S(2)}) collective-permute-start(bf16[128,1024]{1,0:T(8,128)(2,1)S(1)} %finish.2.refs_4_), channel_id=1, source_target_pairs={{0,2},{1,3},{2,4},{3,5},{4,6},{5,7},{6,0},{7,1},{8,10},{9,11},{10,... | collective-permute-start | bytes 786440 | tf_op jit(solution)/shard_map/ppermute | solution.py:323
  25.4 9.4 %collective-permute-start.7 = (bf16[128,1024]{1,0:T(8,128)(2,1)S(1)}, bf16[128,1024]{1,0:T(8,128)(2,1)S(1)}, u32[]{:S(2)}, u32[]{:S(2)}) collective-permute-start(bf16[128,1024]{1,0:T(8,128)(2,1)S(1)} %finish.2.refs_4_), channel_id=1, source_target_pairs={{0,1},{1,0},{2,3},{3,2},{4,5},{5,4},{6,7},{7,6},{8,9},{9,8},{10,11... | collective-permute-start | bytes 786440 | tf_op jit(solution)/shard_map/ppermute | solution.py:323
  28.0 12.5 %collective-permute-start.13 = (bf16[128,1024]{1,0:T(8,128)(2,1)S(1)}, bf16[128,1024]{1,0:T(8,128)(2,1)S(1)}, u32[]{:S(2)}, u32[]{:S(2)}) collective-permute-start(bf16[128,1024]{1,0:T(8,128)(2,1)S(1)} %collective-permute-done.10.refs_2_.refs_4_), channel_id=1, source_target_pairs={{0,2},{1,3},{2,4},{3,5},{4,6},{5,7},{6,0},{7,1},{8,10},{9,11},{10,... | collective-permute-start | bytes 786440 | tf_op jit(solution)/shard_map/ppermute | solution.py:324
  30.4 10.1 %collective-permute-start.14 = (bf16[128,1024]{1,0:T(8,128)(2,1)S(1)}, bf16[128,1024]{1,0:T(8,128)(2,1)S(1)}, u32[]{:S(2)}, u32[]{:S(2)}) collective-permute-start(bf16[128,1024]{1,0:T(8,128)(2,1)S(1)} %get-tuple-element.56), channel_id=1, source_target_pairs={{0,1},{1,0},{2,3},{3,2},{4,5},{5,4},{6,7},{7,6},{8,9},{9,8},{10,11... | collective-permute-start | bytes 786440 | tf_op jit(solution)/shard_map/ppermute | solution.py:326
  34.9 11.2 %collective-permute-start.6 = (bf16[128,1024]{1,0:T(8,128)(2,1)S(1)}, bf16[128,1024]{1,0:T(8,128)(2,1)S(1)}, u32[]{:S(2)}, u32[]{:S(2)}) collective-permute-start(bf16[128,1024]{1,0:T(8,128)(2,1)S(1)} %collective-permute-done.5.refs_2_.refs_5_), channel_id=1, source_target_pairs={{0,2},{1,3},{2,4},{3,5},{4,6},{5,7},{6,0},{7,1},{8,10},{9,11},{10,... | collective-permute-start | bytes 786440 | tf_op jit(solution)/shard_map/ppermute | solution.py:327
  36.8 9.3 %collective-permute-start.12 = (bf16[128,1024]{1,0:T(8,128)(2,1)S(1)}, bf16[128,1024]{1,0:T(8,128)(2,1)S(1)}, u32[]{:S(2)}, u32[]{:S(2)}) collective-permute-start(bf16[128,1024]{1,0:T(8,128)(2,1)S(1)} %get-tuple-element.55), channel_id=1, source_target_pairs={{0,1},{1,0},{2,3},{3,2},{4,5},{5,4},{6,7},{7,6},{8,9},{9,8},{10,11... | collective-permute-start | bytes 786440 | tf_op jit(solution)/shard_map/ppermute | solution.py:329
  40.5 13.0 %collective-permute-start.16 = (bf16[128,1024]{1,0:T(8,128)(2,1)S(1)}, bf16[128,1024]{1,0:T(8,128)(2,1)S(1)}, u32[]{:S(2)}, u32[]{:S(2)}) collective-permute-start(bf16[128,1024]{1,0:T(8,128)(2,1)S(1)} %collective-permute-done.13.refs_2_.refs_4_), channel_id=1, source_target_pairs={{0,2},{1,3},{2,4},{3,5},{4,6},{5,7},{6,0},{7,1},{8,10},{9,11},{10,... | collective-permute-start | bytes 786440 | tf_op jit(solution)/shard_map/ppermute | solution.py:330
  42.4 11.1 %collective-permute-start.17 = (bf16[128,1024]{1,0:T(8,128)(2,1)S(1)}, bf16[128,1024]{1,0:T(8,128)(2,1)S(1)}, u32[]{:S(2)}, u32[]{:S(2)}) collective-permute-start(bf16[128,1024]{1,0:T(8,128)(2,1)S(1)} %get-tuple-element.62), channel_id=1, source_target_pairs={{0,1},{1,0},{2,3},{3,2},{4,5},{5,4},{6,7},{7,6},{8,9},{9,8},{10,11... | collective-permute-start | bytes 786440 | tf_op jit(solution)/shard_map/ppermute | solution.py:332
  46.1 11.3 %collective-permute-start.19 = (bf16[128,1024]{1,0:T(8,128)(2,1)S(1)}, bf16[128,1024]{1,0:T(8,128)(2,1)S(1)}, u32[]{:S(2)}, u32[]{:S(2)}) collective-permute-start(bf16[128,1024]{1,0:T(8,128)(2,1)S(1)} %collective-permute-done.6.refs_2_.refs_4_), channel_id=1, source_target_pairs={{0,2},{1,3},{2,4},{3,5},{4,6},{5,7},{6,0},{7,1},{8,10},{9,11},{10,... | collective-permute-start | bytes 786440 | tf_op jit(solution)/shard_map/ppermute | solution.py:333
  48.0 9.3 %collective-permute-start.20 = (bf16[128,1024]{1,0:T(8,128)(2,1)S(1)}, bf16[128,1024]{1,0:T(8,128)(2,1)S(1)}, u32[]{:S(2)}, u32[]{:S(2)}) collective-permute-start(bf16[128,1024]{1,0:T(8,128)(2,1)S(1)} %get-tuple-element.66), channel_id=1, source_target_pairs={{0,1},{1,0},{2,3},{3,2},{4,5},{5,4},{6,7},{7,6},{8,9},{9,8},{10,11... | collective-permute-start | bytes 786440 | tf_op jit(solution)/shard_map/ppermute | solution.py:335
  49.6 12.0 %collective-permute-start.15 = (bf16[128,1024]{1,0:T(8,128)(2,1)S(1)}, bf16[128,1024]{1,0:T(8,128)(2,1)S(1)}, u32[]{:S(2)}, u32[]{:S(2)}) collective-permute-start(bf16[128,1024]{1,0:T(8,128)(2,1)S(1)} %get-tuple-element.61), channel_id=1, source_target_pairs={{2,0},{3,1},{4,2},{5,3},{6,4},{7,5},{0,6},{1,7},{10,8},{11,9},{12,... | collective-permute-start | bytes 786440 | tf_op jit(solution)/shard_map/ppermute | solution.py:336
  55.4 6.4 %collective-permute-start.18 = (bf16[128,1024]{1,0:T(8,128)(2,1)S(1)}, bf16[128,1024]{1,0:T(8,128)(2,1)S(1)}, u32[]{:S(2)}, u32[]{:S(2)}) collective-permute-start(bf16[128,1024]{1,0:T(8,128)(2,1)S(1)} %get-tuple-element.65), channel_id=1, source_target_pairs={{0,1},{1,0},{2,3},{3,2},{4,5},{5,4},{6,7},{7,6},{8,9},{9,8},{10,11... | collective-permute-start | bytes 786440 | tf_op jit(solution)/shard_map/ppermute | solution.py:338
